TPU v7x, 128 devices: a whole 4x4x4 slice. The times are simulated.
128 devices in a mesh: frame: 8 (over y, core), refl: 16 (over x, z).
Axes of the slice: x: 4, y: 4, z: 4, core: 2. Of those that a mesh axis runs over, the one named last changes fastest.
Arguments:
- image: float32 [64, 512, 512], P('frame', 'refl'), may hold values from 0.5 to 160
- gain: float32 [512, 512], P('refl'), may hold values from 0.5 to 1.5
- pixel_mask: int32 [512, 512], P('refl'), may hold values 0 or 1
- anchor_row: int32 [16384], P(('frame', 'refl')), may hold values from 0 to 16
- anchor_col: int32 [16384], P(('frame', 'refl')), may hold values from 0 to 496
- owner: int32 [16384, 1], P(('frame', 'refl')), may hold values from 0 to 127; in each aligned block of 128 rows (0 to 127, 128 to 255, ...) at most 2 rows name the same one
- region: int32 [16384, 1], P(('frame', 'refl')), may hold values from 0 to 31
Outputs:
- strong: bfloat16 [64, 512, 512], P('frame', 'refl')
- intensity: float32 [128, 256], P(('frame', 'refl'))
- profiles: float32 [32, 729], replicated
Inputs may be any that keep to these rules, and one draw needn't show every extreme that they name: Among the 128 reflections of one source (aligned blocks of 128 rows) at most 2 name the same owner, a bound that some block reaches. Every region is named by some reflection.
All inputs are finite; a program needn't handle non-finite values. No bound on the sum of `pixel_mask` on one device may be relied on, other than what follows from the above.
Results may differ from a plain program's by a relative error of at most 0.006.
Values may be sent and summed in bfloat16 or wider, within the bound.
No kernel may reach another device: no remote copies, remote signals or barrier semaphores. Data moves between devices by JAX's collectives and lax.ppermute only.
A program may use at most 128 MiB of HBM per device.

v0:
```python
import functools

import jax
import jax.numpy as jnp
import numpy as np
from jax import lax
from jax.experimental import pallas as pl
from jax.experimental.pallas import tpu as pltpu
from jax.sharding import PartitionSpec as P

SB_EDGE = 16
GRID = 9
REGIONS = 32
ITERS = 3
HALO = 3
LANES = 128
HALF_BINS = 5
PLANE = 88
HALF_ROWS = HALF_BINS * PLANE
FULL_ROWS = GRID * PLANE
WIDE_ROWS = 896
PARAMS = pltpu.CompilerParams(vmem_limit_bytes=48 * 1024 * 1024)


def tent_values():
    centres = (np.arange(SB_EDGE, dtype=np.float32) + 0.5) * (GRID / SB_EDGE)
    bins = np.arange(GRID, dtype=np.float32) + 0.5
    return np.maximum(0.0, 1.0 - np.abs(centres[None, :] - bins[:, None]))


TENT = tent_values()
EDGE_WEIGHT = TENT.sum(axis=0)


def depth_mixer(rows, frames):
    mixer = np.zeros((2, rows, 8, rows, frames), np.float32)
    for row in range(rows):
        mixer[0, row, :HALF_BINS, row, :] = TENT[:HALF_BINS, :frames]
        mixer[1, row, :HALF_BINS, row, :] = TENT[GRID - HALF_BINS :, frames:]
    return mixer.reshape(2, rows * 8, rows * frames)


def dot(a, b):
    return lax.dot_general(a, b, (((1,), (0,)), ((), ())), preferred_element_type=jnp.float32)


def dot_nt(a, b):
    return lax.dot_general(a, b, (((1,), (1,)), ((), ())), preferred_element_type=jnp.float32)


def split_two(x):
    high = x.astype(jnp.bfloat16)
    return high, (x - high.astype(jnp.float32)).astype(jnp.bfloat16)


def parity(axis):
    return lax.axis_index(axis) % 2 == 1


def send_kernel(
    image,
    gain,
    mask,
    row,
    column,
    region,
    first,
    second,
    core,
    chip,
    kept,
    counts_in,
    gains,
    masks,
    infos,
    arrived,
):
    frames, height, columns = image.shape
    odd_band = parity("refl")
    odd_slab = parity("frame")
    copies = [(image, counts_in), (gain, gains), (mask, masks)]
    copies += [(info, infos.at[k]) for k, info in enumerate((row, column, region))]
    copies = [pltpu.make_async_copy(*copy, arrived.at[k]) for k, copy in enumerate(copies)]
    for copy in copies:
        copy.start()
    for copy in copies:
        copy.wait()
    live = masks[...].astype(jnp.float32)
    values = counts_in[...] * (gains[...] * live)[None]
    kept[0:height] = jnp.transpose(values, (1, 0, 2))

    head, tail = kept[0:HALO], kept[height - HALO : height]
    first[0:HALO] = jnp.where(odd_band, head, tail)
    second[0:HALO] = jnp.where(odd_band, tail, head)
    head, tail = live[0:HALO], live[height - HALO :]
    first[HALO, 0:HALO] = jnp.where(odd_band, head, tail)
    second[HALO, 0:HALO] = jnp.where(odd_band, tail, head)

    counts = values.astype(jnp.bfloat16).astype(jnp.float32)
    inner = counts[1]
    for z in range(2, frames - 1):
        inner = inner + counts[z]
    border = float(EDGE_WEIGHT[0])
    lower = inner + counts[frames - 1] + border * counts[0]
    upper = inner + counts[0] + border * counts[frames - 1]
    core[0:height] = jnp.where(odd_slab, upper, lower)
    chip[0:height] = jnp.where(odd_slab, lower, upper)
    for k in range(3):
        sent = infos[k].astype(jnp.float32)
        core[height + k : height + k + 1, 0:LANES] = sent
        chip[height + k : height + k + 1, 0:LANES] = sent
        kept[height, k : k + 1, 0:LANES] = sent
    for place, whole in enumerate((live, lower, upper)):
        first_row = height + 1 + place * height // 8
        kept[first_row : first_row + height // 8] = whole.reshape(height // 8, 8, columns)


def kept_info(kept, height, k):
    return kept[height, k : k + 1, 0:LANES].astype(jnp.int32)


def kept_rows(kept, height, place):
    first_row = height + 1 + place * height // 8
    return kept[first_row : first_row + height // 8].reshape(height, kept.shape[2])


def shoebox_offsets(anchors, extent):
    return lax.broadcasted_iota(jnp.int32, (extent, LANES), 0) - anchors


def total_weights(anchors, extent):
    offset = shoebox_offsets(anchors, extent)
    inside = (offset >= 0) & (offset < SB_EDGE)
    border = (offset == 0) | (offset == SB_EDGE - 1)
    return jnp.where(border, float(EDGE_WEIGHT[0]), jnp.where(inside, 1.0, 0.0))


def count_totals(levels, row, column):
    height, columns = levels.shape
    high, low = split_two(levels)
    by_column = total_weights(column, columns).astype(jnp.bfloat16)
    sums = dot(high, by_column) + dot(low, by_column)
    return jnp.sum(sums * total_weights(row, height), axis=0, keepdims=True)


def column_tents(column, columns, tents):
    offset = shoebox_offsets(column, columns)
    centre = (offset.astype(jnp.float32) + 0.5) * (GRID / SB_EDGE)
    for c in range(GRID):
        tent = jnp.maximum(1.0 - jnp.abs(centre - (c + 0.5)), 0.0)
        if c == 0:
            tent = jnp.where(offset >= 0, tent, 0.0)
        if c == GRID - 1:
            tent = jnp.where(offset < SB_EDGE, tent, 0.0)
        tents[:, c * LANES : (c + 1) * LANES] = tent.astype(jnp.bfloat16)


def window_sums(x):
    width = x.shape[-1]
    axis = x.ndim - 1
    pairs = x + pltpu.roll(x, 1, axis)
    fours = pairs + pltpu.roll(pairs, 2, axis)
    return fours + pltpu.roll(fours, width - 3, axis) - x


def window_counts(mask_rows, start, rows, terms, at):
    count = mask_rows[start : start + rows, :]
    for k in range(1, 2 * HALO + 1):
        count = count + mask_rows[start + k : start + k + rows, :]
    columns = count.shape[-1]
    tail = jnp.zeros((rows, LANES), jnp.float32)
    count = window_sums(jnp.concatenate([count, tail], axis=1))[:, 0:columns]
    per_spread = 1.0 / jnp.maximum(count - 1.0, 1.0)
    terms[0, at : at + rows, :] = 1.0 / jnp.maximum(count, 1.0)
    terms[1, at : at + rows, :] = per_spread
    terms[2, at : at + rows, :] = 1.0 + 6.0 * jnp.sqrt(2.0 * per_spread)


def row_pair(padded, base, terms, term_row, mask_rows, live_row, strong_rows, fields, slot):
    frames, columns = padded.shape[1:]
    rows = [padded[base + k] for k in range(2 * HALO + 2)]
    shared = rows[1]
    for k in range(2, 2 * HALO + 1):
        shared = shared + rows[k]
    squares = [x * x for x in rows]
    shared_square = squares[1]
    for k in range(2, 2 * HALO + 1):
        shared_square = shared_square + squares[k]
    frame_tail = jnp.zeros((2, frames, LANES), jnp.float32)
    total = jnp.stack([shared + rows[0], shared + rows[-1]])
    square = jnp.stack([shared_square + squares[0], shared_square + squares[-1]])
    total = window_sums(jnp.concatenate([total, frame_tail], axis=2))[:, :, 0:columns]
    square = window_sums(jnp.concatenate([square, frame_tail], axis=2))[:, :, 0:columns]
    value = jnp.stack([rows[HALO], rows[HALO + 1]])

    def every_frame(row):
        return jnp.broadcast_to(row, (frames, columns))

    def term(j):
        return jnp.stack([every_frame(terms[j, pl.ds(term_row + k, 1), :]) for k in range(2)])

    live = jnp.stack([every_frame(mask_rows[pl.ds(live_row + k, 1), :]) for k in range(2)])
    background = total * term(0)
    variance = (square - total * background) * term(1)
    per_root = lax.rsqrt(background + 1.0)
    excess = 2.0 * (variance * (per_root * per_root) - term(2))
    peak = (value - background - 3.0 * jnp.sqrt(background)) * per_root
    weight = live / ((1.0 + jnp.exp(-excess)) * (1.0 + jnp.exp(-peak)))
    weight_b = weight.astype(jnp.bfloat16).astype(jnp.float32)
    value_b = value.astype(jnp.bfloat16).astype(jnp.float32)
    background_b = background.astype(jnp.bfloat16).astype(jnp.float32)
    strong_rows[pl.ds(2 * slot, 2)] = weight_b
    at = pl.ds(pl.multiple_of(slot * 2 * frames, 2 * frames), 2 * frames)
    flat = (2 * frames, columns)
    fields[0, at, :] = (value_b - background_b).reshape(flat).astype(jnp.bfloat16)
    fields[1, at, :] = background_b.reshape(flat).astype(jnp.bfloat16)
    fields[2, at, :] = (weight_b * value_b).reshape(flat).astype(jnp.bfloat16)


def inner_kernel(kept, strong_rows, fields, tents, live, terms):
    height, columns = live.shape
    live[...] = kept_rows(kept, height, 0)
    column_tents(kept_info(kept, height, 1), columns, tents)
    rows = height - 8
    window_counts(live, 1, rows, terms, 0)

    def pair(i, carry):
        row_pair(kept, 2 * i + 1, terms, 2 * i, live, 2 * i + 4, strong_rows, fields, i)
        return carry

    lax.fori_loop(0, rows // 2, pair, 0, unroll=2)


def half_grids(mixed, tents, anchors, spread, packed, take):
    height = mixed.shape[0] // 8
    shift = jnp.broadcast_to(anchors, (8, LANES))
    spread[...] = dot(mixed, tents[...])
    bits = [(shift & (1 << k)) != 0 for k in range(5)]

    def one_column(c, carry):
        at = pl.ds(pl.multiple_of(c * LANES, LANES), LANES)
        rows = [spread[8 * r : 8 * r + 8, at] for r in range(height)]
        rows = [
            jnp.where(bits[4], rows[r + 16], rows[r]) if r + 16 < height else rows[r]
            for r in range(31)
        ]
        for k in (3, 2, 1, 0):
            keep = 16 + (1 << k) - 1
            rows = [jnp.where(bits[k], rows[r + (1 << k)], rows[r]) for r in range(keep)]
        for b in range(GRID):
            value = None
            for y in range(SB_EDGE):
                if TENT[b, y] != 0.0:
                    term = rows[y] * float(TENT[b, y])
                    value = term if value is None else value + term
            packed[pl.ds(pl.multiple_of((b * GRID + c) * 8, 8), 8), :] = value
        return carry

    lax.fori_loop(0, GRID, one_column, 0)
    for a in range(HALF_BINS):
        take(a, packed[pl.ds(a, PLANE, stride=8), :])


def clear_tail(packed):
    used = GRID * GRID * 8
    packed[used:, :] = jnp.zeros((packed.shape[0] - used, LANES), jnp.float32)


def spot_kernel(
    kept,
    halo_first,
    halo_second,
    from_core,
    from_chip,
    mixer,
    inner_fields,
    own_tents,
    edge_strong,
    edge_fields,
    partner_tents,
    rows,
    partial,
    padded,
    mask_rows,
    terms,
    field,
    spread,
    packed,
    contributions,
):
    frames, columns = kept.shape[1:]
    height = field.shape[0] // frames
    odd_band = parity("refl")
    odd_slab = parity("frame")
    has_partner = lax.axis_index("frame") > 0

    halo_a = halo_first[...]
    halo_b = halo_second[...]
    before = jnp.where(odd_band, halo_a, halo_b)
    after = jnp.where(odd_band, halo_b, halo_a)
    near = 4 + HALO
    padded[0:HALO] = before[0:HALO]
    padded[HALO : HALO + near] = kept[0:near]
    padded[HALO + near : HALO + 2 * near] = kept[height - near : height]
    padded[HALO + 2 * near :] = after[0:HALO]
    live = kept_rows(kept, height, 0)
    mask_rows[8 - HALO : 8, :] = before[HALO, 0:HALO]
    mask_rows[8 : 8 + near, :] = live[0:near]
    mask_rows[24 - HALO : 24 - HALO + near, :] = live[height - near :]
    mask_rows[28:31, :] = after[HALO, 0:HALO]
    window_counts(mask_rows, 5, 4, terms, 0)
    window_counts(mask_rows, 21, 4, terms, 8)
    for slot, (base, term_row, live_row) in enumerate(((0, 0, 8), (2, 2, 10), (10, 8, 24), (12, 10, 26))):
        row_pair(padded, base, terms, term_row, mask_rows, live_row, edge_strong, edge_fields, slot)

    partner = jnp.where(odd_slab, from_core[...], from_chip[...])
    following = jnp.where(odd_slab, from_chip[0:height], from_core[0:height])
    lower = kept_rows(kept, height, 1)
    upper = kept_rows(kept, height, 2)
    infos = [kept_info(kept, height, k) for k in range(3)]
    partner_info = [partner[height + k : height + k + 1, 0:LANES].astype(jnp.int32) for k in range(3)]
    rows[0] = infos[0]
    rows[1] = partner_info[0]
    own_total = count_totals(lower + following, infos[0], infos[1])
    partner_total = count_totals(partner[0:height] + upper, partner_info[0], partner_info[1])
    partner_total = jnp.where(has_partner, partner_total, 1.0)
    column_tents(partner_info[1], columns, partner_tents)

    contributions[...] = jnp.zeros(contributions.shape, jnp.float32)
    clear_tail(packed)
    quarter = 4 * frames
    field[0:quarter] = edge_fields[2, 0:quarter]
    field[quarter : height * frames - quarter] = inner_fields[2]
    field[height * frames - quarter :] = edge_fields[2, quarter:]
    for half, (anchors, tents, total) in enumerate(
        ((infos[0], own_tents, own_total), (partner_info[0], partner_tents, partner_total))
    ):
        mixed = dot(mixer[half], field[...]).astype(jnp.bfloat16)
        per_total = 1.0 / total

        def take(a, plane):
            first = (a + half * (GRID - HALF_BINS)) * PLANE
            contributions[first : first + PLANE, half * LANES : (half + 1) * LANES] = plane * per_total

        half_grids(mixed, tents, anchors, spread, packed, take)

    regions = lax.broadcasted_iota(jnp.int32, (REGIONS, LANES), 0)
    own_member = jnp.where(regions == infos[2], 1.0, 0.0)
    partner_member = jnp.where((regions == partner_info[2]) & has_partner, 1.0, 0.0)
    members = jnp.concatenate([own_member, partner_member], axis=1).astype(jnp.bfloat16)
    high, low = split_two(contributions[...])
    partial[...] = dot_nt(members, high) + dot_nt(members, low)


def grid_kernel(half, rows, mixer, edge_fields, inner_fields, tents, grids, field, spread, packed):
    clear_tail(packed)
    total = field.shape[0]
    quarter = edge_fields.shape[1] // 2
    for k in range(2):
        field[0:quarter] = edge_fields[k, 0:quarter]
        field[quarter : total - quarter] = inner_fields[k]
        field[total - quarter :] = edge_fields[k, quarter:]
        mixed = dot(mixer[half], field[...]).astype(jnp.bfloat16)

        def take(a, plane):
            grids[k, a * PLANE : (a + 1) * PLANE, :] = plane.astype(grids.dtype)

        half_grids(mixed, tents, rows[half], spread, packed, take)


def strong_kernel(edge_strong, inner_strong, strong, rows):
    rows[0:4] = edge_strong[0:4]
    rows[4 : rows.shape[0] - 4] = inner_strong[...]
    rows[rows.shape[0] - 4 :] = edge_strong[4:]
    strong[...] = jnp.transpose(rows[...], (1, 0, 2)).astype(jnp.bfloat16)


def fit_kernel(sums, region, slots, lower_grids, upper_core, upper_chip, estimates, signal, back, chosen):
    odd_slab = parity("frame")
    total = jnp.sum(sums[...], axis=1, keepdims=True)
    profile = sums[...] / total
    regions = lax.broadcasted_iota(jnp.int32, (REGIONS, LANES), 0)
    member = jnp.where(regions == region[...], 1.0, 0.0)
    chosen[...] = lax.dot_general(
        jnp.transpose(profile, (1, 0))[0:FULL_ROWS],
        member,
        (((1,), (0,)), ((), ())),
        precision=lax.Precision.HIGHEST,
        preferred_element_type=jnp.float32,
    )
    join = HALF_ROWS - PLANE
    for field, target in ((0, signal), (1, back)):
        upper = jnp.where(odd_slab, upper_chip[field], upper_core[field]).astype(jnp.float32)
        target[0:join] = lower_grids[field, 0:join]
        target[join:HALF_ROWS] = lower_grids[field, join:HALF_ROWS] + upper[0:PLANE]
        target[HALF_ROWS:] = upper[PLANE:HALF_ROWS]
    estimate = jnp.sum(signal[...], axis=0, keepdims=True)
    for _ in range(ITERS):
        weight_var = back[...] + jnp.maximum(estimate, 0.0) * chosen[...] + 1.0
        ratio = chosen[...] / weight_var
        upper_sum = jnp.sum(ratio * signal[...], axis=0, keepdims=True)
        lower_sum = jnp.sum(ratio * chosen[...], axis=0, keepdims=True)
        estimate = upper_sum / lower_sum
    devices = estimates.shape[0]
    target = lax.broadcasted_iota(jnp.int32, (devices, LANES), 0) * 2
    for j in range(2):
        held = jnp.where(slots[...] == target + j, estimate, 0.0)
        estimates[:, j : j + 1] = jnp.sum(held, axis=1, keepdims=True)


def profile_kernel(sums, profiles):
    profile = sums[...] / jnp.sum(sums[...], axis=1, keepdims=True)
    profiles[...] = jnp.concatenate(
        [profile[:, a * PLANE : a * PLANE + GRID * GRID] for a in range(GRID)], axis=1
    )


def spread_kernel(arrived, intensity):
    devices = arrived.shape[0]
    lane = lax.broadcasted_iota(jnp.int32, (devices, 2 * devices), 1)
    source = lax.broadcasted_iota(jnp.int32, (devices, 2 * devices), 0)
    placed = jnp.where(lane == 2 * source, arrived[:, 0:1], 0.0)
    placed = placed + jnp.where(lane == 2 * source + 1, arrived[:, 1:2], 0.0)
    intensity[...] = jnp.sum(placed, axis=0, keepdims=True)


def slot_numbers(owners):
    position = jnp.arange(owners.shape[0], dtype=jnp.int32)
    earlier = (owners[None, :] == owners[:, None]) & (position[None, :] < position[:, None])
    return owners * 2 + jnp.sum(jnp.where(earlier, 1, 0), axis=1).astype(jnp.int32)


def pairs_even(count):
    return [(i, i ^ 1) for i in range(count)]


def pairs_odd(count):
    return [(i, i + 1 if i % 2 else i - 1) for i in range(1, count - 1)]


def swapped(x, axis, flip):
    return lax.ppermute(x, axis, [(i, i ^ flip) for i in range(lax.axis_size(axis))])


def summed_over_four(sums, axis, flips):
    sent = sums.astype(jnp.bfloat16)
    one, two, three = [swapped(sent, axis, flip).astype(jnp.float32) for flip in flips]
    return (sent.astype(jnp.float32) + one) + (two + three)


def per_device(image, gain, pixel_mask, anchor_row, anchor_col, owner, region):
    frames, height, columns = image.shape
    slabs = lax.axis_size("frame")
    bands = lax.axis_size("refl")
    devices = slabs * bands
    f32, bf16 = jnp.float32, jnp.bfloat16
    vmem = pl.BlockSpec(memory_space=pltpu.VMEM)

    def shape(dims, dtype=f32):
        return jax.ShapeDtypeStruct(dims, dtype)

    def call(kernel, operands, outs, scratch=(), name=None, work=1):
        return pl.pallas_call(
            kernel,
            in_specs=[vmem] * len(operands),
            out_specs=[vmem] * len(outs),
            out_shape=outs,
            scratch_shapes=[pltpu.VMEM(s.shape, s.dtype) for s in scratch],
            compiler_params=PARAMS,
            cost_estimate=pl.CostEstimate(flops=work, bytes_accessed=work, transcendentals=0),
            name=name,
        )(*operands)

    row, column, area = (x.reshape(1, -1) for x in (anchor_row, anchor_col, region))
    first, second, core, chip, kept = pl.pallas_call(
        send_kernel,
        in_specs=[pl.BlockSpec(memory_space=pl.ANY)] * 6,
        out_specs=[vmem] * 5,
        out_shape=[shape((HALO + 1, frames, columns))] * 2
        + [shape((height + 8, columns))] * 2
        + [shape((height + 1 + 3 * height // 8, frames, columns))],
        scratch_shapes=[
            pltpu.VMEM((frames, height, columns), f32),
            pltpu.VMEM((height, columns), f32),
            pltpu.VMEM((height, columns), jnp.int32),
            pltpu.VMEM((3, 1, LANES), jnp.int32),
            pltpu.SemaphoreType.DMA((6,)),
        ],
        name="sent",
    )(image, gain, pixel_mask, row, column, area)
    halo_second = lax.ppermute(second, "refl", pairs_odd(bands))
    halo_first = lax.ppermute(first, "refl", pairs_even(bands))
    from_core = lax.ppermute(core, "frame", pairs_even(slabs))
    from_chip = lax.ppermute(chip, "frame", pairs_odd(slabs))
    slots = slot_numbers(owner[:, 0])[None, :]

    inner = height - 8
    tent_shape = shape((columns, GRID * LANES), bf16)
    inner_strong, inner_fields, own_tents = call(
        inner_kernel,
        (kept,),
        [shape((inner, frames, columns)), shape((3, inner * frames, columns), bf16), tent_shape],
        [shape((height, columns)), shape((3, inner, columns))],
        name="inner",
    )

    mixer = jnp.asarray(depth_mixer(height, frames), bf16)
    field_shape = shape((height * frames, columns), bf16)
    spread_shape = shape((height * 8, GRID * LANES))
    packed_shape = shape((PLANE * 8, LANES))
    edge_strong, edge_fields, partner_tents, rows, partial = call(
        spot_kernel,
        (
            kept,
            halo_first,
            halo_second,
            from_core,
            from_chip,
            mixer,
            inner_fields,
            own_tents,
        ),
        [
            shape((8, frames, columns)),
            shape((3, 8 * frames, columns), bf16),
            tent_shape,
            shape((2, 1, LANES), jnp.int32),
            shape((REGIONS, WIDE_ROWS)),
        ],
        [
            shape((2 * (HALO + 4 + HALO), frames, columns)),
            shape((height, columns)),
            shape((3, 16, columns)),
            field_shape,
            spread_shape,
            packed_shape,
            shape((WIDE_ROWS, 2 * LANES)),
        ],
        name="spots",
    )
    sums = partial + swapped(partial, "frame", 1)
    sums, edge_fields = lax.optimization_barrier((sums, edge_fields))
    scratch = [field_shape, spread_shape, packed_shape]
    (upper_grids,) = call(
        functools.partial(grid_kernel, 1),
        (rows, mixer, edge_fields, inner_fields, partner_tents),
        [shape((2, HALF_ROWS, LANES), bf16)],
        scratch,
        name="upper",
    )
    sums = summed_over_four(sums, "refl", (1, 2, 3))
    sums, upper_grids, edge_fields = lax.optimization_barrier((sums, upper_grids, edge_fields))
    upper_core = lax.ppermute(upper_grids, "frame", pairs_even(slabs))
    upper_chip = lax.ppermute(upper_grids, "frame", pairs_odd(slabs))
    sums = summed_over_four(sums, "refl", (4, 8, 12))
    sums, edge_fields = lax.optimization_barrier((sums, edge_fields))
    (lower_grids,) = call(
        functools.partial(grid_kernel, 0),
        (rows, mixer, edge_fields, inner_fields, own_tents),
        [shape((2, HALF_ROWS, LANES))],
        scratch,
        name="lower",
    )
    sums = summed_over_four(sums, "frame", (2, 4, 6))
    (strong,) = call(
        strong_kernel,
        (edge_strong, inner_strong),
        [shape((frames, height, columns), bf16)],
        [shape((height, frames, columns))],
        name="strong",
    )
    (estimates,) = call(
        fit_kernel,
        (sums, area, slots, lower_grids, upper_core, upper_chip),
        [shape((devices, 2))],
        [shape((FULL_ROWS, LANES))] * 3,
        name="fit",
    )
    arrived = lax.all_to_all(estimates, ("frame", "refl"), split_axis=0, concat_axis=0, tiled=True)
    (profiles,) = call(profile_kernel, (sums,), [shape((REGIONS, GRID * GRID * GRID))], name="profiles")
    (intensity,) = call(spread_kernel, (arrived,), [shape((1, devices * 2))], name="intensity")
    return (strong, intensity, profiles)


def solution(mesh):
    in_specs = (
        P("frame", "refl", None),
        P("refl", None),
        P("refl", None),
        P(("frame", "refl")),
        P(("frame", "refl")),
        P(("frame", "refl"), None),
        P(("frame", "refl"), None),
    )
    out_specs = (P("frame", "refl", None), P(("frame", "refl"), None), P())
    return jax.shard_map(
        per_device, mesh=mesh, in_specs=in_specs, out_specs=out_specs, check_vma=False
    )
```

profile of v0, /device:TPU:1, one launch (start us, length us, event | category | flops | bytes accessed | tf_op | source)
XLA Modules:
  0.0 70.9 jit_solution(2589708061600636770)
XLA Ops:
  0.6 2.3 %sent.1 = (f32[4,8,512]{2,1,0:T(8,128)}, f32[4,8,512]{2,1,0:T(8,128)}, f32[40,512]{1,0:T(8,128)}, f32[40,512]{1,0:T(8,128)}, f32[45,8,512]{2,1,0:T(8,128)}) custom-call(f32[8,32,512]{2,1,0:T(8,128)} %image.1, f32[32,512]{1,0:T(8,128)} %gain.1, s32[32,512]{1,0:T(8,128)} %mask.1, s32[1,128]{1,0:T(1,128)} %bitcast.15, s32[1,128]{1,0:T(1,128)} %bitcast.16, ...), custom_call_target="tpu_custom_call" | custom-call | tf_op jit(solution)/shard_map/sent/pallas_call | solution.py:475
  2.9 1.5 %collective-permute-start.2 = (f32[40,512]{1,0:T(8,128)}, f32[40,512]{1,0:T(8,128)S(1)}, u32[]{:S(2)}, u32[]{:S(2)}) collective-permute-start(f32[40,512]{1,0:T(8,128)} %get-tuple-element.26), channel_id=1, source_target_pairs={{0,16},{16,0},{32,48},{48,32},{64,80},{80,64},{96,112},{112,96},{1... | collective-permute-start | bytes 245768 | tf_op jit(solution)/shard_map/ppermute | solution.py:493
  4.4 3.2 %collective-permute-start.3 = (f32[40,512]{1,0:T(8,128)}, f32[40,512]{1,0:T(8,128)S(1)}, u32[]{:S(2)}, u32[]{:S(2)}) collective-permute-start(f32[40,512]{1,0:T(8,128)} %get-tuple-element.27), channel_id=1, source_target_pairs={{16,32},{32,16},{48,64},{64,48},{80,96},{96,80},{17,33},{33,17},{4... | collective-permute-start | bytes 245768 | tf_op jit(solution)/shard_map/ppermute | solution.py:494
  7.6 1.7 %collective-permute-start = (f32[4,8,512]{2,1,0:T(8,128)}, f32[4,8,512]{2,1,0:T(8,128)S(1)}, u32[]{:S(2)}, u32[]{:S(2)}) collective-permute-start(f32[4,8,512]{2,1,0:T(8,128)} %get-tuple-element.24), channel_id=1, source_target_pairs={{0,1},{1,0},{2,3},{3,2},{4,5},{5,4},{6,7},{7,6},{8,9},{9,8},{10,11... | collective-permute-start | bytes 196616 | tf_op jit(solution)/shard_map/ppermute | solution.py:492
  11.1 3.1 %inner.1 = (f32[24,8,512]{2,1,0:T(8,128)S(1)}, bf16[3,192,512]{2,1,0:T(8,128)(2,1)S(1)}, bf16[512,1152]{1,0:T(8,128)(2,1)S(1)}) custom-call(f32[45,8,512]{2,1,0:T(8,128)S(1)} %copy-done), custom_call_target="tpu_custom_call" | custom-call | flops 1 | bytes 1 | tf_op jit(solution)/shard_map/inner/pallas_call | solution.py:463
  14.3 3.4 %spots.1 = (f32[8,8,512]{2,1,0:T(8,128)S(1)}, bf16[3,64,512]{2,1,0:T(8,128)(2,1)S(1)}, bf16[512,1152]{1,0:T(8,128)(2,1)S(1)}, s32[2,1,128]{2,1,0:T(1,128)S(1)}, f32[32,896]{1,0:T(8,128)S(1)}) custom-call(f32[45,8,512]{2,1,0:T(8,128)S(1)} %copy-done, f32[4,8,512]{2,1,0:T(8,128)S(1)} %collective-permute-done.halo_first, ...), custom_call_target="tpu_custom_call" | custom-call | flops 1 | bytes 1 | tf_op jit(solution)/shard_map/spots/pallas_call | solution.py:463
  17.7 1.3 %collective-permute-done.4 = f32[32,896]{1,0:T(8,128)S(1)} collective-permute-done((f32[32,896]{1,0:T(8,128)S(1)}, f32[32,896]{1,0:T(8,128)S(1)}, u32[]{:S(2)}, u32[]{:S(2)}) %collective-permute-start.4) | collective-permute-done | bytes 114720 | tf_op jit(solution)/shard_map/ppermute | solution.py:442
  19.0 4.3 %collective-permute-start.5 = (bf16[32,896]{1,0:T(8,128)(2,1)S(1)}, bf16[32,896]{1,0:T(8,128)(2,1)S(1)}, u32[]{:S(2)}, u32[]{:S(2)}) collective-permute-start(bf16[32,896]{1,0:T(8,128)(2,1)S(1)} %add.40), channel_id=1, source_target_pairs={{0,1},{1,0},{2,3},{3,2},{4,5},{5,4},{6,7},{7,6},{8,9},{9,8},{10,11... | collective-permute-start | bytes 172040 | tf_op jit(solution)/shard_map/ppermute | solution.py:442
  23.3 1.8 %collective-permute-start.6 = (bf16[32,896]{1,0:T(8,128)(2,1)S(1)}, bf16[32,896]{1,0:T(8,128)(2,1)S(1)}, u32[]{:S(2)}, u32[]{:S(2)}) collective-permute-start(bf16[32,896]{1,0:T(8,128)(2,1)S(1)} %add.40), channel_id=1, source_target_pairs={{0,2},{1,3},{2,0},{3,1},{4,6},{5,7},{6,4},{7,5},{8,10},{9,11},{10,... | collective-permute-start | bytes 172040 | tf_op jit(solution)/shard_map/ppermute | solution.py:442
  25.8 1.8 %upper.1 = bf16[2,440,128]{2,1,0:T(8,128)(2,1)S(1)} custom-call(s32[2,1,128]{2,1,0:T(1,128)S(1)} %get-tuple-element.35.rows, bf16[2,256,256]{2,1,0:T(8,128)(2,1)S(1)} %copy-done.1, bf16[3,64,512]{2,1,0:T(8,128)(2,1)S(1)} %get-tuple-element.41.edge_fields, bf16[3,192,512]{2,1,0:T(8,128)(2,1)S(1)} %get-tuple-element.28.inner_fields, ...), custom_call_target="tpu_custom_call" | custom-call | flops 1 | bytes 1 | tf_op jit(solution)/shard_map/upper/pallas_call | solution.py:463
  27.9 1.4 %collective-permute-done.7 = bf16[32,896]{1,0:T(8,128)(2,1)S(1)} collective-permute-done((bf16[32,896]{1,0:T(8,128)(2,1)S(1)}, bf16[32,896]{1,0:T(8,128)(2,1)S(1)}, u32[]{:S(2)}, u32[]{:S(2)}) %collective-permute-start.7) | collective-permute-done | bytes 57376 | tf_op jit(solution)/shard_map/ppermute | solution.py:442
  29.4 2.8 %collective-permute-start.10 = (bf16[32,896]{1,0:T(8,128)(2,1)S(1)}, bf16[32,896]{1,0:T(8,128)(2,1)S(1)}, u32[]{:S(2)}, u32[]{:S(2)}) collective-permute-start(bf16[32,896]{1,0:T(8,128)(2,1)S(1)} %add_add_fusion.2), channel_id=1, source_target_pairs={{0,12},{1,13},{2,14},{3,15},{4,8},{5,9},{6,10},{7,11},{8,4},{9,5},... | collective-permute-start | bytes 172040 | tf_op jit(solution)/shard_map/ppermute | solution.py:442
  32.2 1.3 %collective-permute-start.9 = (bf16[32,896]{1,0:T(8,128)(2,1)S(1)}, bf16[32,896]{1,0:T(8,128)(2,1)S(1)}, u32[]{:S(2)}, u32[]{:S(2)}) collective-permute-start(bf16[32,896]{1,0:T(8,128)(2,1)S(1)} %add_add_fusion.2), channel_id=1, source_target_pairs={{0,8},{1,9},{2,10},{3,11},{4,12},{5,13},{6,14},{7,15},{8,0},{9,1},... | collective-permute-start | bytes 172040 | tf_op jit(solution)/shard_map/ppermute | solution.py:442
  33.8 1.5 %collective-permute-done.8 = bf16[32,896]{1,0:T(8,128)(2,1)S(1)} collective-permute-done((bf16[32,896]{1,0:T(8,128)(2,1)S(1)}, bf16[32,896]{1,0:T(8,128)(2,1)S(1)}, u32[]{:S(2)}, u32[]{:S(2)}) %collective-permute-start.8) | collective-permute-done | bytes 57376 | tf_op jit(solution)/shard_map/ppermute | solution.py:442
  35.3 1.5 %collective-permute-done.9 = bf16[32,896]{1,0:T(8,128)(2,1)S(1)} collective-permute-done((bf16[32,896]{1,0:T(8,128)(2,1)S(1)}, bf16[32,896]{1,0:T(8,128)(2,1)S(1)}, u32[]{:S(2)}, u32[]{:S(2)}) %collective-permute-start.9) | collective-permute-done | bytes 57376 | tf_op jit(solution)/shard_map/ppermute | solution.py:442
  36.8 1.9 %collective-permute-start.11 = (bf16[32,896]{1,0:T(8,128)(2,1)S(1)}, bf16[32,896]{1,0:T(8,128)(2,1)S(1)}, u32[]{:S(2)}, u32[]{:S(2)}) collective-permute-start(bf16[32,896]{1,0:T(8,128)(2,1)S(1)} %add_add_fusion.1), channel_id=1, source_target_pairs={{0,32},{16,48},{32,0},{48,16},{64,96},{80,112},{96,64},{112,80},{1... | collective-permute-start | bytes 172040 | tf_op jit(solution)/shard_map/ppermute | solution.py:442
  38.8 2.3 %collective-permute-start.12 = (bf16[32,896]{1,0:T(8,128)(2,1)S(1)}, bf16[32,896]{1,0:T(8,128)(2,1)S(1)}, u32[]{:S(2)}, u32[]{:S(2)}) collective-permute-start(bf16[32,896]{1,0:T(8,128)(2,1)S(1)} %add_add_fusion.1), channel_id=1, source_target_pairs={{0,64},{16,80},{32,96},{48,112},{64,0},{80,16},{96,32},{112,48},{1... | collective-permute-start | bytes 172040 | tf_op jit(solution)/shard_map/ppermute | solution.py:442
  41.2 4.2 %collective-permute-start.14 = (bf16[2,440,128]{2,1,0:T(8,128)(2,1)S(1)}, bf16[2,440,128]{2,1,0:T(8,128)(2,1)S(1)}, u32[]{:S(2)}, u32[]{:S(2)}) collective-permute-start(bf16[2,440,128]{2,1,0:T(8,128)(2,1)S(1)} %upper.1), channel_id=1, source_target_pairs={{0,16},{16,0},{32,48},{48,32},{64,80},{80,64},{96,112},{112,96},{1... | collective-permute-start | bytes 675848 | tf_op jit(solution)/shard_map/ppermute | solution.py:553
  45.5 2.2 %collective-permute-start.15 = (bf16[2,440,128]{2,1,0:T(8,128)(2,1)S(1)}, bf16[2,440,128]{2,1,0:T(8,128)(2,1)S(1)}, u32[]{:S(2)}, u32[]{:S(2)}) collective-permute-start(bf16[2,440,128]{2,1,0:T(8,128)(2,1)S(1)} %upper.1), channel_id=1, source_target_pairs={{16,32},{32,16},{48,64},{64,48},{80,96},{96,80},{17,33},{33,17},{4... | collective-permute-start | bytes 675848 | tf_op jit(solution)/shard_map/ppermute | solution.py:554
  47.7 1.9 %lower.1.lower_grids = f32[2,440,128]{2,1,0:T(8,128)S(1)} custom-call(s32[2,1,128]{2,1,0:T(1,128)S(1)} %get-tuple-element.35.rows, bf16[2,256,256]{2,1,0:T(8,128)(2,1)S(1)} %copy-done.1, bf16[3,64,512]{2,1,0:T(8,128)(2,1)S(1)} %get-tuple-element.41.edge_fields, bf16[3,192,512]{2,1,0:T(8,128)(2,1)S(1)} %get-tuple-element.28.inner_fields, ...), custom_call_target="tpu_custom_call" | custom-call | flops 1 | bytes 1 | tf_op jit(solution)/shard_map/lower/pallas_call | solution.py:463
  49.7 3.1 %collective-permute-done.15.upper_chip = bf16[2,440,128]{2,1,0:T(8,128)(2,1)S(1)} collective-permute-done((bf16[2,440,128]{2,1,0:T(8,128)(2,1)S(1)}, bf16[2,440,128]{2,1,0:T(8,128)(2,1)S(1)}, u32[]{:S(2)}, u32[]{:S(2)}) %collective-permute-start.15) | collective-permute-done | bytes 225312 | tf_op jit(solution)/shard_map/ppermute | solution.py:554
  52.8 2.1 %fit.1 = f32[128,2]{1,0:T(8,128)} custom-call(f32[32,896]{1,0:T(8,128)S(1)} %add_add_fusion.sums, s32[1,128]{1,0:T(1,128)S(1)} %bitcast.14, s32[1,128]{1,0:T(1,128)S(1)} %bitcast_add_fusion.slots, f32[2,440,128]{2,1,0:T(8,128)S(1)} %lower.1.lower_grids, bf16[2,440,128]{2,1,0:T(8,128)(2,1)S(1)} %collective-permute-done.14.upper_core, ...), custom_call_target="tpu_custom_call" | custom-call | flops 1 | bytes 1 | tf_op jit(solution)/shard_map/fit/pallas_call | solution.py:463
  54.8 5.8 %all-to-all-start = ((f32[128,1,2]{2,1,0:T(1,128)}), f32[128,1,2]{2,1,0:T(1,128)S(1)}, u32[]{:S(2)}, u32[]{:S(2)}) async-start(f32[128,1,2]{2,1,0:T(1,128)} %bitcast.7), calls=%async_computation | async-start | bytes 131072 | tf_op jit(solution)/shard_map/all_to_all | solution.py:579
  62.4 7.9 %all-to-all-done = f32[128,1,2]{2,1,0:T(1,128)S(1)} async-done(((f32[128,1,2]{2,1,0:T(1,128)}), f32[128,1,2]{2,1,0:T(1,128)S(1)}, u32[]{:S(2)}, u32[]{:S(2)}) %all-to-all-start) | async-done | bytes 1056 | tf_op jit(solution)/shard_map/all_to_all | solution.py:579
  (33 shorter events, 5.7 us)
Async XLA Ops:
  0.6 13.6 %copy-start.1 = (bf16[2,256,256]{2,1,0:T(8,128)(2,1)S(1)}, bf16[2,256,256]{2,1,0:T(8,128)(2,1)}, u32[]{:S(2)}) copy-start(bf16[2,256,256]{2,1,0:T(8,128)(2,1)} %constant.8.clone.mixer) | copy-start | bytes 786436
  2.9 11.3 %collective-permute-start.2 = (f32[40,512]{1,0:T(8,128)}, f32[40,512]{1,0:T(8,128)S(1)}, u32[]{:S(2)}, u32[]{:S(2)}) collective-permute-start(f32[40,512]{1,0:T(8,128)} %get-tuple-element.26), channel_id=1, source_target_pairs={{0,16},{16,0},{32,48},{48,32},{64,80},{80,64},{96,112},{112,96},{1... | collective-permute-start | bytes 245768 | tf_op jit(solution)/shard_map/ppermute | solution.py:493
  4.4 9.8 %collective-permute-start.3 = (f32[40,512]{1,0:T(8,128)}, f32[40,512]{1,0:T(8,128)S(1)}, u32[]{:S(2)}, u32[]{:S(2)}) collective-permute-start(f32[40,512]{1,0:T(8,128)} %get-tuple-element.27), channel_id=1, source_target_pairs={{16,32},{32,16},{48,64},{64,48},{80,96},{96,80},{17,33},{33,17},{4... | collective-permute-start | bytes 245768 | tf_op jit(solution)/shard_map/ppermute | solution.py:494
  7.6 6.6 %collective-permute-start = (f32[4,8,512]{2,1,0:T(8,128)}, f32[4,8,512]{2,1,0:T(8,128)S(1)}, u32[]{:S(2)}, u32[]{:S(2)}) collective-permute-start(f32[4,8,512]{2,1,0:T(8,128)} %get-tuple-element.24), channel_id=1, source_target_pairs={{0,1},{1,0},{2,3},{3,2},{4,5},{5,4},{6,7},{7,6},{8,9},{9,8},{10,11... | collective-permute-start | bytes 196616 | tf_op jit(solution)/shard_map/ppermute | solution.py:492
  9.3 4.9 %collective-permute-start.1 = (f32[4,8,512]{2,1,0:T(8,128)}, f32[4,8,512]{2,1,0:T(8,128)S(1)}, u32[]{:S(2)}, u32[]{:S(2)}) collective-permute-start(f32[4,8,512]{2,1,0:T(8,128)} %get-tuple-element.25), channel_id=1, source_target_pairs={{1,2},{2,1},{3,4},{4,3},{5,6},{6,5},{7,8},{8,7},{9,10},{10,9},{11,... | collective-permute-start | bytes 196616 | tf_op jit(solution)/shard_map/ppermute | solution.py:491
  10.0 1.1 %copy-start = (f32[45,8,512]{2,1,0:T(8,128)S(1)}, f32[45,8,512]{2,1,0:T(8,128)}, u32[]{:S(2)}) copy-start(f32[45,8,512]{2,1,0:T(8,128)} %get-tuple-element.23.kept) | copy-start | bytes 2211844
  17.6 1.4 %collective-permute-start.4 = (f32[32,896]{1,0:T(8,128)S(1)}, f32[32,896]{1,0:T(8,128)S(1)}, u32[]{:S(2)}, u32[]{:S(2)}) collective-permute-start(f32[32,896]{1,0:T(8,128)S(1)} %get-tuple-element.32), channel_id=1, source_target_pairs={{0,16},{16,0},{32,48},{48,32},{64,80},{80,64},{96,112},{112,96},{1... | collective-permute-start | bytes 344072 | tf_op jit(solution)/shard_map/ppermute | solution.py:442
  19.0 8.6 %collective-permute-start.5 = (bf16[32,896]{1,0:T(8,128)(2,1)S(1)}, bf16[32,896]{1,0:T(8,128)(2,1)S(1)}, u32[]{:S(2)}, u32[]{:S(2)}) collective-permute-start(bf16[32,896]{1,0:T(8,128)(2,1)S(1)} %add.40), channel_id=1, source_target_pairs={{0,1},{1,0},{2,3},{3,2},{4,5},{5,4},{6,7},{7,6},{8,9},{9,8},{10,11... | collective-permute-start | bytes 172040 | tf_op jit(solution)/shard_map/ppermute | solution.py:442
  23.3 4.6 %collective-permute-start.6 = (bf16[32,896]{1,0:T(8,128)(2,1)S(1)}, bf16[32,896]{1,0:T(8,128)(2,1)S(1)}, u32[]{:S(2)}, u32[]{:S(2)}) collective-permute-start(bf16[32,896]{1,0:T(8,128)(2,1)S(1)} %add.40), channel_id=1, source_target_pairs={{0,2},{1,3},{2,0},{3,1},{4,6},{5,7},{6,4},{7,5},{8,10},{9,11},{10,... | collective-permute-start | bytes 172040 | tf_op jit(solution)/shard_map/ppermute | solution.py:442
  25.1 4.2 %collective-permute-start.7 = (bf16[32,896]{1,0:T(8,128)(2,1)S(1)}, bf16[32,896]{1,0:T(8,128)(2,1)S(1)}, u32[]{:S(2)}, u32[]{:S(2)}) collective-permute-start(bf16[32,896]{1,0:T(8,128)(2,1)S(1)} %add.40), channel_id=1, source_target_pairs={{0,3},{1,2},{2,1},{3,0},{4,7},{5,6},{6,5},{7,4},{8,11},{9,10},{10,... | collective-permute-start | bytes 172040 | tf_op jit(solution)/shard_map/ppermute | solution.py:442
  25.8 7.7 %copy-start.3 = (s32[128,1]{0,1:T(1,128)S(1)}, s32[128,1]{0,1:T(1,128)}, u32[]{:S(2)}) copy-start(s32[128,1]{0,1:T(1,128)} %param.13) | copy-start | bytes 1540
  29.4 4.4 %collective-permute-start.10 = (bf16[32,896]{1,0:T(8,128)(2,1)S(1)}, bf16[32,896]{1,0:T(8,128)(2,1)S(1)}, u32[]{:S(2)}, u32[]{:S(2)}) collective-permute-start(bf16[32,896]{1,0:T(8,128)(2,1)S(1)} %add_add_fusion.2), channel_id=1, source_target_pairs={{0,12},{1,13},{2,14},{3,15},{4,8},{5,9},{6,10},{7,11},{8,4},{9,5},... | collective-permute-start | bytes 172040 | tf_op jit(solution)/shard_map/ppermute | solution.py:442
  32.2 3.0 %collective-permute-start.8 = (bf16[32,896]{1,0:T(8,128)(2,1)S(1)}, bf16[32,896]{1,0:T(8,128)(2,1)S(1)}, u32[]{:S(2)}, u32[]{:S(2)}) collective-permute-start(bf16[32,896]{1,0:T(8,128)(2,1)S(1)} %add_add_fusion.2), channel_id=1, source_target_pairs={{0,4},{1,5},{2,6},{3,7},{4,0},{5,1},{6,2},{7,3},{8,12},{9,13},{10,... | collective-permute-start | bytes 172040 | tf_op jit(solution)/shard_map/ppermute | solution.py:442
  32.2 4.5 %collective-permute-start.9 = (bf16[32,896]{1,0:T(8,128)(2,1)S(1)}, bf16[32,896]{1,0:T(8,128)(2,1)S(1)}, u32[]{:S(2)}, u32[]{:S(2)}) collective-permute-start(bf16[32,896]{1,0:T(8,128)(2,1)S(1)} %add_add_fusion.2), channel_id=1, source_target_pairs={{0,8},{1,9},{2,10},{3,11},{4,12},{5,13},{6,14},{7,15},{8,0},{9,1},... | collective-permute-start | bytes 172040 | tf_op jit(solution)/shard_map/ppermute | solution.py:442
  36.8 12.8 %collective-permute-start.11 = (bf16[32,896]{1,0:T(8,128)(2,1)S(1)}, bf16[32,896]{1,0:T(8,128)(2,1)S(1)}, u32[]{:S(2)}, u32[]{:S(2)}) collective-permute-start(bf16[32,896]{1,0:T(8,128)(2,1)S(1)} %add_add_fusion.1), channel_id=1, source_target_pairs={{0,32},{16,48},{32,0},{48,16},{64,96},{80,112},{96,64},{112,80},{1... | collective-permute-start | bytes 172040 | tf_op jit(solution)/shard_map/ppermute | solution.py:442
  38.8 10.9 %collective-permute-start.12 = (bf16[32,896]{1,0:T(8,128)(2,1)S(1)}, bf16[32,896]{1,0:T(8,128)(2,1)S(1)}, u32[]{:S(2)}, u32[]{:S(2)}) collective-permute-start(bf16[32,896]{1,0:T(8,128)(2,1)S(1)} %add_add_fusion.1), channel_id=1, source_target_pairs={{0,64},{16,80},{32,96},{48,112},{64,0},{80,16},{96,32},{112,48},{1... | collective-permute-start | bytes 172040 | tf_op jit(solution)/shard_map/ppermute | solution.py:442
  41.1 8.6 %collective-permute-start.13 = (bf16[32,896]{1,0:T(8,128)(2,1)S(1)}, bf16[32,896]{1,0:T(8,128)(2,1)S(1)}, u32[]{:S(2)}, u32[]{:S(2)}) collective-permute-start(bf16[32,896]{1,0:T(8,128)(2,1)S(1)} %add_add_fusion.1), channel_id=1, source_target_pairs={{0,96},{16,112},{32,64},{48,80},{64,32},{80,48},{96,0},{112,16},{1... | collective-permute-start | bytes 172040 | tf_op jit(solution)/shard_map/ppermute | solution.py:442
  41.2 11.5 %copy-start.2 = (s32[128,1]{0,1:T(1,128)S(1)}, s32[128,1]{0,1:T(1,128)}, u32[]{:S(2)}) copy-start(s32[128,1]{0,1:T(1,128)} %param.14) | copy-start | bytes 1540
  41.2 8.4 %collective-permute-start.14 = (bf16[2,440,128]{2,1,0:T(8,128)(2,1)S(1)}, bf16[2,440,128]{2,1,0:T(8,128)(2,1)S(1)}, u32[]{:S(2)}, u32[]{:S(2)}) collective-permute-start(bf16[2,440,128]{2,1,0:T(8,128)(2,1)S(1)} %upper.1), channel_id=1, source_target_pairs={{0,16},{16,0},{32,48},{48,32},{64,80},{80,64},{96,112},{112,96},{1... | collective-permute-start | bytes 675848 | tf_op jit(solution)/shard_map/ppermute | solution.py:553
  45.5 7.3 %collective-permute-start.15 = (bf16[2,440,128]{2,1,0:T(8,128)(2,1)S(1)}, bf16[2,440,128]{2,1,0:T(8,128)(2,1)S(1)}, u32[]{:S(2)}, u32[]{:S(2)}) collective-permute-start(bf16[2,440,128]{2,1,0:T(8,128)(2,1)S(1)} %upper.1), channel_id=1, source_target_pairs={{16,32},{32,16},{48,64},{64,48},{80,96},{96,80},{17,33},{33,17},{4... | collective-permute-start | bytes 675848 | tf_op jit(solution)/shard_map/ppermute | solution.py:554
  54.8 15.4 %all-to-all-start = ((f32[128,1,2]{2,1,0:T(1,128)}), f32[128,1,2]{2,1,0:T(1,128)S(1)}, u32[]{:S(2)}, u32[]{:S(2)}) async-start(f32[128,1,2]{2,1,0:T(1,128)} %bitcast.7), calls=%async_computation | async-start | bytes 131072 | tf_op jit(solution)/shard_map/all_to_all | solution.py:579
where the time goes:
time: 71.1 us; the launch traced here: 70.9 us
  starting transfers between devices  34.7 us (49%)
  waiting for transfers between devices  17.1 us (24%)
  Pallas kernels  16.9 us (24%)
  local copies, waits for them, and re-layouts  1.12 us (2%)
  between operations  0.83 us (1%)
    ppermute x10, starting transfers between devices, swapped(): lax.ppermute(x, axis, [(i, i ^ flip) for i in range(lax.axis_size(axis))])  15.4 us
    pallas_call x8, Pallas kernels, call(): pl.pallas_call(kernel, in_specs=[vmem] * len(operands), out_specs=[vmem]...  14.6 us
    all_to_all x1, waiting for transfers between devices, per_device(): lax.all_to_all(estimates, ('frame', 'refl'), split_axis=0, concat_axis=0,...  7.85 us
    ppermute x10, waiting for transfers between devices, swapped(): lax.ppermute(x, axis, [(i, i ^ flip) for i in range(lax.axis_size(axis))])  6.11 us
    all_to_all x1, starting transfers between devices, per_device(): lax.all_to_all(estimates, ('frame', 'refl'), split_axis=0, concat_axis=0,...  5.83 us
    ppermute x1, starting transfers between devices, per_device(): upper_core = lax.ppermute(upper_grids, 'frame', pairs_even(slabs))  4.23 us
    ppermute x1, starting transfers between devices, per_device(): from_chip = lax.ppermute(chip, 'frame', pairs_odd(slabs))  3.19 us
    ppermute x1, waiting for transfers between devices, per_device(): upper_chip = lax.ppermute(upper_grids, 'frame', pairs_odd(slabs))  3.09 us
  transfers between devices with their start and end apart: 17, of which 8 were waited for; matrix products, arithmetic and copies ran while one was open for 0% of the time, Pallas kernels for 12%

commit v1 on v0

--- a/solution.py
+++ b/solution.py
@@ -19,7 +19,7 @@
 HALF_ROWS = HALF_BINS * PLANE
 FULL_ROWS = GRID * PLANE
 WIDE_ROWS = 896
-PARAMS = pltpu.CompilerParams(vmem_limit_bytes=48 * 1024 * 1024)
+PARAMS = pltpu.CompilerParams(vmem_limit_bytes=24 * 1024 * 1024)
 
 
 def tent_values():
@@ -145,14 +145,13 @@
 
 def column_tents(column, columns, tents):
     offset = shoebox_offsets(column, columns)
-    centre = (offset.astype(jnp.float32) + 0.5) * (GRID / SB_EDGE)
+    offset = jnp.where(offset < 0, -2, jnp.where(offset >= SB_EDGE, SB_EDGE + 1, offset))
+    centre = (offset.astype(jnp.float32) + 0.5) * (GRID / SB_EDGE) - GRID / 2
+    centre = centre.astype(jnp.bfloat16)
+    one, zero = jnp.bfloat16(1.0), jnp.bfloat16(0.0)
     for c in range(GRID):
-        tent = jnp.maximum(1.0 - jnp.abs(centre - (c + 0.5)), 0.0)
-        if c == 0:
-            tent = jnp.where(offset >= 0, tent, 0.0)
-        if c == GRID - 1:
-            tent = jnp.where(offset < SB_EDGE, tent, 0.0)
-        tents[:, c * LANES : (c + 1) * LANES] = tent.astype(jnp.bfloat16)
+        distance = jnp.abs(centre - jnp.bfloat16(c - GRID // 2))
+        tents[:, c * LANES : (c + 1) * LANES] = jnp.maximum(one - distance, zero)
 
 
 def window_sums(x):
@@ -172,8 +171,8 @@
     count = window_sums(jnp.concatenate([count, tail], axis=1))[:, 0:columns]
     per_spread = 1.0 / jnp.maximum(count - 1.0, 1.0)
     terms[0, at : at + rows, :] = 1.0 / jnp.maximum(count, 1.0)
-    terms[1, at : at + rows, :] = per_spread
-    terms[2, at : at + rows, :] = 1.0 + 6.0 * jnp.sqrt(2.0 * per_spread)
+    terms[1, at : at + rows, :] = 2.0 * per_spread
+    terms[2, at : at + rows, :] = 2.0 + 12.0 * jnp.sqrt(2.0 * per_spread)
 
 
 def row_pair(padded, base, terms, term_row, mask_rows, live_row, strong_rows, fields, slot):
@@ -203,9 +202,12 @@
     background = total * term(0)
     variance = (square - total * background) * term(1)
     per_root = lax.rsqrt(background + 1.0)
-    excess = 2.0 * (variance * (per_root * per_root) - term(2))
-    peak = (value - background - 3.0 * jnp.sqrt(background)) * per_root
-    weight = live / ((1.0 + jnp.exp(-excess)) * (1.0 + jnp.exp(-peak)))
+    root = background * lax.rsqrt(jnp.maximum(background, 1e-30))
+    shortfall = term(2) - variance * (per_root * per_root)
+    below = (background - value + 3.0 * root) * per_root
+    gates = (1.0 + jnp.exp(shortfall)) * (1.0 + jnp.exp(below))
+    weight = pl.reciprocal(gates, approx=True)
+    weight = live * (weight * (2.0 - gates * weight))
     weight_b = weight.astype(jnp.bfloat16).astype(jnp.float32)
     value_b = value.astype(jnp.bfloat16).astype(jnp.float32)
     background_b = background.astype(jnp.bfloat16).astype(jnp.float32)
@@ -228,17 +230,15 @@
         row_pair(kept, 2 * i + 1, terms, 2 * i, live, 2 * i + 4, strong_rows, fields, i)
         return carry
 
-    lax.fori_loop(0, rows // 2, pair, 0, unroll=2)
+    lax.fori_loop(0, rows // 2, pair, 0, unroll=6)
 
 
 def half_grids(mixed, tents, anchors, spread, packed, take):
     height = mixed.shape[0] // 8
     shift = jnp.broadcast_to(anchors, (8, LANES))
-    spread[...] = dot(mixed, tents[...])
     bits = [(shift & (1 << k)) != 0 for k in range(5)]
 
-    def one_column(c, carry):
-        at = pl.ds(pl.multiple_of(c * LANES, LANES), LANES)
+    def one_column(c, spread, at):
         rows = [spread[8 * r : 8 * r + 8, at] for r in range(height)]
         rows = [
             jnp.where(bits[4], rows[r + 16], rows[r]) if r + 16 < height else rows[r]
@@ -253,10 +253,14 @@
                 if TENT[b, y] != 0.0:
                     term = rows[y] * float(TENT[b, y])
                     value = term if value is None else value + term
-            packed[pl.ds(pl.multiple_of((b * GRID + c) * 8, 8), 8), :] = value
-        return carry
-
-    lax.fori_loop(0, GRID, one_column, 0)
+            packed[(b * GRID + c) * 8 : (b * GRID + c) * 8 + 8, :] = value
+
+    for c in range(0, GRID, 2):
+        end = min(c + 2, GRID)
+        slot = spread.at[c // 2 % 2]
+        slot[:, 0 : (end - c) * LANES] = dot(mixed, tents[:, c * LANES : end * LANES])
+        for k in range(end - c):
+            one_column(c + k, slot, slice(k * LANES, (k + 1) * LANES))
     for a in range(HALF_BINS):
         take(a, packed[pl.ds(a, PLANE, stride=8), :])
 
@@ -279,7 +283,8 @@
     edge_fields,
     partner_tents,
     rows,
-    partial,
+    kept_sums,
+    sent_sums,
     padded,
     mask_rows,
     terms,
@@ -349,7 +354,10 @@
     partner_member = jnp.where((regions == partner_info[2]) & has_partner, 1.0, 0.0)
     members = jnp.concatenate([own_member, partner_member], axis=1).astype(jnp.bfloat16)
     high, low = split_two(contributions[...])
-    partial[...] = dot_nt(members, high) + dot_nt(members, low)
+    sums = dot_nt(members, high) + dot_nt(members, low)
+    early, late = sums[0 : REGIONS // 2], sums[REGIONS // 2 :]
+    kept_sums[...] = jnp.where(odd_slab, late, early)
+    sent_sums[...] = jnp.where(odd_slab, early, late)
 
 
 def grid_kernel(half, rows, mixer, edge_fields, inner_fields, tents, grids, field, spread, packed):
@@ -375,31 +383,44 @@
     strong[...] = jnp.transpose(rows[...], (1, 0, 2)).astype(jnp.bfloat16)
 
 
-def fit_kernel(sums, region, slots, lower_grids, upper_core, upper_chip, estimates, signal, back, chosen):
-    odd_slab = parity("frame")
-    total = jnp.sum(sums[...], axis=1, keepdims=True)
-    profile = sums[...] / total
+def all_regions(own_half, other_half):
+    early = jnp.where(parity("frame"), other_half[...], own_half[...])
+    late = jnp.where(parity("frame"), own_half[...], other_half[...])
+    return jnp.concatenate([early, late], axis=0)
+
+
+def fit_kernel(own_half, other_half, region, slots, lower_grids, upper_grids, estimates, signal, back, chosen):
+    sums = all_regions(own_half, other_half)
+    profile = sums / jnp.sum(sums, axis=1, keepdims=True)
     regions = lax.broadcasted_iota(jnp.int32, (REGIONS, LANES), 0)
-    member = jnp.where(regions == region[...], 1.0, 0.0)
-    chosen[...] = lax.dot_general(
-        jnp.transpose(profile, (1, 0))[0:FULL_ROWS],
-        member,
-        (((1,), (0,)), ((), ())),
-        precision=lax.Precision.HIGHEST,
-        preferred_element_type=jnp.float32,
-    )
+    member = jnp.where(regions == region[...], 1.0, 0.0).astype(jnp.bfloat16)
+    high, low = split_two(jnp.transpose(profile, (1, 0))[0:FULL_ROWS])
+    chosen[...] = dot(high, member) + dot(low, member)
     join = HALF_ROWS - PLANE
+    estimate = jnp.zeros((8, LANES), jnp.float32)
     for field, target in ((0, signal), (1, back)):
-        upper = jnp.where(odd_slab, upper_chip[field], upper_core[field]).astype(jnp.float32)
-        target[0:join] = lower_grids[field, 0:join]
-        target[join:HALF_ROWS] = lower_grids[field, join:HALF_ROWS] + upper[0:PLANE]
-        target[HALF_ROWS:] = upper[PLANE:HALF_ROWS]
-    estimate = jnp.sum(signal[...], axis=0, keepdims=True)
+        upper = upper_grids[field].astype(jnp.float32)
+        for r in range(0, FULL_ROWS, 8):
+            value = lower_grids[field, r : r + 8] if r < HALF_ROWS else None
+            if r >= join:
+                late = upper[r - join : r - join + 8]
+                value = late if value is None else value + late
+            if field == 0:
+                estimate = estimate + value
+            target[r : r + 8] = value if field == 0 else value + 1.0
+    estimate = jnp.sum(estimate, axis=0, keepdims=True)
     for _ in range(ITERS):
-        weight_var = back[...] + jnp.maximum(estimate, 0.0) * chosen[...] + 1.0
-        ratio = chosen[...] / weight_var
-        upper_sum = jnp.sum(ratio * signal[...], axis=0, keepdims=True)
-        lower_sum = jnp.sum(ratio * chosen[...], axis=0, keepdims=True)
+        level = jnp.broadcast_to(jnp.maximum(estimate, 0.0), (8, LANES))
+        sums_up = [jnp.zeros((8, LANES), jnp.float32)] * 2
+        sums_low = [jnp.zeros((8, LANES), jnp.float32)] * 2
+        for r in range(0, FULL_ROWS, 8):
+            share = chosen[r : r + 8]
+            ratio = share / (back[r : r + 8] + level * share)
+            k = r // 8 % 2
+            sums_up[k] = sums_up[k] + ratio * signal[r : r + 8]
+            sums_low[k] = sums_low[k] + ratio * share
+        upper_sum = jnp.sum(sums_up[0] + sums_up[1], axis=0, keepdims=True)
+        lower_sum = jnp.sum(sums_low[0] + sums_low[1], axis=0, keepdims=True)
         estimate = upper_sum / lower_sum
     devices = estimates.shape[0]
     target = lax.broadcasted_iota(jnp.int32, (devices, LANES), 0) * 2
@@ -408,8 +429,9 @@
         estimates[:, j : j + 1] = jnp.sum(held, axis=1, keepdims=True)
 
 
-def profile_kernel(sums, profiles):
-    profile = sums[...] / jnp.sum(sums[...], axis=1, keepdims=True)
+def profile_kernel(own_half, other_half, profiles):
+    sums = all_regions(own_half, other_half)
+    profile = sums / jnp.sum(sums, axis=1, keepdims=True)
     profiles[...] = jnp.concatenate(
         [profile[:, a * PLANE : a * PLANE + GRID * GRID] for a in range(GRID)], axis=1
     )
@@ -506,9 +528,9 @@
 
     mixer = jnp.asarray(depth_mixer(height, frames), bf16)
     field_shape = shape((height * frames, columns), bf16)
-    spread_shape = shape((height * 8, GRID * LANES))
+    spread_shape = shape((2, height * 8, 2 * LANES))
     packed_shape = shape((PLANE * 8, LANES))
-    edge_strong, edge_fields, partner_tents, rows, partial = call(
+    edge_strong, edge_fields, partner_tents, rows, kept_sums, sent_sums = call(
         spot_kernel,
         (
             kept,
@@ -525,7 +547,8 @@
             shape((3, 8 * frames, columns), bf16),
             tent_shape,
             shape((2, 1, LANES), jnp.int32),
-            shape((REGIONS, WIDE_ROWS)),
+            shape((REGIONS // 2, WIDE_ROWS)),
+            shape((REGIONS // 2, WIDE_ROWS)),
         ],
         [
             shape((2 * (HALO + 4 + HALO), frames, columns)),
@@ -538,7 +561,7 @@
         ],
         name="spots",
     )
-    sums = partial + swapped(partial, "frame", 1)
+    sums = kept_sums + swapped(sent_sums, "frame", 1)
     sums, edge_fields = lax.optimization_barrier((sums, edge_fields))
     scratch = [field_shape, spread_shape, packed_shape]
     (upper_grids,) = call(
@@ -550,10 +573,7 @@
     )
     sums = summed_over_four(sums, "refl", (1, 2, 3))
     sums, upper_grids, edge_fields = lax.optimization_barrier((sums, upper_grids, edge_fields))
-    upper_core = lax.ppermute(upper_grids, "frame", pairs_even(slabs))
-    upper_chip = lax.ppermute(upper_grids, "frame", pairs_odd(slabs))
-    sums = summed_over_four(sums, "refl", (4, 8, 12))
-    sums, edge_fields = lax.optimization_barrier((sums, edge_fields))
+    upper_grids = lax.ppermute(upper_grids, "frame", [(i + 1, i) for i in range(slabs - 1)])
     (lower_grids,) = call(
         functools.partial(grid_kernel, 0),
         (rows, mixer, edge_fields, inner_fields, own_tents),
@@ -561,7 +581,10 @@
         scratch,
         name="lower",
     )
+    sums = summed_over_four(sums, "refl", (4, 8, 12))
+    sums, lower_grids = lax.optimization_barrier((sums, lower_grids))
     sums = summed_over_four(sums, "frame", (2, 4, 6))
+    other = swapped(sums, "frame", 1)
     (strong,) = call(
         strong_kernel,
         (edge_strong, inner_strong),
@@ -571,13 +594,13 @@
     )
     (estimates,) = call(
         fit_kernel,
-        (sums, area, slots, lower_grids, upper_core, upper_chip),
+        (sums, other, area, slots, lower_grids, upper_grids),
         [shape((devices, 2))],
         [shape((FULL_ROWS, LANES))] * 3,
         name="fit",
     )
     arrived = lax.all_to_all(estimates, ("frame", "refl"), split_axis=0, concat_axis=0, tiled=True)
-    (profiles,) = call(profile_kernel, (sums,), [shape((REGIONS, GRID * GRID * GRID))], name="profiles")
+    (profiles,) = call(profile_kernel, (sums, other), [shape((REGIONS, GRID * GRID * GRID))], name="profiles")
     (intensity,) = call(spread_kernel, (arrived,), [shape((1, devices * 2))], name="intensity")
     return (strong, intensity, profiles)
 

time: 71.1 us -> 68 us (0.956)
  starting transfers between devices: 34.7 us -> 38.1 us
  waiting for transfers between devices: 17.1 us -> 13.8 us
  Pallas kernels: 16.9 us -> 13.7 us
    ppermute x10 -> x11, starting transfers between devices: 15.4 us -> 18.6 us  [swapped(): lax.ppermute(x, axis, [(i, i ^ flip) for i in range(lax.axis_size(axis))])]
    pallas_call x8, Pallas kernels: 14.6 us -> 11.4 us  [call(): pl.pallas_call(kernel, in_specs=[vmem] * len(operands), out_specs=[vmem]...]
    ppermute x2 -> x1, waiting for transfers between devices: 3.09 us -> 0.17 us  [per_device(): lax.ppermute(upper_grids, 'frame', [(i + 1, i) for i in range(slabs - 1)])]
    ppermute x10 -> x11, waiting for transfers between devices: 6.11 us -> 5.76 us  [swapped(): lax.ppermute(x, axis, [(i, i ^ flip) for i in range(lax.axis_size(axis))])]
    ppermute x2 -> x1, starting transfers between devices: 6.47 us -> 6.13 us  [per_device(): lax.ppermute(upper_grids, 'frame', [(i + 1, i) for i in range(slabs - 1)])]
  transfers between devices with their start and end apart: 17 -> 17, of which waited for: 8 -> 7; matrix products, arithmetic and copies ran while one was open for 0% -> 0% of each run, Pallas kernels for 12% -> 10%
where the time goes in v1:
time: 68 us; the launch traced here: 67.8 us
  starting transfers between devices  38.1 us (56%)
  waiting for transfers between devices  13.8 us (20%)
  Pallas kernels  13.7 us (20%)
  local copies, waits for them, and re-layouts  1.13 us (2%)
  between operations  0.86 us (1%)
    ppermute x11, starting transfers between devices, swapped(): lax.ppermute(x, axis, [(i, i ^ flip) for i in range(lax.axis_size(axis))])  18.6 us
    pallas_call x8, Pallas kernels, call(): pl.pallas_call(kernel, in_specs=[vmem] * len(operands), out_specs=[vmem]...  11.4 us
    all_to_all x1, waiting for transfers between devices, per_device(): lax.all_to_all(estimates, ('frame', 'refl'), split_axis=0, concat_axis=0,...  7.84 us
    all_to_all x1, starting transfers between devices, per_device(): lax.all_to_all(estimates, ('frame', 'refl'), split_axis=0, concat_axis=0,...  6.27 us
    ppermute x1, starting transfers between devices, per_device(): lax.ppermute(upper_grids, 'frame', [(i + 1, i) for i in range(slabs - 1)])  6.13 us
    ppermute x11, waiting for transfers between devices, swapped(): lax.ppermute(x, axis, [(i, i ^ flip) for i in range(lax.axis_size(axis))])  5.76 us
    ppermute x1, starting transfers between devices, per_device(): from_chip = lax.ppermute(chip, 'frame', pairs_odd(slabs))  3.19 us
    pallas_call x1, Pallas kernels, per_device(): pl.pallas_call(send_kernel, in_specs=[pl.BlockSpec(memory_space=pl.ANY)]...  2.26 us
  transfers between devices with their start and end apart: 17, of which 7 were waited for; matrix products, arithmetic and copies ran while one was open for 0% of the time, Pallas kernels for 10%

profile of v1, /device:TPU:1, one launch (start us, length us, event | category | flops | bytes accessed | tf_op | source)
XLA Modules:
  0.0 67.8 jit_solution(5138416977117894170)
XLA Ops:
  0.6 2.3 %sent.1 = (f32[4,8,512]{2,1,0:T(8,128)}, f32[4,8,512]{2,1,0:T(8,128)}, f32[40,512]{1,0:T(8,128)}, f32[40,512]{1,0:T(8,128)}, f32[45,8,512]{2,1,0:T(8,128)}) custom-call(f32[8,32,512]{2,1,0:T(8,128)} %image.1, f32[32,512]{1,0:T(8,128)} %gain.1, s32[32,512]{1,0:T(8,128)} %mask.1, s32[1,128]{1,0:T(1,128)} %bitcast.15, s32[1,128]{1,0:T(1,128)} %bitcast.16, ...), custom_call_target="tpu_custom_call" | custom-call | tf_op jit(solution)/shard_map/sent/pallas_call | solution.py:497
  2.9 1.5 %collective-permute-start.2 = (f32[40,512]{1,0:T(8,128)}, f32[40,512]{1,0:T(8,128)S(1)}, u32[]{:S(2)}, u32[]{:S(2)}) collective-permute-start(f32[40,512]{1,0:T(8,128)} %get-tuple-element.27), channel_id=1, source_target_pairs={{0,16},{16,0},{32,48},{48,32},{64,80},{80,64},{96,112},{112,96},{1... | collective-permute-start | bytes 245768 | tf_op jit(solution)/shard_map/ppermute | solution.py:515
  4.4 3.2 %collective-permute-start.3 = (f32[40,512]{1,0:T(8,128)}, f32[40,512]{1,0:T(8,128)S(1)}, u32[]{:S(2)}, u32[]{:S(2)}) collective-permute-start(f32[40,512]{1,0:T(8,128)} %get-tuple-element.28), channel_id=1, source_target_pairs={{16,32},{32,16},{48,64},{64,48},{80,96},{96,80},{17,33},{33,17},{4... | collective-permute-start | bytes 245768 | tf_op jit(solution)/shard_map/ppermute | solution.py:516
  7.6 1.7 %collective-permute-start = (f32[4,8,512]{2,1,0:T(8,128)}, f32[4,8,512]{2,1,0:T(8,128)S(1)}, u32[]{:S(2)}, u32[]{:S(2)}) collective-permute-start(f32[4,8,512]{2,1,0:T(8,128)} %get-tuple-element.25), channel_id=1, source_target_pairs={{0,1},{1,0},{2,3},{3,2},{4,5},{5,4},{6,7},{7,6},{8,9},{9,8},{10,11... | collective-permute-start | bytes 196616 | tf_op jit(solution)/shard_map/ppermute | solution.py:514
  10.0 1.1 %copy-done = f32[45,8,512]{2,1,0:T(8,128)S(1)} copy-done((f32[45,8,512]{2,1,0:T(8,128)S(1)}, f32[45,8,512]{2,1,0:T(8,128)}, u32[]{:S(2)}) %copy-start) | copy-done | bytes 737304
  11.1 2.7 %inner.1 = (f32[24,8,512]{2,1,0:T(8,128)S(1)}, bf16[3,192,512]{2,1,0:T(8,128)(2,1)S(1)}, bf16[512,1152]{1,0:T(8,128)(2,1)S(1)}) custom-call(f32[45,8,512]{2,1,0:T(8,128)S(1)} %copy-done), custom_call_target="tpu_custom_call" | custom-call | flops 1 | bytes 1 | tf_op jit(solution)/shard_map/inner/pallas_call | solution.py:485
  13.9 2.3 %spots.1 = (f32[8,8,512]{2,1,0:T(8,128)S(1)}, bf16[3,64,512]{2,1,0:T(8,128)(2,1)S(1)}, bf16[512,1152]{1,0:T(8,128)(2,1)S(1)}, s32[2,1,128]{2,1,0:T(1,128)S(1)}, ...) custom-call(f32[45,8,512]{2,1,0:T(8,128)S(1)} %copy-done, f32[4,8,512]{2,1,0:T(8,128)S(1)} %collective-permute-done.halo_first, ...), custom_call_target="tpu_custom_call" | custom-call | flops 1 | bytes 1 | tf_op jit(solution)/shard_map/spots/pallas_call | solution.py:485
  16.3 1.2 %collective-permute-done.4 = f32[16,896]{1,0:T(8,128)S(1)} collective-permute-done((f32[16,896]{1,0:T(8,128)S(1)}, f32[16,896]{1,0:T(8,128)S(1)}, u32[]{:S(2)}, u32[]{:S(2)}) %collective-permute-start.4) | collective-permute-done | bytes 57376 | tf_op jit(solution)/shard_map/ppermute | solution.py:464
  17.5 4.3 %collective-permute-start.5 = (bf16[16,896]{1,0:T(8,128)(2,1)S(1)}, bf16[16,896]{1,0:T(8,128)(2,1)S(1)}, u32[]{:S(2)}, u32[]{:S(2)}) collective-permute-start(bf16[16,896]{1,0:T(8,128)(2,1)S(1)} %add.40), channel_id=1, source_target_pairs={{0,1},{1,0},{2,3},{3,2},{4,5},{5,4},{6,7},{7,6},{8,9},{9,8},{10,11... | collective-permute-start | bytes 86024 | tf_op jit(solution)/shard_map/ppermute | solution.py:464
  21.8 2.0 %collective-permute-start.6 = (bf16[16,896]{1,0:T(8,128)(2,1)S(1)}, bf16[16,896]{1,0:T(8,128)(2,1)S(1)}, u32[]{:S(2)}, u32[]{:S(2)}) collective-permute-start(bf16[16,896]{1,0:T(8,128)(2,1)S(1)} %add.40), channel_id=1, source_target_pairs={{0,2},{1,3},{2,0},{3,1},{4,6},{5,7},{6,4},{7,5},{8,10},{9,11},{10,... | collective-permute-start | bytes 86024 | tf_op jit(solution)/shard_map/ppermute | solution.py:464
  24.3 1.3 %upper.1 = bf16[2,440,128]{2,1,0:T(8,128)(2,1)S(1)} custom-call(s32[2,1,128]{2,1,0:T(1,128)S(1)} %get-tuple-element.37.rows, bf16[2,256,256]{2,1,0:T(8,128)(2,1)S(1)} %copy-done.1, bf16[3,64,512]{2,1,0:T(8,128)(2,1)S(1)} %get-tuple-element.41.edge_fields, bf16[3,192,512]{2,1,0:T(8,128)(2,1)S(1)} %get-tuple-element.29.inner_fields, ...), custom_call_target="tpu_custom_call" | custom-call | flops 1 | bytes 1 | tf_op jit(solution)/shard_map/upper/pallas_call | solution.py:485
  26.0 1.7 %collective-permute-done.7 = bf16[16,896]{1,0:T(8,128)(2,1)S(1)} collective-permute-done((bf16[16,896]{1,0:T(8,128)(2,1)S(1)}, bf16[16,896]{1,0:T(8,128)(2,1)S(1)}, u32[]{:S(2)}, u32[]{:S(2)}) %collective-permute-start.7) | collective-permute-done | bytes 28704 | tf_op jit(solution)/shard_map/ppermute | solution.py:464
  27.8 1.3 %collective-permute-start.10 = (bf16[16,896]{1,0:T(8,128)(2,1)S(1)}, bf16[16,896]{1,0:T(8,128)(2,1)S(1)}, u32[]{:S(2)}, u32[]{:S(2)}) collective-permute-start(bf16[16,896]{1,0:T(8,128)(2,1)S(1)} %add_add_fusion.2), channel_id=1, source_target_pairs={{0,12},{1,13},{2,14},{3,15},{4,8},{5,9},{6,10},{7,11},{8,4},{9,5},... | collective-permute-start | bytes 86024 | tf_op jit(solution)/shard_map/ppermute | solution.py:464
  29.1 1.2 %collective-permute-start.8 = (bf16[16,896]{1,0:T(8,128)(2,1)S(1)}, bf16[16,896]{1,0:T(8,128)(2,1)S(1)}, u32[]{:S(2)}, u32[]{:S(2)}) collective-permute-start(bf16[16,896]{1,0:T(8,128)(2,1)S(1)} %add_add_fusion.2), channel_id=1, source_target_pairs={{0,4},{1,5},{2,6},{3,7},{4,0},{5,1},{6,2},{7,3},{8,12},{9,13},{10,... | collective-permute-start | bytes 86024 | tf_op jit(solution)/shard_map/ppermute | solution.py:464
  30.3 1.4 %collective-permute-start.9 = (bf16[16,896]{1,0:T(8,128)(2,1)S(1)}, bf16[16,896]{1,0:T(8,128)(2,1)S(1)}, u32[]{:S(2)}, u32[]{:S(2)}) collective-permute-start(bf16[16,896]{1,0:T(8,128)(2,1)S(1)} %add_add_fusion.2), channel_id=1, source_target_pairs={{0,8},{1,9},{2,10},{3,11},{4,12},{5,13},{6,14},{7,15},{8,0},{9,1},... | collective-permute-start | bytes 86024 | tf_op jit(solution)/shard_map/ppermute | solution.py:464
  31.7 1.3 %lower.1.lower_grids = f32[2,440,128]{2,1,0:T(8,128)S(1)} custom-call(s32[2,1,128]{2,1,0:T(1,128)S(1)} %get-tuple-element.37.rows, bf16[2,256,256]{2,1,0:T(8,128)(2,1)S(1)} %copy-done.1, bf16[3,64,512]{2,1,0:T(8,128)(2,1)S(1)} %get-tuple-element.41.edge_fields, bf16[3,192,512]{2,1,0:T(8,128)(2,1)S(1)} %get-tuple-element.29.inner_fields, ...), custom_call_target="tpu_custom_call" | custom-call | flops 1 | bytes 1 | tf_op jit(solution)/shard_map/lower/pallas_call | solution.py:485
  33.0 1.5 %collective-permute-done.9 = bf16[16,896]{1,0:T(8,128)(2,1)S(1)} collective-permute-done((bf16[16,896]{1,0:T(8,128)(2,1)S(1)}, bf16[16,896]{1,0:T(8,128)(2,1)S(1)}, u32[]{:S(2)}, u32[]{:S(2)}) %collective-permute-start.9) | collective-permute-done | bytes 28704 | tf_op jit(solution)/shard_map/ppermute | solution.py:464
  34.5 2.5 %collective-permute-start.11 = (bf16[16,896]{1,0:T(8,128)(2,1)S(1)}, bf16[16,896]{1,0:T(8,128)(2,1)S(1)}, u32[]{:S(2)}, u32[]{:S(2)}) collective-permute-start(bf16[16,896]{1,0:T(8,128)(2,1)S(1)} %add_add_fusion.1), channel_id=1, source_target_pairs={{0,32},{16,48},{32,0},{48,16},{64,96},{80,112},{96,64},{112,80},{1... | collective-permute-start | bytes 86024 | tf_op jit(solution)/shard_map/ppermute | solution.py:464
  37.0 2.3 %collective-permute-start.12 = (bf16[16,896]{1,0:T(8,128)(2,1)S(1)}, bf16[16,896]{1,0:T(8,128)(2,1)S(1)}, u32[]{:S(2)}, u32[]{:S(2)}) collective-permute-start(bf16[16,896]{1,0:T(8,128)(2,1)S(1)} %add_add_fusion.1), channel_id=1, source_target_pairs={{0,64},{16,80},{32,96},{48,112},{64,0},{80,16},{96,32},{112,48},{1... | collective-permute-start | bytes 86024 | tf_op jit(solution)/shard_map/ppermute | solution.py:464
  39.7 6.1 %collective-permute-start.15 = (bf16[2,440,128]{2,1,0:T(8,128)(2,1)S(1)}, bf16[2,440,128]{2,1,0:T(8,128)(2,1)S(1)}, u32[]{:S(2)}, u32[]{:S(2)}) collective-permute-start(bf16[2,440,128]{2,1,0:T(8,128)(2,1)S(1)} %upper.1), channel_id=1, source_target_pairs={{16,0},{32,16},{48,32},{64,48},{80,64},{96,80},{112,96},{17,1},{33... | collective-permute-start | bytes 675848 | tf_op jit(solution)/shard_map/ppermute | solution.py:576
  45.9 2.9 %collective-permute-start.14 = (f32[16,896]{1,0:T(8,128)S(1)}, f32[16,896]{1,0:T(8,128)S(1)}, u32[]{:S(2)}, u32[]{:S(2)}) collective-permute-start(f32[16,896]{1,0:T(8,128)S(1)} %add_add_fusion.own_half), channel_id=1, source_target_pairs={{0,16},{16,0},{32,48},{48,32},{64,80},{80,64},{96,112},{112,96},{1... | collective-permute-start | bytes 172040 | tf_op jit(solution)/shard_map/ppermute | solution.py:464
  49.8 1.5 %fit.1 = f32[128,2]{1,0:T(8,128)} custom-call(f32[16,896]{1,0:T(8,128)S(1)} %add_add_fusion.own_half, f32[16,896]{1,0:T(8,128)S(1)} %collective-permute-done.14.other_half, s32[1,128]{1,0:T(1,128)S(1)} %bitcast.14, s32[1,128]{1,0:T(1,128)S(1)} %bitcast_add_fusion.slots, f32[2,440,128]{2,1,0:T(8,128)S(1)} %lower.1.lower_grids, ...), custom_call_target="tpu_custom_call" | custom-call | flops 1 | bytes 1 | tf_op jit(solution)/shard_map/fit/pallas_call | solution.py:485
  51.3 6.3 %all-to-all-start = ((f32[128,1,2]{2,1,0:T(1,128)}), f32[128,1,2]{2,1,0:T(1,128)S(1)}, u32[]{:S(2)}, u32[]{:S(2)}) async-start(f32[128,1,2]{2,1,0:T(1,128)} %bitcast.7), calls=%async_computation | async-start | bytes 131072 | tf_op jit(solution)/shard_map/all_to_all | solution.py:602
  59.3 7.8 %all-to-all-done = f32[128,1,2]{2,1,0:T(1,128)S(1)} async-done(((f32[128,1,2]{2,1,0:T(1,128)}), f32[128,1,2]{2,1,0:T(1,128)S(1)}, u32[]{:S(2)}, u32[]{:S(2)}) %all-to-all-start) | async-done | bytes 1056 | tf_op jit(solution)/shard_map/all_to_all | solution.py:602
  (33 shorter events, 5.5 us)
Async XLA Ops:
  0.6 13.2 %copy-start.1 = (bf16[2,256,256]{2,1,0:T(8,128)(2,1)S(1)}, bf16[2,256,256]{2,1,0:T(8,128)(2,1)}, u32[]{:S(2)}) copy-start(bf16[2,256,256]{2,1,0:T(8,128)(2,1)} %constant.8.clone.mixer) | copy-start | bytes 786436
  2.9 10.9 %collective-permute-start.2 = (f32[40,512]{1,0:T(8,128)}, f32[40,512]{1,0:T(8,128)S(1)}, u32[]{:S(2)}, u32[]{:S(2)}) collective-permute-start(f32[40,512]{1,0:T(8,128)} %get-tuple-element.27), channel_id=1, source_target_pairs={{0,16},{16,0},{32,48},{48,32},{64,80},{80,64},{96,112},{112,96},{1... | collective-permute-start | bytes 245768 | tf_op jit(solution)/shard_map/ppermute | solution.py:515
  4.4 9.4 %collective-permute-start.3 = (f32[40,512]{1,0:T(8,128)}, f32[40,512]{1,0:T(8,128)S(1)}, u32[]{:S(2)}, u32[]{:S(2)}) collective-permute-start(f32[40,512]{1,0:T(8,128)} %get-tuple-element.28), channel_id=1, source_target_pairs={{16,32},{32,16},{48,64},{64,48},{80,96},{96,80},{17,33},{33,17},{4... | collective-permute-start | bytes 245768 | tf_op jit(solution)/shard_map/ppermute | solution.py:516
  7.6 6.2 %collective-permute-start = (f32[4,8,512]{2,1,0:T(8,128)}, f32[4,8,512]{2,1,0:T(8,128)S(1)}, u32[]{:S(2)}, u32[]{:S(2)}) collective-permute-start(f32[4,8,512]{2,1,0:T(8,128)} %get-tuple-element.25), channel_id=1, source_target_pairs={{0,1},{1,0},{2,3},{3,2},{4,5},{5,4},{6,7},{7,6},{8,9},{9,8},{10,11... | collective-permute-start | bytes 196616 | tf_op jit(solution)/shard_map/ppermute | solution.py:514
  9.3 4.5 %collective-permute-start.1 = (f32[4,8,512]{2,1,0:T(8,128)}, f32[4,8,512]{2,1,0:T(8,128)S(1)}, u32[]{:S(2)}, u32[]{:S(2)}) collective-permute-start(f32[4,8,512]{2,1,0:T(8,128)} %get-tuple-element.26), channel_id=1, source_target_pairs={{1,2},{2,1},{3,4},{4,3},{5,6},{6,5},{7,8},{8,7},{9,10},{10,9},{11,... | collective-permute-start | bytes 196616 | tf_op jit(solution)/shard_map/ppermute | solution.py:513
  10.0 1.1 %copy-start = (f32[45,8,512]{2,1,0:T(8,128)S(1)}, f32[45,8,512]{2,1,0:T(8,128)}, u32[]{:S(2)}) copy-start(f32[45,8,512]{2,1,0:T(8,128)} %get-tuple-element.24.kept) | copy-start | bytes 2211844
  16.2 1.3 %collective-permute-start.4 = (f32[16,896]{1,0:T(8,128)S(1)}, f32[16,896]{1,0:T(8,128)S(1)}, u32[]{:S(2)}, u32[]{:S(2)}) collective-permute-start(f32[16,896]{1,0:T(8,128)S(1)} %get-tuple-element.34), channel_id=1, source_target_pairs={{0,16},{16,0},{32,48},{48,32},{64,80},{80,64},{96,112},{112,96},{1... | collective-permute-start | bytes 172040 | tf_op jit(solution)/shard_map/ppermute | solution.py:464
  17.5 8.1 %collective-permute-start.5 = (bf16[16,896]{1,0:T(8,128)(2,1)S(1)}, bf16[16,896]{1,0:T(8,128)(2,1)S(1)}, u32[]{:S(2)}, u32[]{:S(2)}) collective-permute-start(bf16[16,896]{1,0:T(8,128)(2,1)S(1)} %add.40), channel_id=1, source_target_pairs={{0,1},{1,0},{2,3},{3,2},{4,5},{5,4},{6,7},{7,6},{8,9},{9,8},{10,11... | collective-permute-start | bytes 86024 | tf_op jit(solution)/shard_map/ppermute | solution.py:464
  21.8 4.2 %collective-permute-start.6 = (bf16[16,896]{1,0:T(8,128)(2,1)S(1)}, bf16[16,896]{1,0:T(8,128)(2,1)S(1)}, u32[]{:S(2)}, u32[]{:S(2)}) collective-permute-start(bf16[16,896]{1,0:T(8,128)(2,1)S(1)} %add.40), channel_id=1, source_target_pairs={{0,2},{1,3},{2,0},{3,1},{4,6},{5,7},{6,4},{7,5},{8,10},{9,11},{10,... | collective-permute-start | bytes 86024 | tf_op jit(solution)/shard_map/ppermute | solution.py:464
  23.8 3.9 %collective-permute-start.7 = (bf16[16,896]{1,0:T(8,128)(2,1)S(1)}, bf16[16,896]{1,0:T(8,128)(2,1)S(1)}, u32[]{:S(2)}, u32[]{:S(2)}) collective-permute-start(bf16[16,896]{1,0:T(8,128)(2,1)S(1)} %add.40), channel_id=1, source_target_pairs={{0,3},{1,2},{2,1},{3,0},{4,7},{5,6},{6,5},{7,4},{8,11},{9,10},{10,... | collective-permute-start | bytes 86024 | tf_op jit(solution)/shard_map/ppermute | solution.py:464
  27.7 11.8 %copy-start.3 = (s32[128,1]{0,1:T(1,128)S(1)}, s32[128,1]{0,1:T(1,128)}, u32[]{:S(2)}) copy-start(s32[128,1]{0,1:T(1,128)} %param.13) | copy-start | bytes 1540
  27.7 22.1 %copy-start.2 = (s32[128,1]{0,1:T(1,128)S(1)}, s32[128,1]{0,1:T(1,128)}, u32[]{:S(2)}) copy-start(s32[128,1]{0,1:T(1,128)} %param.14) | copy-start | bytes 1540
  27.8 5.2 %collective-permute-start.10 = (bf16[16,896]{1,0:T(8,128)(2,1)S(1)}, bf16[16,896]{1,0:T(8,128)(2,1)S(1)}, u32[]{:S(2)}, u32[]{:S(2)}) collective-permute-start(bf16[16,896]{1,0:T(8,128)(2,1)S(1)} %add_add_fusion.2), channel_id=1, source_target_pairs={{0,12},{1,13},{2,14},{3,15},{4,8},{5,9},{6,10},{7,11},{8,4},{9,5},... | collective-permute-start | bytes 86024 | tf_op jit(solution)/shard_map/ppermute | solution.py:464
  29.1 3.9 %collective-permute-start.8 = (bf16[16,896]{1,0:T(8,128)(2,1)S(1)}, bf16[16,896]{1,0:T(8,128)(2,1)S(1)}, u32[]{:S(2)}, u32[]{:S(2)}) collective-permute-start(bf16[16,896]{1,0:T(8,128)(2,1)S(1)} %add_add_fusion.2), channel_id=1, source_target_pairs={{0,4},{1,5},{2,6},{3,7},{4,0},{5,1},{6,2},{7,3},{8,12},{9,13},{10,... | collective-permute-start | bytes 86024 | tf_op jit(solution)/shard_map/ppermute | solution.py:464
  30.3 4.2 %collective-permute-start.9 = (bf16[16,896]{1,0:T(8,128)(2,1)S(1)}, bf16[16,896]{1,0:T(8,128)(2,1)S(1)}, u32[]{:S(2)}, u32[]{:S(2)}) collective-permute-start(bf16[16,896]{1,0:T(8,128)(2,1)S(1)} %add_add_fusion.2), channel_id=1, source_target_pairs={{0,8},{1,9},{2,10},{3,11},{4,12},{5,13},{6,14},{7,15},{8,0},{9,1},... | collective-permute-start | bytes 86024 | tf_op jit(solution)/shard_map/ppermute | solution.py:464
  34.5 11.3 %collective-permute-start.11 = (bf16[16,896]{1,0:T(8,128)(2,1)S(1)}, bf16[16,896]{1,0:T(8,128)(2,1)S(1)}, u32[]{:S(2)}, u32[]{:S(2)}) collective-permute-start(bf16[16,896]{1,0:T(8,128)(2,1)S(1)} %add_add_fusion.1), channel_id=1, source_target_pairs={{0,32},{16,48},{32,0},{48,16},{64,96},{80,112},{96,64},{112,80},{1... | collective-permute-start | bytes 86024 | tf_op jit(solution)/shard_map/ppermute | solution.py:464
  37.0 8.8 %collective-permute-start.12 = (bf16[16,896]{1,0:T(8,128)(2,1)S(1)}, bf16[16,896]{1,0:T(8,128)(2,1)S(1)}, u32[]{:S(2)}, u32[]{:S(2)}) collective-permute-start(bf16[16,896]{1,0:T(8,128)(2,1)S(1)} %add_add_fusion.1), channel_id=1, source_target_pairs={{0,64},{16,80},{32,96},{48,112},{64,0},{80,16},{96,32},{112,48},{1... | collective-permute-start | bytes 86024 | tf_op jit(solution)/shard_map/ppermute | solution.py:464
  39.3 6.5 %collective-permute-start.13 = (bf16[16,896]{1,0:T(8,128)(2,1)S(1)}, bf16[16,896]{1,0:T(8,128)(2,1)S(1)}, u32[]{:S(2)}, u32[]{:S(2)}) collective-permute-start(bf16[16,896]{1,0:T(8,128)(2,1)S(1)} %add_add_fusion.1), channel_id=1, source_target_pairs={{0,96},{16,112},{32,64},{48,80},{64,32},{80,48},{96,0},{112,16},{1... | collective-permute-start | bytes 86024 | tf_op jit(solution)/shard_map/ppermute | solution.py:464
  39.7 10.1 %collective-permute-start.15 = (bf16[2,440,128]{2,1,0:T(8,128)(2,1)S(1)}, bf16[2,440,128]{2,1,0:T(8,128)(2,1)S(1)}, u32[]{:S(2)}, u32[]{:S(2)}) collective-permute-start(bf16[2,440,128]{2,1,0:T(8,128)(2,1)S(1)} %upper.1), channel_id=1, source_target_pairs={{16,0},{32,16},{48,32},{64,48},{80,64},{96,80},{112,96},{17,1},{33... | collective-permute-start | bytes 675848 | tf_op jit(solution)/shard_map/ppermute | solution.py:576
  45.9 3.7 %collective-permute-start.14 = (f32[16,896]{1,0:T(8,128)S(1)}, f32[16,896]{1,0:T(8,128)S(1)}, u32[]{:S(2)}, u32[]{:S(2)}) collective-permute-start(f32[16,896]{1,0:T(8,128)S(1)} %add_add_fusion.own_half), channel_id=1, source_target_pairs={{0,16},{16,0},{32,48},{48,32},{64,80},{80,64},{96,112},{112,96},{1... | collective-permute-start | bytes 172040 | tf_op jit(solution)/shard_map/ppermute | solution.py:464
  51.3 15.8 %all-to-all-start = ((f32[128,1,2]{2,1,0:T(1,128)}), f32[128,1,2]{2,1,0:T(1,128)S(1)}, u32[]{:S(2)}, u32[]{:S(2)}) async-start(f32[128,1,2]{2,1,0:T(1,128)} %bitcast.7), calls=%async_computation | async-start | bytes 131072 | tf_op jit(solution)/shard_map/all_to_all | solution.py:602

commit v2 on v1

--- a/solution.py
+++ b/solution.py
@@ -301,8 +301,9 @@
 
     halo_a = halo_first[...]
     halo_b = halo_second[...]
-    before = jnp.where(odd_band, halo_a, halo_b)
-    after = jnp.where(odd_band, halo_b, halo_a)
+    band = lax.axis_index("refl")
+    before = jnp.where(odd_band, halo_a, jnp.where(band > 0, halo_b, 0.0))
+    after = jnp.where(odd_band, jnp.where(band < lax.axis_size("refl") - 1, halo_b, 0.0), halo_a)
     near = 4 + HALO
     padded[0:HALO] = before[0:HALO]
     padded[HALO : HALO + near] = kept[0:near]
@@ -320,6 +321,7 @@
 
     partner = jnp.where(odd_slab, from_core[...], from_chip[...])
     following = jnp.where(odd_slab, from_chip[0:height], from_core[0:height])
+    following = jnp.where(lax.axis_index("frame") < lax.axis_size("frame") - 1, following, 0.0)
     lower = kept_rows(kept, height, 1)
     upper = kept_rows(kept, height, 2)
     infos = [kept_info(kept, height, k) for k in range(3)]
@@ -397,9 +399,10 @@
     high, low = split_two(jnp.transpose(profile, (1, 0))[0:FULL_ROWS])
     chosen[...] = dot(high, member) + dot(low, member)
     join = HALF_ROWS - PLANE
+    has_following = lax.axis_index("frame") < lax.axis_size("frame") - 1
     estimate = jnp.zeros((8, LANES), jnp.float32)
     for field, target in ((0, signal), (1, back)):
-        upper = upper_grids[field].astype(jnp.float32)
+        upper = jnp.where(has_following, upper_grids[field].astype(jnp.float32), 0.0)
         for r in range(0, FULL_ROWS, 8):
             value = lower_grids[field, r : r + 8] if r < HALF_ROWS else None
             if r >= join:
@@ -457,7 +460,8 @@
 
 
 def pairs_odd(count):
-    return [(i, i + 1 if i % 2 else i - 1) for i in range(1, count - 1)]
+    inner = [(i, i + 1 if i % 2 else i - 1) for i in range(1, count - 1)]
+    return [(0, 0)] + inner + [(count - 1, count - 1)]
 
 
 def swapped(x, axis, flip):
@@ -573,7 +577,7 @@
     )
     sums = summed_over_four(sums, "refl", (1, 2, 3))
     sums, upper_grids, edge_fields = lax.optimization_barrier((sums, upper_grids, edge_fields))
-    upper_grids = lax.ppermute(upper_grids, "frame", [(i + 1, i) for i in range(slabs - 1)])
+    upper_grids = lax.ppermute(upper_grids, "frame", [((i + 1) % slabs, i) for i in range(slabs)])
     (lower_grids,) = call(
         functools.partial(grid_kernel, 0),
         (rows, mixer, edge_fields, inner_fields, own_tents),

time: 68 us -> 66.2 us (0.974)
  starting transfers between devices: 38.1 us -> 36.4 us
    ppermute x1, starting transfers between devices: 6.13 us -> 4.24 us  [per_device(): lax.ppermute(upper_grids, 'frame', [((i + 1) % slabs, i) for i in range(s...]
    all_to_all x1, starting transfers between devices: 6.27 us -> 4.55 us  [per_device(): lax.all_to_all(estimates, ('frame', 'refl'), split_axis=0, concat_axis=0,...]
    ppermute x11, starting transfers between devices: 18.6 us -> 19.7 us  [swapped(): lax.ppermute(x, axis, [(i, i ^ flip) for i in range(lax.axis_size(axis))])]
    ppermute x1, starting transfers between devices: 0.65 us -> 1.49 us  [per_device(): halo_second = lax.ppermute(second, 'refl', pairs_odd(bands))]
  transfers between devices with their start and end apart: 17 -> 17, of which waited for: 7 -> 6; matrix products, arithmetic and copies ran while one was open for 0% -> 0% of each run, Pallas kernels for 10% -> 11%
where the time goes in v2:
time: 66.2 us; the launch traced here: 65.9 us
  starting transfers between devices  36.4 us (55%)
  Pallas kernels  13.7 us (21%)
  waiting for transfers between devices  13.6 us (21%)
  local copies, waits for them, and re-layouts  1.13 us (2%)
  between operations  0.82 us (1%)
    ppermute x11, starting transfers between devices, swapped(): lax.ppermute(x, axis, [(i, i ^ flip) for i in range(lax.axis_size(axis))])  19.7 us
    pallas_call x8, Pallas kernels, call(): pl.pallas_call(kernel, in_specs=[vmem] * len(operands), out_specs=[vmem]...  11.4 us
    all_to_all x1, waiting for transfers between devices, per_device(): lax.all_to_all(estimates, ('frame', 'refl'), split_axis=0, concat_axis=0,...  7.84 us
    ppermute x11, waiting for transfers between devices, swapped(): lax.ppermute(x, axis, [(i, i ^ flip) for i in range(lax.axis_size(axis))])  5.76 us
    all_to_all x1, starting transfers between devices, per_device(): lax.all_to_all(estimates, ('frame', 'refl'), split_axis=0, concat_axis=0,...  4.55 us
    ppermute x1, starting transfers between devices, per_device(): lax.ppermute(upper_grids, 'frame', [((i + 1) % slabs, i) for i in range(s...  4.24 us
    ppermute x1, starting transfers between devices, per_device(): from_chip = lax.ppermute(chip, 'frame', pairs_odd(slabs))  3.19 us
    pallas_call x1, Pallas kernels, per_device(): pl.pallas_call(send_kernel, in_specs=[pl.BlockSpec(memory_space=pl.ANY)]...  2.26 us
  transfers between devices with their start and end apart: 17, of which 6 were waited for; matrix products, arithmetic and copies ran while one was open for 0% of the time, Pallas kernels for 11%

profile of v2, /device:TPU:1, one launch (start us, length us, event | category | flops | bytes accessed | tf_op | source)
XLA Modules:
  0.0 65.9 jit_solution(2200647690660875265)
XLA Ops:
  0.6 2.3 %sent.1 = (f32[4,8,512]{2,1,0:T(8,128)}, f32[4,8,512]{2,1,0:T(8,128)}, f32[40,512]{1,0:T(8,128)}, f32[40,512]{1,0:T(8,128)}, f32[45,8,512]{2,1,0:T(8,128)}) custom-call(f32[8,32,512]{2,1,0:T(8,128)} %image.1, f32[32,512]{1,0:T(8,128)} %gain.1, s32[32,512]{1,0:T(8,128)} %mask.1, s32[1,128]{1,0:T(1,128)} %bitcast.15, s32[1,128]{1,0:T(1,128)} %bitcast.16, ...), custom_call_target="tpu_custom_call" | custom-call | tf_op jit(solution)/shard_map/sent/pallas_call | solution.py:501
  2.9 1.5 %collective-permute-start.2 = (f32[40,512]{1,0:T(8,128)}, f32[40,512]{1,0:T(8,128)S(1)}, u32[]{:S(2)}, u32[]{:S(2)}) collective-permute-start(f32[40,512]{1,0:T(8,128)} %get-tuple-element.27), channel_id=1, source_target_pairs={{0,16},{16,0},{32,48},{48,32},{64,80},{80,64},{96,112},{112,96},{1... | collective-permute-start | bytes 245768 | tf_op jit(solution)/shard_map/ppermute | solution.py:519
  4.4 3.2 %collective-permute-start.3 = (f32[40,512]{1,0:T(8,128)}, f32[40,512]{1,0:T(8,128)S(1)}, u32[]{:S(2)}, u32[]{:S(2)}) collective-permute-start(f32[40,512]{1,0:T(8,128)} %get-tuple-element.28), channel_id=1, source_target_pairs={{0,0},{16,32},{32,16},{48,64},{64,48},{80,96},{96,80},{112,112},{1... | collective-permute-start | bytes 245768 | tf_op jit(solution)/shard_map/ppermute | solution.py:520
  7.6 1.7 %collective-permute-start = (f32[4,8,512]{2,1,0:T(8,128)}, f32[4,8,512]{2,1,0:T(8,128)S(1)}, u32[]{:S(2)}, u32[]{:S(2)}) collective-permute-start(f32[4,8,512]{2,1,0:T(8,128)} %get-tuple-element.25), channel_id=1, source_target_pairs={{0,1},{1,0},{2,3},{3,2},{4,5},{5,4},{6,7},{7,6},{8,9},{9,8},{10,11... | collective-permute-start | bytes 196616 | tf_op jit(solution)/shard_map/ppermute | solution.py:518
  9.3 1.5 %collective-permute-start.1 = (f32[4,8,512]{2,1,0:T(8,128)}, f32[4,8,512]{2,1,0:T(8,128)S(1)}, u32[]{:S(2)}, u32[]{:S(2)}) collective-permute-start(f32[4,8,512]{2,1,0:T(8,128)} %get-tuple-element.26), channel_id=1, source_target_pairs={{0,0},{1,2},{2,1},{3,4},{4,3},{5,6},{6,5},{7,8},{8,7},{9,10},{10,9... | collective-permute-start | bytes 196616 | tf_op jit(solution)/shard_map/ppermute | solution.py:517
  11.9 2.7 %inner.1 = (f32[24,8,512]{2,1,0:T(8,128)S(1)}, bf16[3,192,512]{2,1,0:T(8,128)(2,1)S(1)}, bf16[512,1152]{1,0:T(8,128)(2,1)S(1)}) custom-call(f32[45,8,512]{2,1,0:T(8,128)S(1)} %copy-done), custom_call_target="tpu_custom_call" | custom-call | flops 1 | bytes 1 | tf_op jit(solution)/shard_map/inner/pallas_call | solution.py:489
  14.7 2.3 %spots.1 = (f32[8,8,512]{2,1,0:T(8,128)S(1)}, bf16[3,64,512]{2,1,0:T(8,128)(2,1)S(1)}, bf16[512,1152]{1,0:T(8,128)(2,1)S(1)}, s32[2,1,128]{2,1,0:T(1,128)S(1)}, ...) custom-call(f32[45,8,512]{2,1,0:T(8,128)S(1)} %copy-done, f32[4,8,512]{2,1,0:T(8,128)S(1)} %collective-permute-done.halo_first, ...), custom_call_target="tpu_custom_call" | custom-call | flops 1 | bytes 1 | tf_op jit(solution)/shard_map/spots/pallas_call | solution.py:489
  17.1 1.2 %collective-permute-done.4 = f32[16,896]{1,0:T(8,128)S(1)} collective-permute-done((f32[16,896]{1,0:T(8,128)S(1)}, f32[16,896]{1,0:T(8,128)S(1)}, u32[]{:S(2)}, u32[]{:S(2)}) %collective-permute-start.4) | collective-permute-done | bytes 57376 | tf_op jit(solution)/shard_map/ppermute | solution.py:468
  18.3 3.5 %collective-permute-start.5 = (bf16[16,896]{1,0:T(8,128)(2,1)S(1)}, bf16[16,896]{1,0:T(8,128)(2,1)S(1)}, u32[]{:S(2)}, u32[]{:S(2)}) collective-permute-start(bf16[16,896]{1,0:T(8,128)(2,1)S(1)} %add.40), channel_id=1, source_target_pairs={{0,1},{1,0},{2,3},{3,2},{4,5},{5,4},{6,7},{7,6},{8,9},{9,8},{10,11... | collective-permute-start | bytes 86024 | tf_op jit(solution)/shard_map/ppermute | solution.py:468
  21.8 2.0 %collective-permute-start.6 = (bf16[16,896]{1,0:T(8,128)(2,1)S(1)}, bf16[16,896]{1,0:T(8,128)(2,1)S(1)}, u32[]{:S(2)}, u32[]{:S(2)}) collective-permute-start(bf16[16,896]{1,0:T(8,128)(2,1)S(1)} %add.40), channel_id=1, source_target_pairs={{0,2},{1,3},{2,0},{3,1},{4,6},{5,7},{6,4},{7,5},{8,10},{9,11},{10,... | collective-permute-start | bytes 86024 | tf_op jit(solution)/shard_map/ppermute | solution.py:468
  24.3 1.3 %upper.1 = bf16[2,440,128]{2,1,0:T(8,128)(2,1)S(1)} custom-call(s32[2,1,128]{2,1,0:T(1,128)S(1)} %get-tuple-element.37.rows, bf16[2,256,256]{2,1,0:T(8,128)(2,1)S(1)} %copy-done.1, bf16[3,64,512]{2,1,0:T(8,128)(2,1)S(1)} %get-tuple-element.41.edge_fields, bf16[3,192,512]{2,1,0:T(8,128)(2,1)S(1)} %get-tuple-element.29.inner_fields, ...), custom_call_target="tpu_custom_call" | custom-call | flops 1 | bytes 1 | tf_op jit(solution)/shard_map/upper/pallas_call | solution.py:489
  26.0 1.7 %collective-permute-done.7 = bf16[16,896]{1,0:T(8,128)(2,1)S(1)} collective-permute-done((bf16[16,896]{1,0:T(8,128)(2,1)S(1)}, bf16[16,896]{1,0:T(8,128)(2,1)S(1)}, u32[]{:S(2)}, u32[]{:S(2)}) %collective-permute-start.7) | collective-permute-done | bytes 28704 | tf_op jit(solution)/shard_map/ppermute | solution.py:468
  27.8 1.3 %collective-permute-start.10 = (bf16[16,896]{1,0:T(8,128)(2,1)S(1)}, bf16[16,896]{1,0:T(8,128)(2,1)S(1)}, u32[]{:S(2)}, u32[]{:S(2)}) collective-permute-start(bf16[16,896]{1,0:T(8,128)(2,1)S(1)} %add_add_fusion.2), channel_id=1, source_target_pairs={{0,12},{1,13},{2,14},{3,15},{4,8},{5,9},{6,10},{7,11},{8,4},{9,5},... | collective-permute-start | bytes 86024 | tf_op jit(solution)/shard_map/ppermute | solution.py:468
  29.1 1.2 %collective-permute-start.8 = (bf16[16,896]{1,0:T(8,128)(2,1)S(1)}, bf16[16,896]{1,0:T(8,128)(2,1)S(1)}, u32[]{:S(2)}, u32[]{:S(2)}) collective-permute-start(bf16[16,896]{1,0:T(8,128)(2,1)S(1)} %add_add_fusion.2), channel_id=1, source_target_pairs={{0,4},{1,5},{2,6},{3,7},{4,0},{5,1},{6,2},{7,3},{8,12},{9,13},{10,... | collective-permute-start | bytes 86024 | tf_op jit(solution)/shard_map/ppermute | solution.py:468
  30.3 1.4 %collective-permute-start.9 = (bf16[16,896]{1,0:T(8,128)(2,1)S(1)}, bf16[16,896]{1,0:T(8,128)(2,1)S(1)}, u32[]{:S(2)}, u32[]{:S(2)}) collective-permute-start(bf16[16,896]{1,0:T(8,128)(2,1)S(1)} %add_add_fusion.2), channel_id=1, source_target_pairs={{0,8},{1,9},{2,10},{3,11},{4,12},{5,13},{6,14},{7,15},{8,0},{9,1},... | collective-permute-start | bytes 86024 | tf_op jit(solution)/shard_map/ppermute | solution.py:468
  31.7 1.3 %lower.1.lower_grids = f32[2,440,128]{2,1,0:T(8,128)S(1)} custom-call(s32[2,1,128]{2,1,0:T(1,128)S(1)} %get-tuple-element.37.rows, bf16[2,256,256]{2,1,0:T(8,128)(2,1)S(1)} %copy-done.1, bf16[3,64,512]{2,1,0:T(8,128)(2,1)S(1)} %get-tuple-element.41.edge_fields, bf16[3,192,512]{2,1,0:T(8,128)(2,1)S(1)} %get-tuple-element.29.inner_fields, ...), custom_call_target="tpu_custom_call" | custom-call | flops 1 | bytes 1 | tf_op jit(solution)/shard_map/lower/pallas_call | solution.py:489
  33.0 1.5 %collective-permute-done.9 = bf16[16,896]{1,0:T(8,128)(2,1)S(1)} collective-permute-done((bf16[16,896]{1,0:T(8,128)(2,1)S(1)}, bf16[16,896]{1,0:T(8,128)(2,1)S(1)}, u32[]{:S(2)}, u32[]{:S(2)}) %collective-permute-start.9) | collective-permute-done | bytes 28704 | tf_op jit(solution)/shard_map/ppermute | solution.py:468
  34.5 2.5 %collective-permute-start.11 = (bf16[16,896]{1,0:T(8,128)(2,1)S(1)}, bf16[16,896]{1,0:T(8,128)(2,1)S(1)}, u32[]{:S(2)}, u32[]{:S(2)}) collective-permute-start(bf16[16,896]{1,0:T(8,128)(2,1)S(1)} %add_add_fusion.1), channel_id=1, source_target_pairs={{0,32},{16,48},{32,0},{48,16},{64,96},{80,112},{96,64},{112,80},{1... | collective-permute-start | bytes 86024 | tf_op jit(solution)/shard_map/ppermute | solution.py:468
  37.0 2.3 %collective-permute-start.12 = (bf16[16,896]{1,0:T(8,128)(2,1)S(1)}, bf16[16,896]{1,0:T(8,128)(2,1)S(1)}, u32[]{:S(2)}, u32[]{:S(2)}) collective-permute-start(bf16[16,896]{1,0:T(8,128)(2,1)S(1)} %add_add_fusion.1), channel_id=1, source_target_pairs={{0,64},{16,80},{32,96},{48,112},{64,0},{80,16},{96,32},{112,48},{1... | collective-permute-start | bytes 86024 | tf_op jit(solution)/shard_map/ppermute | solution.py:468
  39.7 4.2 %collective-permute-start.15 = (bf16[2,440,128]{2,1,0:T(8,128)(2,1)S(1)}, bf16[2,440,128]{2,1,0:T(8,128)(2,1)S(1)}, u32[]{:S(2)}, u32[]{:S(2)}) collective-permute-start(bf16[2,440,128]{2,1,0:T(8,128)(2,1)S(1)} %upper.1), channel_id=1, source_target_pairs={{16,0},{32,16},{48,32},{64,48},{80,64},{96,80},{112,96},{0,112},{1... | collective-permute-start | bytes 675848 | tf_op jit(solution)/shard_map/ppermute | solution.py:580
  44.0 4.8 %collective-permute-start.14 = (f32[16,896]{1,0:T(8,128)S(1)}, f32[16,896]{1,0:T(8,128)S(1)}, u32[]{:S(2)}, u32[]{:S(2)}) collective-permute-start(f32[16,896]{1,0:T(8,128)S(1)} %add_add_fusion.own_half), channel_id=1, source_target_pairs={{0,16},{16,0},{32,48},{48,32},{64,80},{80,64},{96,112},{112,96},{1... | collective-permute-start | bytes 172040 | tf_op jit(solution)/shard_map/ppermute | solution.py:468
  49.7 1.5 %fit.1 = f32[128,2]{1,0:T(8,128)} custom-call(f32[16,896]{1,0:T(8,128)S(1)} %add_add_fusion.own_half, f32[16,896]{1,0:T(8,128)S(1)} %collective-permute-done.14.other_half, s32[1,128]{1,0:T(1,128)S(1)} %bitcast.14, s32[1,128]{1,0:T(1,128)S(1)} %bitcast_add_fusion.slots, f32[2,440,128]{2,1,0:T(8,128)S(1)} %lower.1.lower_grids, ...), custom_call_target="tpu_custom_call" | custom-call | flops 1 | bytes 1 | tf_op jit(solution)/shard_map/fit/pallas_call | solution.py:489
  51.1 4.6 %all-to-all-start = ((f32[128,1,2]{2,1,0:T(1,128)}), f32[128,1,2]{2,1,0:T(1,128)S(1)}, u32[]{:S(2)}, u32[]{:S(2)}) async-start(f32[128,1,2]{2,1,0:T(1,128)} %bitcast.7), calls=%async_computation | async-start | bytes 131072 | tf_op jit(solution)/shard_map/all_to_all | solution.py:606
  57.4 7.8 %all-to-all-done = f32[128,1,2]{2,1,0:T(1,128)S(1)} async-done(((f32[128,1,2]{2,1,0:T(1,128)}), f32[128,1,2]{2,1,0:T(1,128)S(1)}, u32[]{:S(2)}, u32[]{:S(2)}) %all-to-all-start) | async-done | bytes 1056 | tf_op jit(solution)/shard_map/all_to_all | solution.py:606
  (33 shorter events, 5.8 us)
Async XLA Ops:
  0.6 14.1 %copy-start.1 = (bf16[2,256,256]{2,1,0:T(8,128)(2,1)S(1)}, bf16[2,256,256]{2,1,0:T(8,128)(2,1)}, u32[]{:S(2)}) copy-start(bf16[2,256,256]{2,1,0:T(8,128)(2,1)} %constant.8.clone.mixer) | copy-start | bytes 786436
  2.9 11.8 %collective-permute-start.2 = (f32[40,512]{1,0:T(8,128)}, f32[40,512]{1,0:T(8,128)S(1)}, u32[]{:S(2)}, u32[]{:S(2)}) collective-permute-start(f32[40,512]{1,0:T(8,128)} %get-tuple-element.27), channel_id=1, source_target_pairs={{0,16},{16,0},{32,48},{48,32},{64,80},{80,64},{96,112},{112,96},{1... | collective-permute-start | bytes 245768 | tf_op jit(solution)/shard_map/ppermute | solution.py:519
  4.4 10.3 %collective-permute-start.3 = (f32[40,512]{1,0:T(8,128)}, f32[40,512]{1,0:T(8,128)S(1)}, u32[]{:S(2)}, u32[]{:S(2)}) collective-permute-start(f32[40,512]{1,0:T(8,128)} %get-tuple-element.28), channel_id=1, source_target_pairs={{0,0},{16,32},{32,16},{48,64},{64,48},{80,96},{96,80},{112,112},{1... | collective-permute-start | bytes 245768 | tf_op jit(solution)/shard_map/ppermute | solution.py:520
  7.6 7.0 %collective-permute-start = (f32[4,8,512]{2,1,0:T(8,128)}, f32[4,8,512]{2,1,0:T(8,128)S(1)}, u32[]{:S(2)}, u32[]{:S(2)}) collective-permute-start(f32[4,8,512]{2,1,0:T(8,128)} %get-tuple-element.25), channel_id=1, source_target_pairs={{0,1},{1,0},{2,3},{3,2},{4,5},{5,4},{6,7},{7,6},{8,9},{9,8},{10,11... | collective-permute-start | bytes 196616 | tf_op jit(solution)/shard_map/ppermute | solution.py:518
  9.3 5.3 %collective-permute-start.1 = (f32[4,8,512]{2,1,0:T(8,128)}, f32[4,8,512]{2,1,0:T(8,128)S(1)}, u32[]{:S(2)}, u32[]{:S(2)}) collective-permute-start(f32[4,8,512]{2,1,0:T(8,128)} %get-tuple-element.26), channel_id=1, source_target_pairs={{0,0},{1,2},{2,1},{3,4},{4,3},{5,6},{6,5},{7,8},{8,7},{9,10},{10,9... | collective-permute-start | bytes 196616 | tf_op jit(solution)/shard_map/ppermute | solution.py:517
  10.8 1.1 %copy-start = (f32[45,8,512]{2,1,0:T(8,128)S(1)}, f32[45,8,512]{2,1,0:T(8,128)}, u32[]{:S(2)}) copy-start(f32[45,8,512]{2,1,0:T(8,128)} %get-tuple-element.24.kept) | copy-start | bytes 2211844
  17.0 1.3 %collective-permute-start.4 = (f32[16,896]{1,0:T(8,128)S(1)}, f32[16,896]{1,0:T(8,128)S(1)}, u32[]{:S(2)}, u32[]{:S(2)}) collective-permute-start(f32[16,896]{1,0:T(8,128)S(1)} %get-tuple-element.34), channel_id=1, source_target_pairs={{0,16},{16,0},{32,48},{48,32},{64,80},{80,64},{96,112},{112,96},{1... | collective-permute-start | bytes 172040 | tf_op jit(solution)/shard_map/ppermute | solution.py:468
  18.3 7.2 %collective-permute-start.5 = (bf16[16,896]{1,0:T(8,128)(2,1)S(1)}, bf16[16,896]{1,0:T(8,128)(2,1)S(1)}, u32[]{:S(2)}, u32[]{:S(2)}) collective-permute-start(bf16[16,896]{1,0:T(8,128)(2,1)S(1)} %add.40), channel_id=1, source_target_pairs={{0,1},{1,0},{2,3},{3,2},{4,5},{5,4},{6,7},{7,6},{8,9},{9,8},{10,11... | collective-permute-start | bytes 86024 | tf_op jit(solution)/shard_map/ppermute | solution.py:468
  21.8 4.2 %collective-permute-start.6 = (bf16[16,896]{1,0:T(8,128)(2,1)S(1)}, bf16[16,896]{1,0:T(8,128)(2,1)S(1)}, u32[]{:S(2)}, u32[]{:S(2)}) collective-permute-start(bf16[16,896]{1,0:T(8,128)(2,1)S(1)} %add.40), channel_id=1, source_target_pairs={{0,2},{1,3},{2,0},{3,1},{4,6},{5,7},{6,4},{7,5},{8,10},{9,11},{10,... | collective-permute-start | bytes 86024 | tf_op jit(solution)/shard_map/ppermute | solution.py:468
  23.8 3.9 %collective-permute-start.7 = (bf16[16,896]{1,0:T(8,128)(2,1)S(1)}, bf16[16,896]{1,0:T(8,128)(2,1)S(1)}, u32[]{:S(2)}, u32[]{:S(2)}) collective-permute-start(bf16[16,896]{1,0:T(8,128)(2,1)S(1)} %add.40), channel_id=1, source_target_pairs={{0,3},{1,2},{2,1},{3,0},{4,7},{5,6},{6,5},{7,4},{8,11},{9,10},{10,... | collective-permute-start | bytes 86024 | tf_op jit(solution)/shard_map/ppermute | solution.py:468
  27.7 11.8 %copy-start.3 = (s32[128,1]{0,1:T(1,128)S(1)}, s32[128,1]{0,1:T(1,128)}, u32[]{:S(2)}) copy-start(s32[128,1]{0,1:T(1,128)} %param.13) | copy-start | bytes 1540
  27.8 21.9 %copy-start.2 = (s32[128,1]{0,1:T(1,128)S(1)}, s32[128,1]{0,1:T(1,128)}, u32[]{:S(2)}) copy-start(s32[128,1]{0,1:T(1,128)} %param.14) | copy-start | bytes 1540
  27.8 5.2 %collective-permute-start.10 = (bf16[16,896]{1,0:T(8,128)(2,1)S(1)}, bf16[16,896]{1,0:T(8,128)(2,1)S(1)}, u32[]{:S(2)}, u32[]{:S(2)}) collective-permute-start(bf16[16,896]{1,0:T(8,128)(2,1)S(1)} %add_add_fusion.2), channel_id=1, source_target_pairs={{0,12},{1,13},{2,14},{3,15},{4,8},{5,9},{6,10},{7,11},{8,4},{9,5},... | collective-permute-start | bytes 86024 | tf_op jit(solution)/shard_map/ppermute | solution.py:468
  29.1 3.9 %collective-permute-start.8 = (bf16[16,896]{1,0:T(8,128)(2,1)S(1)}, bf16[16,896]{1,0:T(8,128)(2,1)S(1)}, u32[]{:S(2)}, u32[]{:S(2)}) collective-permute-start(bf16[16,896]{1,0:T(8,128)(2,1)S(1)} %add_add_fusion.2), channel_id=1, source_target_pairs={{0,4},{1,5},{2,6},{3,7},{4,0},{5,1},{6,2},{7,3},{8,12},{9,13},{10,... | collective-permute-start | bytes 86024 | tf_op jit(solution)/shard_map/ppermute | solution.py:468
  30.3 4.2 %collective-permute-start.9 = (bf16[16,896]{1,0:T(8,128)(2,1)S(1)}, bf16[16,896]{1,0:T(8,128)(2,1)S(1)}, u32[]{:S(2)}, u32[]{:S(2)}) collective-permute-start(bf16[16,896]{1,0:T(8,128)(2,1)S(1)} %add_add_fusion.2), channel_id=1, source_target_pairs={{0,8},{1,9},{2,10},{3,11},{4,12},{5,13},{6,14},{7,15},{8,0},{9,1},... | collective-permute-start | bytes 86024 | tf_op jit(solution)/shard_map/ppermute | solution.py:468
  34.5 9.4 %collective-permute-start.11 = (bf16[16,896]{1,0:T(8,128)(2,1)S(1)}, bf16[16,896]{1,0:T(8,128)(2,1)S(1)}, u32[]{:S(2)}, u32[]{:S(2)}) collective-permute-start(bf16[16,896]{1,0:T(8,128)(2,1)S(1)} %add_add_fusion.1), channel_id=1, source_target_pairs={{0,32},{16,48},{32,0},{48,16},{64,96},{80,112},{96,64},{112,80},{1... | collective-permute-start | bytes 86024 | tf_op jit(solution)/shard_map/ppermute | solution.py:468
  37.0 6.9 %collective-permute-start.12 = (bf16[16,896]{1,0:T(8,128)(2,1)S(1)}, bf16[16,896]{1,0:T(8,128)(2,1)S(1)}, u32[]{:S(2)}, u32[]{:S(2)}) collective-permute-start(bf16[16,896]{1,0:T(8,128)(2,1)S(1)} %add_add_fusion.1), channel_id=1, source_target_pairs={{0,64},{16,80},{32,96},{48,112},{64,0},{80,16},{96,32},{112,48},{1... | collective-permute-start | bytes 86024 | tf_op jit(solution)/shard_map/ppermute | solution.py:468
  39.4 4.6 %collective-permute-start.13 = (bf16[16,896]{1,0:T(8,128)(2,1)S(1)}, bf16[16,896]{1,0:T(8,128)(2,1)S(1)}, u32[]{:S(2)}, u32[]{:S(2)}) collective-permute-start(bf16[16,896]{1,0:T(8,128)(2,1)S(1)} %add_add_fusion.1), channel_id=1, source_target_pairs={{0,96},{16,112},{32,64},{48,80},{64,32},{80,48},{96,0},{112,16},{1... | collective-permute-start | bytes 86024 | tf_op jit(solution)/shard_map/ppermute | solution.py:468
  39.7 9.9 %collective-permute-start.15 = (bf16[2,440,128]{2,1,0:T(8,128)(2,1)S(1)}, bf16[2,440,128]{2,1,0:T(8,128)(2,1)S(1)}, u32[]{:S(2)}, u32[]{:S(2)}) collective-permute-start(bf16[2,440,128]{2,1,0:T(8,128)(2,1)S(1)} %upper.1), channel_id=1, source_target_pairs={{16,0},{32,16},{48,32},{64,48},{80,64},{96,80},{112,96},{0,112},{1... | collective-permute-start | bytes 675848 | tf_op jit(solution)/shard_map/ppermute | solution.py:580
  44.0 5.7 %collective-permute-start.14 = (f32[16,896]{1,0:T(8,128)S(1)}, f32[16,896]{1,0:T(8,128)S(1)}, u32[]{:S(2)}, u32[]{:S(2)}) collective-permute-start(f32[16,896]{1,0:T(8,128)S(1)} %add_add_fusion.own_half), channel_id=1, source_target_pairs={{0,16},{16,0},{32,48},{48,32},{64,80},{80,64},{96,112},{112,96},{1... | collective-permute-start | bytes 172040 | tf_op jit(solution)/shard_map/ppermute | solution.py:468
  51.1 14.1 %all-to-all-start = ((f32[128,1,2]{2,1,0:T(1,128)}), f32[128,1,2]{2,1,0:T(1,128)S(1)}, u32[]{:S(2)}, u32[]{:S(2)}) async-start(f32[128,1,2]{2,1,0:T(1,128)} %bitcast.7), calls=%async_computation | async-start | bytes 131072 | tf_op jit(solution)/shard_map/all_to_all | solution.py:606

commit v3 on v2

--- a/solution.py
+++ b/solution.py
@@ -175,8 +175,7 @@
     terms[2, at : at + rows, :] = 2.0 + 12.0 * jnp.sqrt(2.0 * per_spread)
 
 
-def row_pair(padded, base, terms, term_row, mask_rows, live_row, strong_rows, fields, slot):
-    frames, columns = padded.shape[1:]
+def vertical_sums(padded, base):
     rows = [padded[base + k] for k in range(2 * HALO + 2)]
     shared = rows[1]
     for k in range(2, 2 * HALO + 1):
@@ -185,12 +184,24 @@
     shared_square = squares[1]
     for k in range(2, 2 * HALO + 1):
         shared_square = shared_square + squares[k]
-    frame_tail = jnp.zeros((2, frames, LANES), jnp.float32)
     total = jnp.stack([shared + rows[0], shared + rows[-1]])
     square = jnp.stack([shared_square + squares[0], shared_square + squares[-1]])
-    total = window_sums(jnp.concatenate([total, frame_tail], axis=2))[:, :, 0:columns]
-    square = window_sums(jnp.concatenate([square, frame_tail], axis=2))[:, :, 0:columns]
-    value = jnp.stack([rows[HALO], rows[HALO + 1]])
+    return total, square
+
+
+def row_pair(padded, base, terms, term_row, mask_rows, live_row, fields, slot):
+    frames, columns = padded.shape[1:]
+    frame_tail = jnp.zeros((2, frames, LANES), jnp.float32)
+    total, square = [
+        window_sums(jnp.concatenate([x, frame_tail], axis=2))[:, :, 0:columns]
+        for x in vertical_sums(padded, base)
+    ]
+    row_weights(total, square, padded, base, terms, term_row, mask_rows, live_row, fields, slot)
+
+
+def row_weights(total, square, padded, base, terms, term_row, mask_rows, live_row, fields, slot):
+    frames, columns = padded.shape[1:]
+    value = jnp.stack([padded[base + HALO], padded[base + HALO + 1]])
 
     def every_frame(row):
         return jnp.broadcast_to(row, (frames, columns))
@@ -208,29 +219,51 @@
     gates = (1.0 + jnp.exp(shortfall)) * (1.0 + jnp.exp(below))
     weight = pl.reciprocal(gates, approx=True)
     weight = live * (weight * (2.0 - gates * weight))
-    weight_b = weight.astype(jnp.bfloat16).astype(jnp.float32)
-    value_b = value.astype(jnp.bfloat16).astype(jnp.float32)
-    background_b = background.astype(jnp.bfloat16).astype(jnp.float32)
-    strong_rows[pl.ds(2 * slot, 2)] = weight_b
+    flat = (2 * frames, columns)
+    weight, value, background = (
+        x.reshape(flat).astype(jnp.bfloat16) for x in (weight, value, background)
+    )
     at = pl.ds(pl.multiple_of(slot * 2 * frames, 2 * frames), 2 * frames)
-    flat = (2 * frames, columns)
-    fields[0, at, :] = (value_b - background_b).reshape(flat).astype(jnp.bfloat16)
-    fields[1, at, :] = background_b.reshape(flat).astype(jnp.bfloat16)
-    fields[2, at, :] = (weight_b * value_b).reshape(flat).astype(jnp.bfloat16)
-
-
-def inner_kernel(kept, strong_rows, fields, tents, live, terms):
+    fields[0, at, :] = value - background
+    fields[1, at, :] = background
+    fields[2, at, :] = weight * value
+    fields[3, at, :] = weight
+
+
+def inner_kernel(kept, fields, tents, live, terms, parts, windows, band):
     height, columns = live.shape
     live[...] = kept_rows(kept, height, 0)
     column_tents(kept_info(kept, height, 1), columns, tents)
     rows = height - 8
     window_counts(live, 1, rows, terms, 0)
 
-    def pair(i, carry):
-        row_pair(kept, 2 * i + 1, terms, 2 * i, live, 2 * i + 4, strong_rows, fields, i)
+    frames = kept.shape[1]
+    pairs = rows // 2
+    step = 2 * frames
+
+    def down(i, carry):
+        at = pl.ds(pl.multiple_of(i * step, step), step)
+        for k, x in enumerate(vertical_sums(kept, 2 * i + 1)):
+            high, low = split_two(x.reshape(step, columns))
+            parts[k, at, 0:columns] = high
+            parts[k, at, columns:] = low
         return carry
 
-    lax.fori_loop(0, rows // 2, pair, 0, unroll=6)
+    def across(i, carry):
+        at = pl.ds(pl.multiple_of(i * step, step), step)
+        total, square = [windows[k, at, :].reshape(2, frames, columns) for k in range(2)]
+        row_weights(total, square, kept, 2 * i + 1, terms, 2 * i, live, 2 * i + 4, fields, i)
+        return carry
+
+    shape = (columns, columns)
+    apart = lax.broadcasted_iota(jnp.int32, shape, 0) - lax.broadcasted_iota(jnp.int32, shape, 1)
+    near = jnp.where(jnp.abs(apart) <= HALO, 1.0, 0.0).astype(jnp.bfloat16)
+    band[0:columns] = near
+    band[columns:] = near
+    lax.fori_loop(0, pairs, down, 0, unroll=6)
+    for k in range(2):
+        windows[k] = dot(parts[k], band[...])
+    lax.fori_loop(0, pairs, across, 0, unroll=6)
 
 
 def half_grids(mixed, tents, anchors, spread, packed, take):
@@ -279,7 +312,6 @@
     mixer,
     inner_fields,
     own_tents,
-    edge_strong,
     edge_fields,
     partner_tents,
     rows,
@@ -300,7 +332,7 @@
     has_partner = lax.axis_index("frame") > 0
 
     halo_a = halo_first[...]
-    halo_b = halo_second[...]
+    halo_b = halo_second[0 : HALO + 1]
     band = lax.axis_index("refl")
     before = jnp.where(odd_band, halo_a, jnp.where(band > 0, halo_b, 0.0))
     after = jnp.where(odd_band, jnp.where(band < lax.axis_size("refl") - 1, halo_b, 0.0), halo_a)
@@ -317,7 +349,7 @@
     window_counts(mask_rows, 5, 4, terms, 0)
     window_counts(mask_rows, 21, 4, terms, 8)
     for slot, (base, term_row, live_row) in enumerate(((0, 0, 8), (2, 2, 10), (10, 8, 24), (12, 10, 26))):
-        row_pair(padded, base, terms, term_row, mask_rows, live_row, edge_strong, edge_fields, slot)
+        row_pair(padded, base, terms, term_row, mask_rows, live_row, edge_fields, slot)
 
     partner = jnp.where(odd_slab, from_core[...], from_chip[...])
     following = jnp.where(odd_slab, from_chip[0:height], from_core[0:height])
@@ -378,11 +410,13 @@
         half_grids(mixed, tents, rows[half], spread, packed, take)
 
 
-def strong_kernel(edge_strong, inner_strong, strong, rows):
-    rows[0:4] = edge_strong[0:4]
-    rows[4 : rows.shape[0] - 4] = inner_strong[...]
-    rows[rows.shape[0] - 4 :] = edge_strong[4:]
-    strong[...] = jnp.transpose(rows[...], (1, 0, 2)).astype(jnp.bfloat16)
+def strong_kernel(edge_fields, inner_fields, strong):
+    frames, height, columns = strong.shape
+    quarter = edge_fields.shape[1] // 2
+    edges, inner = edge_fields[3].astype(jnp.float32), inner_fields[3].astype(jnp.float32)
+    rows = jnp.concatenate([edges[0:quarter], inner, edges[quarter:]], axis=0)
+    rows = rows.reshape(height, frames, columns)
+    strong[...] = jnp.transpose(rows, (1, 0, 2)).astype(jnp.bfloat16)
 
 
 def all_regions(own_half, other_half):
@@ -502,7 +536,7 @@
         send_kernel,
         in_specs=[pl.BlockSpec(memory_space=pl.ANY)] * 6,
         out_specs=[vmem] * 5,
-        out_shape=[shape((HALO + 1, frames, columns))] * 2
+        out_shape=[shape((HALO + 1, frames, columns)), shape((HALO + 3, frames, columns))]
         + [shape((height + 8, columns))] * 2
         + [shape((height + 1 + 3 * height // 8, frames, columns))],
         scratch_shapes=[
@@ -522,11 +556,17 @@
 
     inner = height - 8
     tent_shape = shape((columns, GRID * LANES), bf16)
-    inner_strong, inner_fields, own_tents = call(
+    inner_fields, own_tents = call(
         inner_kernel,
         (kept,),
-        [shape((inner, frames, columns)), shape((3, inner * frames, columns), bf16), tent_shape],
-        [shape((height, columns)), shape((3, inner, columns))],
+        [shape((4, inner * frames, columns), bf16), tent_shape],
+        [
+            shape((height, columns)),
+            shape((3, inner, columns)),
+            shape((2, inner * frames, 2 * columns), bf16),
+            shape((2, inner * frames, columns)),
+            shape((2 * columns, columns), bf16),
+        ],
         name="inner",
     )
 
@@ -534,7 +574,7 @@
     field_shape = shape((height * frames, columns), bf16)
     spread_shape = shape((2, height * 8, 2 * LANES))
     packed_shape = shape((PLANE * 8, LANES))
-    edge_strong, edge_fields, partner_tents, rows, kept_sums, sent_sums = call(
+    edge_fields, partner_tents, rows, kept_sums, sent_sums = call(
         spot_kernel,
         (
             kept,
@@ -547,8 +587,7 @@
             own_tents,
         ),
         [
-            shape((8, frames, columns)),
-            shape((3, 8 * frames, columns), bf16),
+            shape((4, 8 * frames, columns), bf16),
             tent_shape,
             shape((2, 1, LANES), jnp.int32),
             shape((REGIONS // 2, WIDE_ROWS)),
@@ -591,9 +630,8 @@
     other = swapped(sums, "frame", 1)
     (strong,) = call(
         strong_kernel,
-        (edge_strong, inner_strong),
+        (edge_fields, inner_fields),
         [shape((frames, height, columns), bf16)],
-        [shape((height, frames, columns))],
         name="strong",
     )
     (estimates,) = call(

time: 66.2 us -> 66.4 us (level)
  starting transfers between devices: 36.4 us -> 38.8 us
  waiting for transfers between devices: 13.6 us -> 12.1 us
  Pallas kernels: 13.7 us -> 13 us
    all_to_all x1, starting transfers between devices: 4.55 us -> 7.18 us  [per_device(): lax.all_to_all(estimates, ('frame', 'refl'), split_axis=0, concat_axis=0,...]
    ppermute x1, starting transfers between devices: 1.72 us -> 4.1 us  [per_device(): halo_first = lax.ppermute(first, 'refl', pairs_even(bands))]
    ppermute x11, starting transfers between devices: 19.7 us -> 17.7 us  [swapped(): lax.ppermute(x, axis, [(i, i ^ flip) for i in range(lax.axis_size(axis))])]
    ppermute x11, waiting for transfers between devices: 5.76 us -> 4.22 us  [swapped(): lax.ppermute(x, axis, [(i, i ^ flip) for i in range(lax.axis_size(axis))])]
    pallas_call x8, Pallas kernels: 11.4 us -> 10.8 us  [call(): pl.pallas_call(kernel, in_specs=[vmem] * len(operands), out_specs=[vmem]...]
  transfers between devices with their start and end apart: 17 -> 17, of which waited for: 6 -> 6; matrix products, arithmetic and copies ran while one was open for 0% -> 0% of each run, Pallas kernels for 11% -> 10%
where the time goes in v3:
time: 66.4 us; the launch traced here: 66.1 us
  starting transfers between devices  38.8 us (58%)
  Pallas kernels  13 us (20%)
  waiting for transfers between devices  12.1 us (18%)
  local copies, waits for them, and re-layouts  1.13 us (2%)
  between operations  0.82 us (1%)
    ppermute x11, starting transfers between devices, swapped(): lax.ppermute(x, axis, [(i, i ^ flip) for i in range(lax.axis_size(axis))])  17.7 us
    pallas_call x8, Pallas kernels, call(): pl.pallas_call(kernel, in_specs=[vmem] * len(operands), out_specs=[vmem]...  10.8 us
    all_to_all x1, waiting for transfers between devices, per_device(): lax.all_to_all(estimates, ('frame', 'refl'), split_axis=0, concat_axis=0,...  7.82 us
    all_to_all x1, starting transfers between devices, per_device(): lax.all_to_all(estimates, ('frame', 'refl'), split_axis=0, concat_axis=0,...  7.18 us
    ppermute x11, waiting for transfers between devices, swapped(): lax.ppermute(x, axis, [(i, i ^ flip) for i in range(lax.axis_size(axis))])  4.22 us
    ppermute x1, starting transfers between devices, per_device(): halo_first = lax.ppermute(first, 'refl', pairs_even(bands))  4.1 us
    ppermute x1, starting transfers between devices, per_device(): lax.ppermute(upper_grids, 'frame', [((i + 1) % slabs, i) for i in range(s...  3.68 us
    ppermute x1, starting transfers between devices, per_device(): from_chip = lax.ppermute(chip, 'frame', pairs_odd(slabs))  3.16 us
  transfers between devices with their start and end apart: 17, of which 6 were waited for; matrix products, arithmetic and copies ran while one was open for 0% of the time, Pallas kernels for 10%

profile of v3, /device:TPU:1, one launch (start us, length us, event | category | flops | bytes accessed | tf_op | source)
XLA Modules:
  0.0 66.1 jit_solution(13820101716672261953)
XLA Ops:
  0.6 2.3 %sent.1 = (f32[4,8,512]{2,1,0:T(8,128)}, f32[6,8,512]{2,1,0:T(8,128)}, f32[40,512]{1,0:T(8,128)}, f32[40,512]{1,0:T(8,128)}, f32[45,8,512]{2,1,0:T(8,128)}) custom-call(f32[8,32,512]{2,1,0:T(8,128)} %image.1, f32[32,512]{1,0:T(8,128)} %gain.1, s32[32,512]{1,0:T(8,128)} %mask.1, s32[1,128]{1,0:T(1,128)} %bitcast.15, s32[1,128]{1,0:T(1,128)} %bitcast.16, ...), custom_call_target="tpu_custom_call" | custom-call | tf_op jit(solution)/shard_map/sent/pallas_call | solution.py:535
  2.9 1.6 %collective-permute-start.1 = (f32[6,8,512]{2,1,0:T(8,128)}, f32[6,8,512]{2,1,0:T(8,128)S(1)}, u32[]{:S(2)}, u32[]{:S(2)}) collective-permute-start(f32[6,8,512]{2,1,0:T(8,128)} %get-tuple-element.24), channel_id=1, source_target_pairs={{0,0},{1,2},{2,1},{3,4},{4,3},{5,6},{6,5},{7,8},{8,7},{9,10},{10,9... | collective-permute-start | bytes 294920 | tf_op jit(solution)/shard_map/ppermute | solution.py:551
  4.5 1.4 %collective-permute-start.2 = (f32[40,512]{1,0:T(8,128)}, f32[40,512]{1,0:T(8,128)S(1)}, u32[]{:S(2)}, u32[]{:S(2)}) collective-permute-start(f32[40,512]{1,0:T(8,128)} %get-tuple-element.25), channel_id=1, source_target_pairs={{0,16},{16,0},{32,48},{48,32},{64,80},{80,64},{96,112},{112,96},{1... | collective-permute-start | bytes 245768 | tf_op jit(solution)/shard_map/ppermute | solution.py:553
  5.9 3.2 %collective-permute-start.3 = (f32[40,512]{1,0:T(8,128)}, f32[40,512]{1,0:T(8,128)S(1)}, u32[]{:S(2)}, u32[]{:S(2)}) collective-permute-start(f32[40,512]{1,0:T(8,128)} %get-tuple-element.26), channel_id=1, source_target_pairs={{0,0},{16,32},{32,16},{48,64},{64,48},{80,96},{96,80},{112,112},{1... | collective-permute-start | bytes 245768 | tf_op jit(solution)/shard_map/ppermute | solution.py:554
  9.1 4.1 %collective-permute-start = (f32[4,8,512]{2,1,0:T(8,128)}, f32[4,8,512]{2,1,0:T(8,128)S(1)}, u32[]{:S(2)}, u32[]{:S(2)}) collective-permute-start(f32[4,8,512]{2,1,0:T(8,128)} %get-tuple-element.23), channel_id=1, source_target_pairs={{0,1},{1,0},{2,3},{3,2},{4,5},{5,4},{6,7},{7,6},{8,9},{9,8},{10,11... | collective-permute-start | bytes 196616 | tf_op jit(solution)/shard_map/ppermute | solution.py:552
  13.2 1.1 %copy-done = f32[45,8,512]{2,1,0:T(8,128)S(1)} copy-done((f32[45,8,512]{2,1,0:T(8,128)S(1)}, f32[45,8,512]{2,1,0:T(8,128)}, u32[]{:S(2)}) %copy-start) | copy-done | bytes 737304
  14.3 2.1 %inner.1 = (bf16[4,192,512]{2,1,0:T(8,128)(2,1)S(1)}, bf16[512,1152]{1,0:T(8,128)(2,1)S(1)}) custom-call(f32[45,8,512]{2,1,0:T(8,128)S(1)} %copy-done), custom_call_target="tpu_custom_call" | custom-call | flops 1 | bytes 1 | tf_op jit(solution)/shard_map/inner/pallas_call | solution.py:523
  16.4 2.3 %spots.1 = (bf16[4,64,512]{2,1,0:T(8,128)(2,1)S(1)}, bf16[512,1152]{1,0:T(8,128)(2,1)S(1)}, s32[2,1,128]{2,1,0:T(1,128)S(1)}, f32[16,896]{1,0:T(8,128)S(1)}, f32[16,896]{1,0:T(8,128)S(1)}) custom-call(f32[45,8,512]{2,1,0:T(8,128)S(1)} %copy-done, f32[4,8,512]{2,1,0:T(8,128)S(1)} %collective-permute-done.halo_first, ...), custom_call_target="tpu_custom_call" | custom-call | flops 1 | bytes 1 | tf_op jit(solution)/shard_map/spots/pallas_call | solution.py:523
  18.8 1.2 %collective-permute-done.4 = f32[16,896]{1,0:T(8,128)S(1)} collective-permute-done((f32[16,896]{1,0:T(8,128)S(1)}, f32[16,896]{1,0:T(8,128)S(1)}, u32[]{:S(2)}, u32[]{:S(2)}) %collective-permute-start.4) | collective-permute-done | bytes 57376 | tf_op jit(solution)/shard_map/ppermute | solution.py:502
  20.2 1.5 %collective-permute-start.6 = (bf16[16,896]{1,0:T(8,128)(2,1)S(1)}, bf16[16,896]{1,0:T(8,128)(2,1)S(1)}, u32[]{:S(2)}, u32[]{:S(2)}) collective-permute-start(bf16[16,896]{1,0:T(8,128)(2,1)S(1)} %add.40), channel_id=1, source_target_pairs={{0,2},{1,3},{2,0},{3,1},{4,6},{5,7},{6,4},{7,5},{8,10},{9,11},{10,... | collective-permute-start | bytes 86024 | tf_op jit(solution)/shard_map/ppermute | solution.py:502
  21.7 2.2 %collective-permute-start.7 = (bf16[16,896]{1,0:T(8,128)(2,1)S(1)}, bf16[16,896]{1,0:T(8,128)(2,1)S(1)}, u32[]{:S(2)}, u32[]{:S(2)}) collective-permute-start(bf16[16,896]{1,0:T(8,128)(2,1)S(1)} %add.40), channel_id=1, source_target_pairs={{0,3},{1,2},{2,1},{3,0},{4,7},{5,6},{6,5},{7,4},{8,11},{9,10},{10,... | collective-permute-start | bytes 86024 | tf_op jit(solution)/shard_map/ppermute | solution.py:502
  23.9 1.3 %upper.1 = bf16[2,440,128]{2,1,0:T(8,128)(2,1)S(1)} custom-call(s32[2,1,128]{2,1,0:T(1,128)S(1)} %get-tuple-element.33.rows, bf16[2,256,256]{2,1,0:T(8,128)(2,1)S(1)} %copy-done.1, bf16[4,64,512]{2,1,0:T(8,128)(2,1)S(1)} %get-tuple-element.36.edge_fields, bf16[4,192,512]{2,1,0:T(8,128)(2,1)S(1)} %get-tuple-element.27.inner_fields, ...), custom_call_target="tpu_custom_call" | custom-call | flops 1 | bytes 1 | tf_op jit(solution)/shard_map/upper/pallas_call | solution.py:523
  25.7 3.5 %collective-permute-start.10 = (bf16[16,896]{1,0:T(8,128)(2,1)S(1)}, bf16[16,896]{1,0:T(8,128)(2,1)S(1)}, u32[]{:S(2)}, u32[]{:S(2)}) collective-permute-start(bf16[16,896]{1,0:T(8,128)(2,1)S(1)} %add_add_fusion.2), channel_id=1, source_target_pairs={{0,12},{1,13},{2,14},{3,15},{4,8},{5,9},{6,10},{7,11},{8,4},{9,5},... | collective-permute-start | bytes 86024 | tf_op jit(solution)/shard_map/ppermute | solution.py:502
  29.1 1.3 %collective-permute-start.9 = (bf16[16,896]{1,0:T(8,128)(2,1)S(1)}, bf16[16,896]{1,0:T(8,128)(2,1)S(1)}, u32[]{:S(2)}, u32[]{:S(2)}) collective-permute-start(bf16[16,896]{1,0:T(8,128)(2,1)S(1)} %add_add_fusion.2), channel_id=1, source_target_pairs={{0,8},{1,9},{2,10},{3,11},{4,12},{5,13},{6,14},{7,15},{8,0},{9,1},... | collective-permute-start | bytes 86024 | tf_op jit(solution)/shard_map/ppermute | solution.py:502
  30.4 1.3 %lower.1.lower_grids = f32[2,440,128]{2,1,0:T(8,128)S(1)} custom-call(s32[2,1,128]{2,1,0:T(1,128)S(1)} %get-tuple-element.33.rows, bf16[2,256,256]{2,1,0:T(8,128)(2,1)S(1)} %copy-done.1, bf16[4,64,512]{2,1,0:T(8,128)(2,1)S(1)} %get-tuple-element.36.edge_fields, bf16[4,192,512]{2,1,0:T(8,128)(2,1)S(1)} %get-tuple-element.27.inner_fields, ...), custom_call_target="tpu_custom_call" | custom-call | flops 1 | bytes 1 | tf_op jit(solution)/shard_map/lower/pallas_call | solution.py:523
  32.2 1.2 %collective-permute-done.9 = bf16[16,896]{1,0:T(8,128)(2,1)S(1)} collective-permute-done((bf16[16,896]{1,0:T(8,128)(2,1)S(1)}, bf16[16,896]{1,0:T(8,128)(2,1)S(1)}, u32[]{:S(2)}, u32[]{:S(2)}) %collective-permute-start.9) | collective-permute-done | bytes 28704 | tf_op jit(solution)/shard_map/ppermute | solution.py:502
  33.4 1.7 %collective-permute-start.11 = (bf16[16,896]{1,0:T(8,128)(2,1)S(1)}, bf16[16,896]{1,0:T(8,128)(2,1)S(1)}, u32[]{:S(2)}, u32[]{:S(2)}) collective-permute-start(bf16[16,896]{1,0:T(8,128)(2,1)S(1)} %add_add_fusion.1), channel_id=1, source_target_pairs={{0,32},{16,48},{32,0},{48,16},{64,96},{80,112},{96,64},{112,80},{1... | collective-permute-start | bytes 86024 | tf_op jit(solution)/shard_map/ppermute | solution.py:502
  35.1 2.3 %collective-permute-start.12 = (bf16[16,896]{1,0:T(8,128)(2,1)S(1)}, bf16[16,896]{1,0:T(8,128)(2,1)S(1)}, u32[]{:S(2)}, u32[]{:S(2)}) collective-permute-start(bf16[16,896]{1,0:T(8,128)(2,1)S(1)} %add_add_fusion.1), channel_id=1, source_target_pairs={{0,64},{16,80},{32,96},{48,112},{64,0},{80,16},{96,32},{112,48},{1... | collective-permute-start | bytes 86024 | tf_op jit(solution)/shard_map/ppermute | solution.py:502
  37.7 3.7 %collective-permute-start.15 = (bf16[2,440,128]{2,1,0:T(8,128)(2,1)S(1)}, bf16[2,440,128]{2,1,0:T(8,128)(2,1)S(1)}, u32[]{:S(2)}, u32[]{:S(2)}) collective-permute-start(bf16[2,440,128]{2,1,0:T(8,128)(2,1)S(1)} %upper.1), channel_id=1, source_target_pairs={{16,0},{32,16},{48,32},{64,48},{80,64},{96,80},{112,96},{0,112},{1... | collective-permute-start | bytes 675848 | tf_op jit(solution)/shard_map/ppermute | solution.py:619
  41.4 4.9 %collective-permute-start.14 = (f32[16,896]{1,0:T(8,128)S(1)}, f32[16,896]{1,0:T(8,128)S(1)}, u32[]{:S(2)}, u32[]{:S(2)}) collective-permute-start(f32[16,896]{1,0:T(8,128)S(1)} %add_add_fusion.own_half), channel_id=1, source_target_pairs={{0,16},{16,0},{32,48},{48,32},{64,80},{80,64},{96,112},{112,96},{1... | collective-permute-start | bytes 172040 | tf_op jit(solution)/shard_map/ppermute | solution.py:502
  46.3 0.9 %collective-permute-done.14.other_half = f32[16,896]{1,0:T(8,128)S(1)} collective-permute-done((f32[16,896]{1,0:T(8,128)S(1)}, f32[16,896]{1,0:T(8,128)S(1)}, u32[]{:S(2)}, u32[]{:S(2)}) %collective-permute-start.14) | collective-permute-done | bytes 57376 | tf_op jit(solution)/shard_map/ppermute | solution.py:502
  47.2 1.5 %fit.1 = f32[128,2]{1,0:T(8,128)} custom-call(f32[16,896]{1,0:T(8,128)S(1)} %add_add_fusion.own_half, f32[16,896]{1,0:T(8,128)S(1)} %collective-permute-done.14.other_half, s32[1,128]{1,0:T(1,128)S(1)} %bitcast.14, s32[1,128]{1,0:T(1,128)S(1)} %bitcast_add_fusion.slots, f32[2,440,128]{2,1,0:T(8,128)S(1)} %lower.1.lower_grids, ...), custom_call_target="tpu_custom_call" | custom-call | flops 1 | bytes 1 | tf_op jit(solution)/shard_map/fit/pallas_call | solution.py:523
  48.7 7.2 %all-to-all-start = ((f32[128,1,2]{2,1,0:T(1,128)}), f32[128,1,2]{2,1,0:T(1,128)S(1)}, u32[]{:S(2)}, u32[]{:S(2)}) async-start(f32[128,1,2]{2,1,0:T(1,128)} %bitcast.7), calls=%async_computation | async-start | bytes 131072 | tf_op jit(solution)/shard_map/all_to_all | solution.py:644
  57.6 7.8 %all-to-all-done = f32[128,1,2]{2,1,0:T(1,128)S(1)} async-done(((f32[128,1,2]{2,1,0:T(1,128)}), f32[128,1,2]{2,1,0:T(1,128)S(1)}, u32[]{:S(2)}, u32[]{:S(2)}) %all-to-all-start) | async-done | bytes 1056 | tf_op jit(solution)/shard_map/all_to_all | solution.py:644
  (33 shorter events, 3.9 us)
Async XLA Ops:
  0.6 15.8 %copy-start.1 = (bf16[2,256,256]{2,1,0:T(8,128)(2,1)S(1)}, bf16[2,256,256]{2,1,0:T(8,128)(2,1)}, u32[]{:S(2)}) copy-start(bf16[2,256,256]{2,1,0:T(8,128)(2,1)} %constant.8.clone.mixer) | copy-start | bytes 786436
  2.9 13.5 %collective-permute-start.1 = (f32[6,8,512]{2,1,0:T(8,128)}, f32[6,8,512]{2,1,0:T(8,128)S(1)}, u32[]{:S(2)}, u32[]{:S(2)}) collective-permute-start(f32[6,8,512]{2,1,0:T(8,128)} %get-tuple-element.24), channel_id=1, source_target_pairs={{0,0},{1,2},{2,1},{3,4},{4,3},{5,6},{6,5},{7,8},{8,7},{9,10},{10,9... | collective-permute-start | bytes 294920 | tf_op jit(solution)/shard_map/ppermute | solution.py:551
  4.5 11.9 %collective-permute-start.2 = (f32[40,512]{1,0:T(8,128)}, f32[40,512]{1,0:T(8,128)S(1)}, u32[]{:S(2)}, u32[]{:S(2)}) collective-permute-start(f32[40,512]{1,0:T(8,128)} %get-tuple-element.25), channel_id=1, source_target_pairs={{0,16},{16,0},{32,48},{48,32},{64,80},{80,64},{96,112},{112,96},{1... | collective-permute-start | bytes 245768 | tf_op jit(solution)/shard_map/ppermute | solution.py:553
  5.9 10.5 %collective-permute-start.3 = (f32[40,512]{1,0:T(8,128)}, f32[40,512]{1,0:T(8,128)S(1)}, u32[]{:S(2)}, u32[]{:S(2)}) collective-permute-start(f32[40,512]{1,0:T(8,128)} %get-tuple-element.26), channel_id=1, source_target_pairs={{0,0},{16,32},{32,16},{48,64},{64,48},{80,96},{96,80},{112,112},{1... | collective-permute-start | bytes 245768 | tf_op jit(solution)/shard_map/ppermute | solution.py:554
  9.1 7.3 %collective-permute-start = (f32[4,8,512]{2,1,0:T(8,128)}, f32[4,8,512]{2,1,0:T(8,128)S(1)}, u32[]{:S(2)}, u32[]{:S(2)}) collective-permute-start(f32[4,8,512]{2,1,0:T(8,128)} %get-tuple-element.23), channel_id=1, source_target_pairs={{0,1},{1,0},{2,3},{3,2},{4,5},{5,4},{6,7},{7,6},{8,9},{9,8},{10,11... | collective-permute-start | bytes 196616 | tf_op jit(solution)/shard_map/ppermute | solution.py:552
  13.2 1.1 %copy-start = (f32[45,8,512]{2,1,0:T(8,128)S(1)}, f32[45,8,512]{2,1,0:T(8,128)}, u32[]{:S(2)}) copy-start(f32[45,8,512]{2,1,0:T(8,128)} %get-tuple-element.22.kept) | copy-start | bytes 2211844
  18.7 1.3 %collective-permute-start.4 = (f32[16,896]{1,0:T(8,128)S(1)}, f32[16,896]{1,0:T(8,128)S(1)}, u32[]{:S(2)}, u32[]{:S(2)}) collective-permute-start(f32[16,896]{1,0:T(8,128)S(1)} %get-tuple-element.30), channel_id=1, source_target_pairs={{0,16},{16,0},{32,48},{48,32},{64,80},{80,64},{96,112},{112,96},{1... | collective-permute-start | bytes 172040 | tf_op jit(solution)/shard_map/ppermute | solution.py:502
  20.0 5.2 %collective-permute-start.5 = (bf16[16,896]{1,0:T(8,128)(2,1)S(1)}, bf16[16,896]{1,0:T(8,128)(2,1)S(1)}, u32[]{:S(2)}, u32[]{:S(2)}) collective-permute-start(bf16[16,896]{1,0:T(8,128)(2,1)S(1)} %add.40), channel_id=1, source_target_pairs={{0,1},{1,0},{2,3},{3,2},{4,5},{5,4},{6,7},{7,6},{8,9},{9,8},{10,11... | collective-permute-start | bytes 86024 | tf_op jit(solution)/shard_map/ppermute | solution.py:502
  20.2 5.0 %collective-permute-start.6 = (bf16[16,896]{1,0:T(8,128)(2,1)S(1)}, bf16[16,896]{1,0:T(8,128)(2,1)S(1)}, u32[]{:S(2)}, u32[]{:S(2)}) collective-permute-start(bf16[16,896]{1,0:T(8,128)(2,1)S(1)} %add.40), channel_id=1, source_target_pairs={{0,2},{1,3},{2,0},{3,1},{4,6},{5,7},{6,4},{7,5},{8,10},{9,11},{10,... | collective-permute-start | bytes 86024 | tf_op jit(solution)/shard_map/ppermute | solution.py:502
  21.7 3.9 %collective-permute-start.7 = (bf16[16,896]{1,0:T(8,128)(2,1)S(1)}, bf16[16,896]{1,0:T(8,128)(2,1)S(1)}, u32[]{:S(2)}, u32[]{:S(2)}) collective-permute-start(bf16[16,896]{1,0:T(8,128)(2,1)S(1)} %add.40), channel_id=1, source_target_pairs={{0,3},{1,2},{2,1},{3,0},{4,7},{5,6},{6,5},{7,4},{8,11},{9,10},{10,... | collective-permute-start | bytes 86024 | tf_op jit(solution)/shard_map/ppermute | solution.py:502
  25.7 11.9 %copy-start.3 = (s32[128,1]{0,1:T(1,128)S(1)}, s32[128,1]{0,1:T(1,128)}, u32[]{:S(2)}) copy-start(s32[128,1]{0,1:T(1,128)} %param.13) | copy-start | bytes 1540
  25.7 21.5 %copy-start.2 = (s32[128,1]{0,1:T(1,128)S(1)}, s32[128,1]{0,1:T(1,128)}, u32[]{:S(2)}) copy-start(s32[128,1]{0,1:T(1,128)} %param.14) | copy-start | bytes 1540
  25.7 6.0 %collective-permute-start.10 = (bf16[16,896]{1,0:T(8,128)(2,1)S(1)}, bf16[16,896]{1,0:T(8,128)(2,1)S(1)}, u32[]{:S(2)}, u32[]{:S(2)}) collective-permute-start(bf16[16,896]{1,0:T(8,128)(2,1)S(1)} %add_add_fusion.2), channel_id=1, source_target_pairs={{0,12},{1,13},{2,14},{3,15},{4,8},{5,9},{6,10},{7,11},{8,4},{9,5},... | collective-permute-start | bytes 86024 | tf_op jit(solution)/shard_map/ppermute | solution.py:502
  29.1 3.0 %collective-permute-start.8 = (bf16[16,896]{1,0:T(8,128)(2,1)S(1)}, bf16[16,896]{1,0:T(8,128)(2,1)S(1)}, u32[]{:S(2)}, u32[]{:S(2)}) collective-permute-start(bf16[16,896]{1,0:T(8,128)(2,1)S(1)} %add_add_fusion.2), channel_id=1, source_target_pairs={{0,4},{1,5},{2,6},{3,7},{4,0},{5,1},{6,2},{7,3},{8,12},{9,13},{10,... | collective-permute-start | bytes 86024 | tf_op jit(solution)/shard_map/ppermute | solution.py:502
  29.1 4.2 %collective-permute-start.9 = (bf16[16,896]{1,0:T(8,128)(2,1)S(1)}, bf16[16,896]{1,0:T(8,128)(2,1)S(1)}, u32[]{:S(2)}, u32[]{:S(2)}) collective-permute-start(bf16[16,896]{1,0:T(8,128)(2,1)S(1)} %add_add_fusion.2), channel_id=1, source_target_pairs={{0,8},{1,9},{2,10},{3,11},{4,12},{5,13},{6,14},{7,15},{8,0},{9,1},... | collective-permute-start | bytes 86024 | tf_op jit(solution)/shard_map/ppermute | solution.py:502
  33.4 8.0 %collective-permute-start.11 = (bf16[16,896]{1,0:T(8,128)(2,1)S(1)}, bf16[16,896]{1,0:T(8,128)(2,1)S(1)}, u32[]{:S(2)}, u32[]{:S(2)}) collective-permute-start(bf16[16,896]{1,0:T(8,128)(2,1)S(1)} %add_add_fusion.1), channel_id=1, source_target_pairs={{0,32},{16,48},{32,0},{48,16},{64,96},{80,112},{96,64},{112,80},{1... | collective-permute-start | bytes 86024 | tf_op jit(solution)/shard_map/ppermute | solution.py:502
  35.1 6.3 %collective-permute-start.12 = (bf16[16,896]{1,0:T(8,128)(2,1)S(1)}, bf16[16,896]{1,0:T(8,128)(2,1)S(1)}, u32[]{:S(2)}, u32[]{:S(2)}) collective-permute-start(bf16[16,896]{1,0:T(8,128)(2,1)S(1)} %add_add_fusion.1), channel_id=1, source_target_pairs={{0,64},{16,80},{32,96},{48,112},{64,0},{80,16},{96,32},{112,48},{1... | collective-permute-start | bytes 86024 | tf_op jit(solution)/shard_map/ppermute | solution.py:502
  37.4 4.0 %collective-permute-start.13 = (bf16[16,896]{1,0:T(8,128)(2,1)S(1)}, bf16[16,896]{1,0:T(8,128)(2,1)S(1)}, u32[]{:S(2)}, u32[]{:S(2)}) collective-permute-start(bf16[16,896]{1,0:T(8,128)(2,1)S(1)} %add_add_fusion.1), channel_id=1, source_target_pairs={{0,96},{16,112},{32,64},{48,80},{64,32},{80,48},{96,0},{112,16},{1... | collective-permute-start | bytes 86024 | tf_op jit(solution)/shard_map/ppermute | solution.py:502
  37.7 9.5 %collective-permute-start.15 = (bf16[2,440,128]{2,1,0:T(8,128)(2,1)S(1)}, bf16[2,440,128]{2,1,0:T(8,128)(2,1)S(1)}, u32[]{:S(2)}, u32[]{:S(2)}) collective-permute-start(bf16[2,440,128]{2,1,0:T(8,128)(2,1)S(1)} %upper.1), channel_id=1, source_target_pairs={{16,0},{32,16},{48,32},{64,48},{80,64},{96,80},{112,96},{0,112},{1... | collective-permute-start | bytes 675848 | tf_op jit(solution)/shard_map/ppermute | solution.py:619
  41.4 5.8 %collective-permute-start.14 = (f32[16,896]{1,0:T(8,128)S(1)}, f32[16,896]{1,0:T(8,128)S(1)}, u32[]{:S(2)}, u32[]{:S(2)}) collective-permute-start(f32[16,896]{1,0:T(8,128)S(1)} %add_add_fusion.own_half), channel_id=1, source_target_pairs={{0,16},{16,0},{32,48},{48,32},{64,80},{80,64},{96,112},{112,96},{1... | collective-permute-start | bytes 172040 | tf_op jit(solution)/shard_map/ppermute | solution.py:502
  48.7 16.7 %all-to-all-start = ((f32[128,1,2]{2,1,0:T(1,128)}), f32[128,1,2]{2,1,0:T(1,128)S(1)}, u32[]{:S(2)}, u32[]{:S(2)}) async-start(f32[128,1,2]{2,1,0:T(1,128)} %bitcast.7), calls=%async_computation | async-start | bytes 131072 | tf_op jit(solution)/shard_map/all_to_all | solution.py:644

commit v4 on v2

--- a/solution.py
+++ b/solution.py
@@ -396,8 +396,11 @@
     profile = sums / jnp.sum(sums, axis=1, keepdims=True)
     regions = lax.broadcasted_iota(jnp.int32, (REGIONS, LANES), 0)
     member = jnp.where(regions == region[...], 1.0, 0.0).astype(jnp.bfloat16)
-    high, low = split_two(jnp.transpose(profile, (1, 0))[0:FULL_ROWS])
-    chosen[...] = dot(high, member) + dot(low, member)
+    both = jnp.concatenate(split_two(profile[:, 0:FULL_ROWS]), axis=0)
+    twice = jnp.concatenate([member, member], axis=0)
+    chosen[...] = lax.dot_general(
+        both, twice, (((0,), (0,)), ((), ())), preferred_element_type=jnp.float32
+    )
     join = HALF_ROWS - PLANE
     has_following = lax.axis_index("frame") < lax.axis_size("frame") - 1
     estimate = jnp.zeros((8, LANES), jnp.float32)
@@ -575,7 +578,7 @@
         scratch,
         name="upper",
     )
-    sums = summed_over_four(sums, "refl", (1, 2, 3))
+    sums = summed_over_four(sums, "refl", (4, 8, 12))
     sums, upper_grids, edge_fields = lax.optimization_barrier((sums, upper_grids, edge_fields))
     upper_grids = lax.ppermute(upper_grids, "frame", [((i + 1) % slabs, i) for i in range(slabs)])
     (lower_grids,) = call(
@@ -585,7 +588,7 @@
         scratch,
         name="lower",
     )
-    sums = summed_over_four(sums, "refl", (4, 8, 12))
+    sums = summed_over_four(sums, "refl", (1, 2, 3))
     sums, lower_grids = lax.optimization_barrier((sums, lower_grids))
     sums = summed_over_four(sums, "frame", (2, 4, 6))
     other = swapped(sums, "frame", 1)

time: 66.2 us -> 66.2 us (level)
  starting transfers between devices: 36.4 us -> 37.1 us
  waiting for transfers between devices: 13.6 us -> 12.9 us
    all_to_all x1, starting transfers between devices: 4.55 us -> 5.72 us  [per_device(): lax.all_to_all(estimates, ('frame', 'refl'), split_axis=0, concat_axis=0,...]
    ppermute x11, waiting for transfers between devices: 5.76 us -> 5.04 us  [swapped(): lax.ppermute(x, axis, [(i, i ^ flip) for i in range(lax.axis_size(axis))])]
where the time goes in v4:
time: 66.2 us; the launch traced here: 65.9 us
  starting transfers between devices  37.1 us (56%)
  Pallas kernels  13.7 us (21%)
  waiting for transfers between devices  12.9 us (19%)
  local copies, waits for them, and re-layouts  1.13 us (2%)
  between operations  0.82 us (1%)
    ppermute x11, starting transfers between devices, swapped(): lax.ppermute(x, axis, [(i, i ^ flip) for i in range(lax.axis_size(axis))])  19.6 us
    pallas_call x8, Pallas kernels, call(): pl.pallas_call(kernel, in_specs=[vmem] * len(operands), out_specs=[vmem]...  11.4 us
    all_to_all x1, waiting for transfers between devices, per_device(): lax.all_to_all(estimates, ('frame', 'refl'), split_axis=0, concat_axis=0,...  7.84 us
    all_to_all x1, starting transfers between devices, per_device(): lax.all_to_all(estimates, ('frame', 'refl'), split_axis=0, concat_axis=0,...  5.72 us
    ppermute x11, waiting for transfers between devices, swapped(): lax.ppermute(x, axis, [(i, i ^ flip) for i in range(lax.axis_size(axis))])  5.04 us
    ppermute x1, starting transfers between devices, per_device(): lax.ppermute(upper_grids, 'frame', [((i + 1) % slabs, i) for i in range(s...  3.87 us
    ppermute x1, starting transfers between devices, per_device(): from_chip = lax.ppermute(chip, 'frame', pairs_odd(slabs))  3.19 us
    pallas_call x1, Pallas kernels, per_device(): pl.pallas_call(send_kernel, in_specs=[pl.BlockSpec(memory_space=pl.ANY)]...  2.26 us
  transfers between devices with their start and end apart: 17, of which 6 were waited for; matrix products, arithmetic and copies ran while one was open for 0% of the time, Pallas kernels for 11%

profile of v4, /device:TPU:1, one launch (start us, length us, event | category | flops | bytes accessed | tf_op | source)
XLA Modules:
  0.0 65.9 jit_solution(2382675277660981419)
XLA Ops:
  0.6 2.3 %sent.1 = (f32[4,8,512]{2,1,0:T(8,128)}, f32[4,8,512]{2,1,0:T(8,128)}, f32[40,512]{1,0:T(8,128)}, f32[40,512]{1,0:T(8,128)}, f32[45,8,512]{2,1,0:T(8,128)}) custom-call(f32[8,32,512]{2,1,0:T(8,128)} %image.1, f32[32,512]{1,0:T(8,128)} %gain.1, s32[32,512]{1,0:T(8,128)} %mask.1, s32[1,128]{1,0:T(1,128)} %bitcast.15, s32[1,128]{1,0:T(1,128)} %bitcast.16, ...), custom_call_target="tpu_custom_call" | custom-call | tf_op jit(solution)/shard_map/sent/pallas_call | solution.py:504
  2.9 1.5 %collective-permute-start.2 = (f32[40,512]{1,0:T(8,128)}, f32[40,512]{1,0:T(8,128)S(1)}, u32[]{:S(2)}, u32[]{:S(2)}) collective-permute-start(f32[40,512]{1,0:T(8,128)} %get-tuple-element.27), channel_id=1, source_target_pairs={{0,16},{16,0},{32,48},{48,32},{64,80},{80,64},{96,112},{112,96},{1... | collective-permute-start | bytes 245768 | tf_op jit(solution)/shard_map/ppermute | solution.py:522
  4.4 3.2 %collective-permute-start.3 = (f32[40,512]{1,0:T(8,128)}, f32[40,512]{1,0:T(8,128)S(1)}, u32[]{:S(2)}, u32[]{:S(2)}) collective-permute-start(f32[40,512]{1,0:T(8,128)} %get-tuple-element.28), channel_id=1, source_target_pairs={{0,0},{16,32},{32,16},{48,64},{64,48},{80,96},{96,80},{112,112},{1... | collective-permute-start | bytes 245768 | tf_op jit(solution)/shard_map/ppermute | solution.py:523
  7.6 1.7 %collective-permute-start = (f32[4,8,512]{2,1,0:T(8,128)}, f32[4,8,512]{2,1,0:T(8,128)S(1)}, u32[]{:S(2)}, u32[]{:S(2)}) collective-permute-start(f32[4,8,512]{2,1,0:T(8,128)} %get-tuple-element.25), channel_id=1, source_target_pairs={{0,1},{1,0},{2,3},{3,2},{4,5},{5,4},{6,7},{7,6},{8,9},{9,8},{10,11... | collective-permute-start | bytes 196616 | tf_op jit(solution)/shard_map/ppermute | solution.py:521
  9.3 1.5 %collective-permute-start.1 = (f32[4,8,512]{2,1,0:T(8,128)}, f32[4,8,512]{2,1,0:T(8,128)S(1)}, u32[]{:S(2)}, u32[]{:S(2)}) collective-permute-start(f32[4,8,512]{2,1,0:T(8,128)} %get-tuple-element.26), channel_id=1, source_target_pairs={{0,0},{1,2},{2,1},{3,4},{4,3},{5,6},{6,5},{7,8},{8,7},{9,10},{10,9... | collective-permute-start | bytes 196616 | tf_op jit(solution)/shard_map/ppermute | solution.py:520
  10.8 1.1 %copy-done = f32[45,8,512]{2,1,0:T(8,128)S(1)} copy-done((f32[45,8,512]{2,1,0:T(8,128)S(1)}, f32[45,8,512]{2,1,0:T(8,128)}, u32[]{:S(2)}) %copy-start) | copy-done | bytes 737304
  11.9 2.7 %inner.1 = (f32[24,8,512]{2,1,0:T(8,128)S(1)}, bf16[3,192,512]{2,1,0:T(8,128)(2,1)S(1)}, bf16[512,1152]{1,0:T(8,128)(2,1)S(1)}) custom-call(f32[45,8,512]{2,1,0:T(8,128)S(1)} %copy-done), custom_call_target="tpu_custom_call" | custom-call | flops 1 | bytes 1 | tf_op jit(solution)/shard_map/inner/pallas_call | solution.py:492
  14.7 2.3 %spots.1 = (f32[8,8,512]{2,1,0:T(8,128)S(1)}, bf16[3,64,512]{2,1,0:T(8,128)(2,1)S(1)}, bf16[512,1152]{1,0:T(8,128)(2,1)S(1)}, s32[2,1,128]{2,1,0:T(1,128)S(1)}, ...) custom-call(f32[45,8,512]{2,1,0:T(8,128)S(1)} %copy-done, f32[4,8,512]{2,1,0:T(8,128)S(1)} %collective-permute-done.halo_first, ...), custom_call_target="tpu_custom_call" | custom-call | flops 1 | bytes 1 | tf_op jit(solution)/shard_map/spots/pallas_call | solution.py:492
  17.1 1.2 %collective-permute-done.4 = f32[16,896]{1,0:T(8,128)S(1)} collective-permute-done((f32[16,896]{1,0:T(8,128)S(1)}, f32[16,896]{1,0:T(8,128)S(1)}, u32[]{:S(2)}, u32[]{:S(2)}) %collective-permute-start.4) | collective-permute-done | bytes 57376 | tf_op jit(solution)/shard_map/ppermute | solution.py:471
  18.3 3.9 %collective-permute-start.5 = (bf16[16,896]{1,0:T(8,128)(2,1)S(1)}, bf16[16,896]{1,0:T(8,128)(2,1)S(1)}, u32[]{:S(2)}, u32[]{:S(2)}) collective-permute-start(bf16[16,896]{1,0:T(8,128)(2,1)S(1)} %add.40), channel_id=1, source_target_pairs={{0,4},{1,5},{2,6},{3,7},{4,0},{5,1},{6,2},{7,3},{8,12},{9,13},{10,... | collective-permute-start | bytes 86024 | tf_op jit(solution)/shard_map/ppermute | solution.py:471
  22.3 2.7 %collective-permute-start.6 = (bf16[16,896]{1,0:T(8,128)(2,1)S(1)}, bf16[16,896]{1,0:T(8,128)(2,1)S(1)}, u32[]{:S(2)}, u32[]{:S(2)}) collective-permute-start(bf16[16,896]{1,0:T(8,128)(2,1)S(1)} %add.40), channel_id=1, source_target_pairs={{0,8},{1,9},{2,10},{3,11},{4,12},{5,13},{6,14},{7,15},{8,0},{9,1},... | collective-permute-start | bytes 86024 | tf_op jit(solution)/shard_map/ppermute | solution.py:471
  25.0 1.3 %upper.1 = bf16[2,440,128]{2,1,0:T(8,128)(2,1)S(1)} custom-call(s32[2,1,128]{2,1,0:T(1,128)S(1)} %get-tuple-element.37.rows, bf16[2,256,256]{2,1,0:T(8,128)(2,1)S(1)} %copy-done.1, bf16[3,64,512]{2,1,0:T(8,128)(2,1)S(1)} %get-tuple-element.41.edge_fields, bf16[3,192,512]{2,1,0:T(8,128)(2,1)S(1)} %get-tuple-element.29.inner_fields, ...), custom_call_target="tpu_custom_call" | custom-call | flops 1 | bytes 1 | tf_op jit(solution)/shard_map/upper/pallas_call | solution.py:492
  26.6 2.4 %collective-permute-done.7 = bf16[16,896]{1,0:T(8,128)(2,1)S(1)} collective-permute-done((bf16[16,896]{1,0:T(8,128)(2,1)S(1)}, bf16[16,896]{1,0:T(8,128)(2,1)S(1)}, u32[]{:S(2)}, u32[]{:S(2)}) %collective-permute-start.7) | collective-permute-done | bytes 28704 | tf_op jit(solution)/shard_map/ppermute | solution.py:471
  29.6 3.3 %collective-permute-start.9 = (bf16[16,896]{1,0:T(8,128)(2,1)S(1)}, bf16[16,896]{1,0:T(8,128)(2,1)S(1)}, u32[]{:S(2)}, u32[]{:S(2)}) collective-permute-start(bf16[16,896]{1,0:T(8,128)(2,1)S(1)} %add_add_fusion.2), channel_id=1, source_target_pairs={{0,2},{1,3},{2,0},{3,1},{4,6},{5,7},{6,4},{7,5},{8,10},{9,11},{10,... | collective-permute-start | bytes 86024 | tf_op jit(solution)/shard_map/ppermute | solution.py:471
  32.9 1.3 %lower.1.lower_grids = f32[2,440,128]{2,1,0:T(8,128)S(1)} custom-call(s32[2,1,128]{2,1,0:T(1,128)S(1)} %get-tuple-element.37.rows, bf16[2,256,256]{2,1,0:T(8,128)(2,1)S(1)} %copy-done.1, bf16[3,64,512]{2,1,0:T(8,128)(2,1)S(1)} %get-tuple-element.41.edge_fields, bf16[3,192,512]{2,1,0:T(8,128)(2,1)S(1)} %get-tuple-element.29.inner_fields, ...), custom_call_target="tpu_custom_call" | custom-call | flops 1 | bytes 1 | tf_op jit(solution)/shard_map/lower/pallas_call | solution.py:492
  34.5 1.7 %collective-permute-start.11 = (bf16[16,896]{1,0:T(8,128)(2,1)S(1)}, bf16[16,896]{1,0:T(8,128)(2,1)S(1)}, u32[]{:S(2)}, u32[]{:S(2)}) collective-permute-start(bf16[16,896]{1,0:T(8,128)(2,1)S(1)} %add_add_fusion.1), channel_id=1, source_target_pairs={{0,32},{16,48},{32,0},{48,16},{64,96},{80,112},{96,64},{112,80},{1... | collective-permute-start | bytes 86024 | tf_op jit(solution)/shard_map/ppermute | solution.py:471
  36.2 2.3 %collective-permute-start.12 = (bf16[16,896]{1,0:T(8,128)(2,1)S(1)}, bf16[16,896]{1,0:T(8,128)(2,1)S(1)}, u32[]{:S(2)}, u32[]{:S(2)}) collective-permute-start(bf16[16,896]{1,0:T(8,128)(2,1)S(1)} %add_add_fusion.1), channel_id=1, source_target_pairs={{0,64},{16,80},{32,96},{48,112},{64,0},{80,16},{96,32},{112,48},{1... | collective-permute-start | bytes 86024 | tf_op jit(solution)/shard_map/ppermute | solution.py:471
  38.9 3.9 %collective-permute-start.15 = (bf16[2,440,128]{2,1,0:T(8,128)(2,1)S(1)}, bf16[2,440,128]{2,1,0:T(8,128)(2,1)S(1)}, u32[]{:S(2)}, u32[]{:S(2)}) collective-permute-start(bf16[2,440,128]{2,1,0:T(8,128)(2,1)S(1)} %upper.1), channel_id=1, source_target_pairs={{16,0},{32,16},{48,32},{64,48},{80,64},{96,80},{112,96},{0,112},{1... | collective-permute-start | bytes 675848 | tf_op jit(solution)/shard_map/ppermute | solution.py:583
  42.8 4.8 %collective-permute-start.14 = (f32[16,896]{1,0:T(8,128)S(1)}, f32[16,896]{1,0:T(8,128)S(1)}, u32[]{:S(2)}, u32[]{:S(2)}) collective-permute-start(f32[16,896]{1,0:T(8,128)S(1)} %add_add_fusion.own_half), channel_id=1, source_target_pairs={{0,16},{16,0},{32,48},{48,32},{64,80},{80,64},{96,112},{112,96},{1... | collective-permute-start | bytes 172040 | tf_op jit(solution)/shard_map/ppermute | solution.py:471
  47.6 0.9 %collective-permute-done.14.other_half = f32[16,896]{1,0:T(8,128)S(1)} collective-permute-done((f32[16,896]{1,0:T(8,128)S(1)}, f32[16,896]{1,0:T(8,128)S(1)}, u32[]{:S(2)}, u32[]{:S(2)}) %collective-permute-start.14) | collective-permute-done | bytes 57376 | tf_op jit(solution)/shard_map/ppermute | solution.py:471
  48.5 1.4 %fit.1 = f32[128,2]{1,0:T(8,128)} custom-call(f32[16,896]{1,0:T(8,128)S(1)} %add_add_fusion.own_half, f32[16,896]{1,0:T(8,128)S(1)} %collective-permute-done.14.other_half, s32[1,128]{1,0:T(1,128)S(1)} %bitcast.14, s32[1,128]{1,0:T(1,128)S(1)} %bitcast_add_fusion.slots, f32[2,440,128]{2,1,0:T(8,128)S(1)} %lower.1.lower_grids, ...), custom_call_target="tpu_custom_call" | custom-call | flops 1 | bytes 1 | tf_op jit(solution)/shard_map/fit/pallas_call | solution.py:492
  49.9 5.7 %all-to-all-start = ((f32[128,1,2]{2,1,0:T(1,128)}), f32[128,1,2]{2,1,0:T(1,128)S(1)}, u32[]{:S(2)}, u32[]{:S(2)}) async-start(f32[128,1,2]{2,1,0:T(1,128)} %bitcast.7), calls=%async_computation | async-start | bytes 131072 | tf_op jit(solution)/shard_map/all_to_all | solution.py:609
  56.5 0.9 %profiles.1 = f32[32,729]{1,0:T(8,128)} custom-call(f32[16,896]{1,0:T(8,128)S(1)} %add_add_fusion.own_half, f32[16,896]{1,0:T(8,128)S(1)} %collective-permute-done.14.other_half), custom_call_target="tpu_custom_call" | custom-call | flops 1 | bytes 1 | tf_op jit(solution)/shard_map/profiles/pallas_call | solution.py:492
  57.3 7.8 %all-to-all-done = f32[128,1,2]{2,1,0:T(1,128)S(1)} async-done(((f32[128,1,2]{2,1,0:T(1,128)}), f32[128,1,2]{2,1,0:T(1,128)S(1)}, u32[]{:S(2)}, u32[]{:S(2)}) %all-to-all-start) | async-done | bytes 1056 | tf_op jit(solution)/shard_map/all_to_all | solution.py:609
  (33 shorter events, 3.2 us)
Async XLA Ops:
  0.6 14.1 %copy-start.1 = (bf16[2,256,256]{2,1,0:T(8,128)(2,1)S(1)}, bf16[2,256,256]{2,1,0:T(8,128)(2,1)}, u32[]{:S(2)}) copy-start(bf16[2,256,256]{2,1,0:T(8,128)(2,1)} %constant.8.clone.mixer) | copy-start | bytes 786436
  2.9 11.8 %collective-permute-start.2 = (f32[40,512]{1,0:T(8,128)}, f32[40,512]{1,0:T(8,128)S(1)}, u32[]{:S(2)}, u32[]{:S(2)}) collective-permute-start(f32[40,512]{1,0:T(8,128)} %get-tuple-element.27), channel_id=1, source_target_pairs={{0,16},{16,0},{32,48},{48,32},{64,80},{80,64},{96,112},{112,96},{1... | collective-permute-start | bytes 245768 | tf_op jit(solution)/shard_map/ppermute | solution.py:522
  4.4 10.3 %collective-permute-start.3 = (f32[40,512]{1,0:T(8,128)}, f32[40,512]{1,0:T(8,128)S(1)}, u32[]{:S(2)}, u32[]{:S(2)}) collective-permute-start(f32[40,512]{1,0:T(8,128)} %get-tuple-element.28), channel_id=1, source_target_pairs={{0,0},{16,32},{32,16},{48,64},{64,48},{80,96},{96,80},{112,112},{1... | collective-permute-start | bytes 245768 | tf_op jit(solution)/shard_map/ppermute | solution.py:523
  7.6 7.0 %collective-permute-start = (f32[4,8,512]{2,1,0:T(8,128)}, f32[4,8,512]{2,1,0:T(8,128)S(1)}, u32[]{:S(2)}, u32[]{:S(2)}) collective-permute-start(f32[4,8,512]{2,1,0:T(8,128)} %get-tuple-element.25), channel_id=1, source_target_pairs={{0,1},{1,0},{2,3},{3,2},{4,5},{5,4},{6,7},{7,6},{8,9},{9,8},{10,11... | collective-permute-start | bytes 196616 | tf_op jit(solution)/shard_map/ppermute | solution.py:521
  9.3 5.3 %collective-permute-start.1 = (f32[4,8,512]{2,1,0:T(8,128)}, f32[4,8,512]{2,1,0:T(8,128)S(1)}, u32[]{:S(2)}, u32[]{:S(2)}) collective-permute-start(f32[4,8,512]{2,1,0:T(8,128)} %get-tuple-element.26), channel_id=1, source_target_pairs={{0,0},{1,2},{2,1},{3,4},{4,3},{5,6},{6,5},{7,8},{8,7},{9,10},{10,9... | collective-permute-start | bytes 196616 | tf_op jit(solution)/shard_map/ppermute | solution.py:520
  10.8 1.1 %copy-start = (f32[45,8,512]{2,1,0:T(8,128)S(1)}, f32[45,8,512]{2,1,0:T(8,128)}, u32[]{:S(2)}) copy-start(f32[45,8,512]{2,1,0:T(8,128)} %get-tuple-element.24.kept) | copy-start | bytes 2211844
  17.0 1.3 %collective-permute-start.4 = (f32[16,896]{1,0:T(8,128)S(1)}, f32[16,896]{1,0:T(8,128)S(1)}, u32[]{:S(2)}, u32[]{:S(2)}) collective-permute-start(f32[16,896]{1,0:T(8,128)S(1)} %get-tuple-element.34), channel_id=1, source_target_pairs={{0,16},{16,0},{32,48},{48,32},{64,80},{80,64},{96,112},{112,96},{1... | collective-permute-start | bytes 172040 | tf_op jit(solution)/shard_map/ppermute | solution.py:471
  18.3 7.9 %collective-permute-start.5 = (bf16[16,896]{1,0:T(8,128)(2,1)S(1)}, bf16[16,896]{1,0:T(8,128)(2,1)S(1)}, u32[]{:S(2)}, u32[]{:S(2)}) collective-permute-start(bf16[16,896]{1,0:T(8,128)(2,1)S(1)} %add.40), channel_id=1, source_target_pairs={{0,4},{1,5},{2,6},{3,7},{4,0},{5,1},{6,2},{7,3},{8,12},{9,13},{10,... | collective-permute-start | bytes 86024 | tf_op jit(solution)/shard_map/ppermute | solution.py:471
  22.3 4.3 %collective-permute-start.6 = (bf16[16,896]{1,0:T(8,128)(2,1)S(1)}, bf16[16,896]{1,0:T(8,128)(2,1)S(1)}, u32[]{:S(2)}, u32[]{:S(2)}) collective-permute-start(bf16[16,896]{1,0:T(8,128)(2,1)S(1)} %add.40), channel_id=1, source_target_pairs={{0,8},{1,9},{2,10},{3,11},{4,12},{5,13},{6,14},{7,15},{8,0},{9,1},... | collective-permute-start | bytes 86024 | tf_op jit(solution)/shard_map/ppermute | solution.py:471
  25.0 3.9 %collective-permute-start.7 = (bf16[16,896]{1,0:T(8,128)(2,1)S(1)}, bf16[16,896]{1,0:T(8,128)(2,1)S(1)}, u32[]{:S(2)}, u32[]{:S(2)}) collective-permute-start(bf16[16,896]{1,0:T(8,128)(2,1)S(1)} %add.40), channel_id=1, source_target_pairs={{0,12},{1,13},{2,14},{3,15},{4,8},{5,9},{6,10},{7,11},{8,4},{9,5},... | collective-permute-start | bytes 86024 | tf_op jit(solution)/shard_map/ppermute | solution.py:471
  29.0 9.8 %copy-start.3 = (s32[128,1]{0,1:T(1,128)S(1)}, s32[128,1]{0,1:T(1,128)}, u32[]{:S(2)}) copy-start(s32[128,1]{0,1:T(1,128)} %param.13) | copy-start | bytes 1540
  29.0 19.5 %copy-start.2 = (s32[128,1]{0,1:T(1,128)S(1)}, s32[128,1]{0,1:T(1,128)}, u32[]{:S(2)}) copy-start(s32[128,1]{0,1:T(1,128)} %param.14) | copy-start | bytes 1540
  29.0 5.2 %collective-permute-start.10 = (bf16[16,896]{1,0:T(8,128)(2,1)S(1)}, bf16[16,896]{1,0:T(8,128)(2,1)S(1)}, u32[]{:S(2)}, u32[]{:S(2)}) collective-permute-start(bf16[16,896]{1,0:T(8,128)(2,1)S(1)} %add_add_fusion.2), channel_id=1, source_target_pairs={{0,3},{1,2},{2,1},{3,0},{4,7},{5,6},{6,5},{7,4},{8,11},{9,10},{10,... | collective-permute-start | bytes 86024 | tf_op jit(solution)/shard_map/ppermute | solution.py:471
  29.5 4.7 %collective-permute-start.8 = (bf16[16,896]{1,0:T(8,128)(2,1)S(1)}, bf16[16,896]{1,0:T(8,128)(2,1)S(1)}, u32[]{:S(2)}, u32[]{:S(2)}) collective-permute-start(bf16[16,896]{1,0:T(8,128)(2,1)S(1)} %add_add_fusion.2), channel_id=1, source_target_pairs={{0,1},{1,0},{2,3},{3,2},{4,5},{5,4},{6,7},{7,6},{8,9},{9,8},{10,11... | collective-permute-start | bytes 86024 | tf_op jit(solution)/shard_map/ppermute | solution.py:471
  29.6 4.9 %collective-permute-start.9 = (bf16[16,896]{1,0:T(8,128)(2,1)S(1)}, bf16[16,896]{1,0:T(8,128)(2,1)S(1)}, u32[]{:S(2)}, u32[]{:S(2)}) collective-permute-start(bf16[16,896]{1,0:T(8,128)(2,1)S(1)} %add_add_fusion.2), channel_id=1, source_target_pairs={{0,2},{1,3},{2,0},{3,1},{4,6},{5,7},{6,4},{7,5},{8,10},{9,11},{10,... | collective-permute-start | bytes 86024 | tf_op jit(solution)/shard_map/ppermute | solution.py:471
  34.5 8.3 %collective-permute-start.11 = (bf16[16,896]{1,0:T(8,128)(2,1)S(1)}, bf16[16,896]{1,0:T(8,128)(2,1)S(1)}, u32[]{:S(2)}, u32[]{:S(2)}) collective-permute-start(bf16[16,896]{1,0:T(8,128)(2,1)S(1)} %add_add_fusion.1), channel_id=1, source_target_pairs={{0,32},{16,48},{32,0},{48,16},{64,96},{80,112},{96,64},{112,80},{1... | collective-permute-start | bytes 86024 | tf_op jit(solution)/shard_map/ppermute | solution.py:471
  36.2 6.5 %collective-permute-start.12 = (bf16[16,896]{1,0:T(8,128)(2,1)S(1)}, bf16[16,896]{1,0:T(8,128)(2,1)S(1)}, u32[]{:S(2)}, u32[]{:S(2)}) collective-permute-start(bf16[16,896]{1,0:T(8,128)(2,1)S(1)} %add_add_fusion.1), channel_id=1, source_target_pairs={{0,64},{16,80},{32,96},{48,112},{64,0},{80,16},{96,32},{112,48},{1... | collective-permute-start | bytes 86024 | tf_op jit(solution)/shard_map/ppermute | solution.py:471
  38.5 4.2 %collective-permute-start.13 = (bf16[16,896]{1,0:T(8,128)(2,1)S(1)}, bf16[16,896]{1,0:T(8,128)(2,1)S(1)}, u32[]{:S(2)}, u32[]{:S(2)}) collective-permute-start(bf16[16,896]{1,0:T(8,128)(2,1)S(1)} %add_add_fusion.1), channel_id=1, source_target_pairs={{0,96},{16,112},{32,64},{48,80},{64,32},{80,48},{96,0},{112,16},{1... | collective-permute-start | bytes 86024 | tf_op jit(solution)/shard_map/ppermute | solution.py:471
  38.9 9.6 %collective-permute-start.15 = (bf16[2,440,128]{2,1,0:T(8,128)(2,1)S(1)}, bf16[2,440,128]{2,1,0:T(8,128)(2,1)S(1)}, u32[]{:S(2)}, u32[]{:S(2)}) collective-permute-start(bf16[2,440,128]{2,1,0:T(8,128)(2,1)S(1)} %upper.1), channel_id=1, source_target_pairs={{16,0},{32,16},{48,32},{64,48},{80,64},{96,80},{112,96},{0,112},{1... | collective-permute-start | bytes 675848 | tf_op jit(solution)/shard_map/ppermute | solution.py:583
  42.8 5.7 %collective-permute-start.14 = (f32[16,896]{1,0:T(8,128)S(1)}, f32[16,896]{1,0:T(8,128)S(1)}, u32[]{:S(2)}, u32[]{:S(2)}) collective-permute-start(f32[16,896]{1,0:T(8,128)S(1)} %add_add_fusion.own_half), channel_id=1, source_target_pairs={{0,16},{16,0},{32,48},{48,32},{64,80},{80,64},{96,112},{112,96},{1... | collective-permute-start | bytes 172040 | tf_op jit(solution)/shard_map/ppermute | solution.py:471
  49.9 15.3 %all-to-all-start = ((f32[128,1,2]{2,1,0:T(1,128)}), f32[128,1,2]{2,1,0:T(1,128)S(1)}, u32[]{:S(2)}, u32[]{:S(2)}) async-start(f32[128,1,2]{2,1,0:T(1,128)} %bitcast.7), calls=%async_computation | async-start | bytes 131072 | tf_op jit(solution)/shard_map/all_to_all | solution.py:609

commit v5 on v4

--- a/solution.py
+++ b/solution.py
@@ -175,7 +175,7 @@
     terms[2, at : at + rows, :] = 2.0 + 12.0 * jnp.sqrt(2.0 * per_spread)
 
 
-def row_pair(padded, base, terms, term_row, mask_rows, live_row, strong_rows, fields, slot):
+def row_pair(padded, base, terms, term_row, mask_rows, live_row, fields, slot):
     frames, columns = padded.shape[1:]
     rows = [padded[base + k] for k in range(2 * HALO + 2)]
     shared = rows[1]
@@ -208,18 +208,18 @@
     gates = (1.0 + jnp.exp(shortfall)) * (1.0 + jnp.exp(below))
     weight = pl.reciprocal(gates, approx=True)
     weight = live * (weight * (2.0 - gates * weight))
-    weight_b = weight.astype(jnp.bfloat16).astype(jnp.float32)
-    value_b = value.astype(jnp.bfloat16).astype(jnp.float32)
-    background_b = background.astype(jnp.bfloat16).astype(jnp.float32)
-    strong_rows[pl.ds(2 * slot, 2)] = weight_b
+    flat = (2 * frames, columns)
+    weight, value, background = (
+        x.reshape(flat).astype(jnp.bfloat16) for x in (weight, value, background)
+    )
     at = pl.ds(pl.multiple_of(slot * 2 * frames, 2 * frames), 2 * frames)
-    flat = (2 * frames, columns)
-    fields[0, at, :] = (value_b - background_b).reshape(flat).astype(jnp.bfloat16)
-    fields[1, at, :] = background_b.reshape(flat).astype(jnp.bfloat16)
-    fields[2, at, :] = (weight_b * value_b).reshape(flat).astype(jnp.bfloat16)
-
-
-def inner_kernel(kept, strong_rows, fields, tents, live, terms):
+    fields[0, at, :] = value - background
+    fields[1, at, :] = background
+    fields[2, at, :] = weight * value
+    fields[3, at, :] = weight
+
+
+def inner_kernel(kept, fields, tents, live, terms):
     height, columns = live.shape
     live[...] = kept_rows(kept, height, 0)
     column_tents(kept_info(kept, height, 1), columns, tents)
@@ -227,7 +227,7 @@
     window_counts(live, 1, rows, terms, 0)
 
     def pair(i, carry):
-        row_pair(kept, 2 * i + 1, terms, 2 * i, live, 2 * i + 4, strong_rows, fields, i)
+        row_pair(kept, 2 * i + 1, terms, 2 * i, live, 2 * i + 4, fields, i)
         return carry
 
     lax.fori_loop(0, rows // 2, pair, 0, unroll=6)
@@ -279,7 +279,6 @@
     mixer,
     inner_fields,
     own_tents,
-    edge_strong,
     edge_fields,
     partner_tents,
     rows,
@@ -317,7 +316,7 @@
     window_counts(mask_rows, 5, 4, terms, 0)
     window_counts(mask_rows, 21, 4, terms, 8)
     for slot, (base, term_row, live_row) in enumerate(((0, 0, 8), (2, 2, 10), (10, 8, 24), (12, 10, 26))):
-        row_pair(padded, base, terms, term_row, mask_rows, live_row, edge_strong, edge_fields, slot)
+        row_pair(padded, base, terms, term_row, mask_rows, live_row, edge_fields, slot)
 
     partner = jnp.where(odd_slab, from_core[...], from_chip[...])
     following = jnp.where(odd_slab, from_chip[0:height], from_core[0:height])
@@ -378,11 +377,13 @@
         half_grids(mixed, tents, rows[half], spread, packed, take)
 
 
-def strong_kernel(edge_strong, inner_strong, strong, rows):
-    rows[0:4] = edge_strong[0:4]
-    rows[4 : rows.shape[0] - 4] = inner_strong[...]
-    rows[rows.shape[0] - 4 :] = edge_strong[4:]
-    strong[...] = jnp.transpose(rows[...], (1, 0, 2)).astype(jnp.bfloat16)
+def strong_kernel(edge_fields, inner_fields, strong):
+    frames, height, columns = strong.shape
+    quarter = edge_fields.shape[1] // 2
+    edges, inner = edge_fields[3].astype(jnp.float32), inner_fields[3].astype(jnp.float32)
+    rows = jnp.concatenate([edges[0:quarter], inner, edges[quarter:]], axis=0)
+    rows = rows.reshape(height, frames, columns)
+    strong[...] = jnp.transpose(rows, (1, 0, 2)).astype(jnp.bfloat16)
 
 
 def all_regions(own_half, other_half):
@@ -525,10 +526,10 @@
 
     inner = height - 8
     tent_shape = shape((columns, GRID * LANES), bf16)
-    inner_strong, inner_fields, own_tents = call(
+    inner_fields, own_tents = call(
         inner_kernel,
         (kept,),
-        [shape((inner, frames, columns)), shape((3, inner * frames, columns), bf16), tent_shape],
+        [shape((4, inner * frames, columns), bf16), tent_shape],
         [shape((height, columns)), shape((3, inner, columns))],
         name="inner",
     )
@@ -537,7 +538,7 @@
     field_shape = shape((height * frames, columns), bf16)
     spread_shape = shape((2, height * 8, 2 * LANES))
     packed_shape = shape((PLANE * 8, LANES))
-    edge_strong, edge_fields, partner_tents, rows, kept_sums, sent_sums = call(
+    edge_fields, partner_tents, rows, kept_sums, sent_sums = call(
         spot_kernel,
         (
             kept,
@@ -550,8 +551,7 @@
             own_tents,
         ),
         [
-            shape((8, frames, columns)),
-            shape((3, 8 * frames, columns), bf16),
+            shape((4, 8 * frames, columns), bf16),
             tent_shape,
             shape((2, 1, LANES), jnp.int32),
             shape((REGIONS // 2, WIDE_ROWS)),
@@ -594,9 +594,8 @@
     other = swapped(sums, "frame", 1)
     (strong,) = call(
         strong_kernel,
-        (edge_strong, inner_strong),
+        (edge_fields, inner_fields),
         [shape((frames, height, columns), bf16)],
-        [shape((height, frames, columns))],
         name="strong",
     )
     (estimates,) = call(

time: 66.2 us -> 66.1 us (level)
  no operation moved by 1% of the time
where the time goes in v5:
time: 66.1 us; the launch traced here: 65.8 us
  starting transfers between devices  37.1 us (56%)
  Pallas kernels  13.6 us (21%)
  waiting for transfers between devices  12.9 us (20%)
  local copies, waits for them, and re-layouts  1.13 us (2%)
  between operations  0.81 us (1%)
    ppermute x11, starting transfers between devices, swapped(): lax.ppermute(x, axis, [(i, i ^ flip) for i in range(lax.axis_size(axis))])  19.7 us
    pallas_call x8, Pallas kernels, call(): pl.pallas_call(kernel, in_specs=[vmem] * len(operands), out_specs=[vmem]...  11.3 us
    all_to_all x1, waiting for transfers between devices, per_device(): lax.all_to_all(estimates, ('frame', 'refl'), split_axis=0, concat_axis=0,...  7.82 us
    all_to_all x1, starting transfers between devices, per_device(): lax.all_to_all(estimates, ('frame', 'refl'), split_axis=0, concat_axis=0,...  5.72 us
    ppermute x11, waiting for transfers between devices, swapped(): lax.ppermute(x, axis, [(i, i ^ flip) for i in range(lax.axis_size(axis))])  5.06 us
    ppermute x1, starting transfers between devices, per_device(): lax.ppermute(upper_grids, 'frame', [((i + 1) % slabs, i) for i in range(s...  3.85 us
    ppermute x1, starting transfers between devices, per_device(): from_chip = lax.ppermute(chip, 'frame', pairs_odd(slabs))  3.19 us
    pallas_call x1, Pallas kernels, per_device(): pl.pallas_call(send_kernel, in_specs=[pl.BlockSpec(memory_space=pl.ANY)]...  2.26 us
  transfers between devices with their start and end apart: 17, of which 6 were waited for; matrix products, arithmetic and copies ran while one was open for 0% of the time, Pallas kernels for 11%

profile of v5, /device:TPU:1, one launch (start us, length us, event | category | flops | bytes accessed | tf_op | source)
XLA Modules:
  0.0 65.8 jit_solution(16673680185796297513)
XLA Ops:
  0.6 2.3 %sent.1 = (f32[4,8,512]{2,1,0:T(8,128)}, f32[4,8,512]{2,1,0:T(8,128)}, f32[40,512]{1,0:T(8,128)}, f32[40,512]{1,0:T(8,128)}, f32[45,8,512]{2,1,0:T(8,128)}) custom-call(f32[8,32,512]{2,1,0:T(8,128)} %image.1, f32[32,512]{1,0:T(8,128)} %gain.1, s32[32,512]{1,0:T(8,128)} %mask.1, s32[1,128]{1,0:T(1,128)} %bitcast.15, s32[1,128]{1,0:T(1,128)} %bitcast.16, ...), custom_call_target="tpu_custom_call" | custom-call | tf_op jit(solution)/shard_map/sent/pallas_call | solution.py:505
  2.9 1.5 %collective-permute-start.2 = (f32[40,512]{1,0:T(8,128)}, f32[40,512]{1,0:T(8,128)S(1)}, u32[]{:S(2)}, u32[]{:S(2)}) collective-permute-start(f32[40,512]{1,0:T(8,128)} %get-tuple-element.25), channel_id=1, source_target_pairs={{0,16},{16,0},{32,48},{48,32},{64,80},{80,64},{96,112},{112,96},{1... | collective-permute-start | bytes 245768 | tf_op jit(solution)/shard_map/ppermute | solution.py:523
  4.4 3.2 %collective-permute-start.3 = (f32[40,512]{1,0:T(8,128)}, f32[40,512]{1,0:T(8,128)S(1)}, u32[]{:S(2)}, u32[]{:S(2)}) collective-permute-start(f32[40,512]{1,0:T(8,128)} %get-tuple-element.26), channel_id=1, source_target_pairs={{0,0},{16,32},{32,16},{48,64},{64,48},{80,96},{96,80},{112,112},{1... | collective-permute-start | bytes 245768 | tf_op jit(solution)/shard_map/ppermute | solution.py:524
  7.6 1.7 %collective-permute-start = (f32[4,8,512]{2,1,0:T(8,128)}, f32[4,8,512]{2,1,0:T(8,128)S(1)}, u32[]{:S(2)}, u32[]{:S(2)}) collective-permute-start(f32[4,8,512]{2,1,0:T(8,128)} %get-tuple-element.23), channel_id=1, source_target_pairs={{0,1},{1,0},{2,3},{3,2},{4,5},{5,4},{6,7},{7,6},{8,9},{9,8},{10,11... | collective-permute-start | bytes 196616 | tf_op jit(solution)/shard_map/ppermute | solution.py:522
  9.3 1.5 %collective-permute-start.1 = (f32[4,8,512]{2,1,0:T(8,128)}, f32[4,8,512]{2,1,0:T(8,128)S(1)}, u32[]{:S(2)}, u32[]{:S(2)}) collective-permute-start(f32[4,8,512]{2,1,0:T(8,128)} %get-tuple-element.24), channel_id=1, source_target_pairs={{0,0},{1,2},{2,1},{3,4},{4,3},{5,6},{6,5},{7,8},{8,7},{9,10},{10,9... | collective-permute-start | bytes 196616 | tf_op jit(solution)/shard_map/ppermute | solution.py:521
  10.8 1.1 %copy-done = f32[45,8,512]{2,1,0:T(8,128)S(1)} copy-done((f32[45,8,512]{2,1,0:T(8,128)S(1)}, f32[45,8,512]{2,1,0:T(8,128)}, u32[]{:S(2)}) %copy-start) | copy-done | bytes 737304
  11.9 2.7 %inner.1 = (bf16[4,192,512]{2,1,0:T(8,128)(2,1)S(1)}, bf16[512,1152]{1,0:T(8,128)(2,1)S(1)}) custom-call(f32[45,8,512]{2,1,0:T(8,128)S(1)} %copy-done), custom_call_target="tpu_custom_call" | custom-call | flops 1 | bytes 1 | tf_op jit(solution)/shard_map/inner/pallas_call | solution.py:493
  14.7 2.3 %spots.1 = (bf16[4,64,512]{2,1,0:T(8,128)(2,1)S(1)}, bf16[512,1152]{1,0:T(8,128)(2,1)S(1)}, s32[2,1,128]{2,1,0:T(1,128)S(1)}, f32[16,896]{1,0:T(8,128)S(1)}, f32[16,896]{1,0:T(8,128)S(1)}) custom-call(f32[45,8,512]{2,1,0:T(8,128)S(1)} %copy-done, f32[4,8,512]{2,1,0:T(8,128)S(1)} %collective-permute-done.halo_first, ...), custom_call_target="tpu_custom_call" | custom-call | flops 1 | bytes 1 | tf_op jit(solution)/shard_map/spots/pallas_call | solution.py:493
  17.0 1.2 %collective-permute-done.4 = f32[16,896]{1,0:T(8,128)S(1)} collective-permute-done((f32[16,896]{1,0:T(8,128)S(1)}, f32[16,896]{1,0:T(8,128)S(1)}, u32[]{:S(2)}, u32[]{:S(2)}) %collective-permute-start.4) | collective-permute-done | bytes 57376 | tf_op jit(solution)/shard_map/ppermute | solution.py:472
  18.3 3.9 %collective-permute-start.5 = (bf16[16,896]{1,0:T(8,128)(2,1)S(1)}, bf16[16,896]{1,0:T(8,128)(2,1)S(1)}, u32[]{:S(2)}, u32[]{:S(2)}) collective-permute-start(bf16[16,896]{1,0:T(8,128)(2,1)S(1)} %add.40), channel_id=1, source_target_pairs={{0,4},{1,5},{2,6},{3,7},{4,0},{5,1},{6,2},{7,3},{8,12},{9,13},{10,... | collective-permute-start | bytes 86024 | tf_op jit(solution)/shard_map/ppermute | solution.py:472
  22.2 2.7 %collective-permute-start.6 = (bf16[16,896]{1,0:T(8,128)(2,1)S(1)}, bf16[16,896]{1,0:T(8,128)(2,1)S(1)}, u32[]{:S(2)}, u32[]{:S(2)}) collective-permute-start(bf16[16,896]{1,0:T(8,128)(2,1)S(1)} %add.40), channel_id=1, source_target_pairs={{0,8},{1,9},{2,10},{3,11},{4,12},{5,13},{6,14},{7,15},{8,0},{9,1},... | collective-permute-start | bytes 86024 | tf_op jit(solution)/shard_map/ppermute | solution.py:472
  25.0 1.3 %upper.1 = bf16[2,440,128]{2,1,0:T(8,128)(2,1)S(1)} custom-call(s32[2,1,128]{2,1,0:T(1,128)S(1)} %get-tuple-element.33.rows, bf16[2,256,256]{2,1,0:T(8,128)(2,1)S(1)} %copy-done.1, bf16[4,64,512]{2,1,0:T(8,128)(2,1)S(1)} %get-tuple-element.36.edge_fields, bf16[4,192,512]{2,1,0:T(8,128)(2,1)S(1)} %get-tuple-element.27.inner_fields, ...), custom_call_target="tpu_custom_call" | custom-call | flops 1 | bytes 1 | tf_op jit(solution)/shard_map/upper/pallas_call | solution.py:493
  26.5 2.4 %collective-permute-done.7 = bf16[16,896]{1,0:T(8,128)(2,1)S(1)} collective-permute-done((bf16[16,896]{1,0:T(8,128)(2,1)S(1)}, bf16[16,896]{1,0:T(8,128)(2,1)S(1)}, u32[]{:S(2)}, u32[]{:S(2)}) %collective-permute-start.7) | collective-permute-done | bytes 28704 | tf_op jit(solution)/shard_map/ppermute | solution.py:472
  29.6 3.3 %collective-permute-start.9 = (bf16[16,896]{1,0:T(8,128)(2,1)S(1)}, bf16[16,896]{1,0:T(8,128)(2,1)S(1)}, u32[]{:S(2)}, u32[]{:S(2)}) collective-permute-start(bf16[16,896]{1,0:T(8,128)(2,1)S(1)} %add_add_fusion.2), channel_id=1, source_target_pairs={{0,2},{1,3},{2,0},{3,1},{4,6},{5,7},{6,4},{7,5},{8,10},{9,11},{10,... | collective-permute-start | bytes 86024 | tf_op jit(solution)/shard_map/ppermute | solution.py:472
  32.9 1.3 %lower.1.lower_grids = f32[2,440,128]{2,1,0:T(8,128)S(1)} custom-call(s32[2,1,128]{2,1,0:T(1,128)S(1)} %get-tuple-element.33.rows, bf16[2,256,256]{2,1,0:T(8,128)(2,1)S(1)} %copy-done.1, bf16[4,64,512]{2,1,0:T(8,128)(2,1)S(1)} %get-tuple-element.36.edge_fields, bf16[4,192,512]{2,1,0:T(8,128)(2,1)S(1)} %get-tuple-element.27.inner_fields, ...), custom_call_target="tpu_custom_call" | custom-call | flops 1 | bytes 1 | tf_op jit(solution)/shard_map/lower/pallas_call | solution.py:493
  34.5 1.8 %collective-permute-start.11 = (bf16[16,896]{1,0:T(8,128)(2,1)S(1)}, bf16[16,896]{1,0:T(8,128)(2,1)S(1)}, u32[]{:S(2)}, u32[]{:S(2)}) collective-permute-start(bf16[16,896]{1,0:T(8,128)(2,1)S(1)} %add_add_fusion.1), channel_id=1, source_target_pairs={{0,32},{16,48},{32,0},{48,16},{64,96},{80,112},{96,64},{112,80},{1... | collective-permute-start | bytes 86024 | tf_op jit(solution)/shard_map/ppermute | solution.py:472
  36.2 2.3 %collective-permute-start.12 = (bf16[16,896]{1,0:T(8,128)(2,1)S(1)}, bf16[16,896]{1,0:T(8,128)(2,1)S(1)}, u32[]{:S(2)}, u32[]{:S(2)}) collective-permute-start(bf16[16,896]{1,0:T(8,128)(2,1)S(1)} %add_add_fusion.1), channel_id=1, source_target_pairs={{0,64},{16,80},{32,96},{48,112},{64,0},{80,16},{96,32},{112,48},{1... | collective-permute-start | bytes 86024 | tf_op jit(solution)/shard_map/ppermute | solution.py:472
  38.9 3.9 %collective-permute-start.15 = (bf16[2,440,128]{2,1,0:T(8,128)(2,1)S(1)}, bf16[2,440,128]{2,1,0:T(8,128)(2,1)S(1)}, u32[]{:S(2)}, u32[]{:S(2)}) collective-permute-start(bf16[2,440,128]{2,1,0:T(8,128)(2,1)S(1)} %upper.1), channel_id=1, source_target_pairs={{16,0},{32,16},{48,32},{64,48},{80,64},{96,80},{112,96},{0,112},{1... | collective-permute-start | bytes 675848 | tf_op jit(solution)/shard_map/ppermute | solution.py:583
  42.8 4.8 %collective-permute-start.14 = (f32[16,896]{1,0:T(8,128)S(1)}, f32[16,896]{1,0:T(8,128)S(1)}, u32[]{:S(2)}, u32[]{:S(2)}) collective-permute-start(f32[16,896]{1,0:T(8,128)S(1)} %add_add_fusion.own_half), channel_id=1, source_target_pairs={{0,16},{16,0},{32,48},{48,32},{64,80},{80,64},{96,112},{112,96},{1... | collective-permute-start | bytes 172040 | tf_op jit(solution)/shard_map/ppermute | solution.py:472
  47.6 0.9 %collective-permute-done.14.other_half = f32[16,896]{1,0:T(8,128)S(1)} collective-permute-done((f32[16,896]{1,0:T(8,128)S(1)}, f32[16,896]{1,0:T(8,128)S(1)}, u32[]{:S(2)}, u32[]{:S(2)}) %collective-permute-start.14) | collective-permute-done | bytes 57376 | tf_op jit(solution)/shard_map/ppermute | solution.py:472
  48.4 1.4 %fit.1 = f32[128,2]{1,0:T(8,128)} custom-call(f32[16,896]{1,0:T(8,128)S(1)} %add_add_fusion.own_half, f32[16,896]{1,0:T(8,128)S(1)} %collective-permute-done.14.other_half, s32[1,128]{1,0:T(1,128)S(1)} %bitcast.14, s32[1,128]{1,0:T(1,128)S(1)} %bitcast_add_fusion.slots, f32[2,440,128]{2,1,0:T(8,128)S(1)} %lower.1.lower_grids, ...), custom_call_target="tpu_custom_call" | custom-call | flops 1 | bytes 1 | tf_op jit(solution)/shard_map/fit/pallas_call | solution.py:493
  49.9 5.7 %all-to-all-start = ((f32[128,1,2]{2,1,0:T(1,128)}), f32[128,1,2]{2,1,0:T(1,128)S(1)}, u32[]{:S(2)}, u32[]{:S(2)}) async-start(f32[128,1,2]{2,1,0:T(1,128)} %bitcast.7), calls=%async_computation | async-start | bytes 131072 | tf_op jit(solution)/shard_map/all_to_all | solution.py:608
  56.4 0.9 %profiles.1 = f32[32,729]{1,0:T(8,128)} custom-call(f32[16,896]{1,0:T(8,128)S(1)} %add_add_fusion.own_half, f32[16,896]{1,0:T(8,128)S(1)} %collective-permute-done.14.other_half), custom_call_target="tpu_custom_call" | custom-call | flops 1 | bytes 1 | tf_op jit(solution)/shard_map/profiles/pallas_call | solution.py:493
  57.3 7.8 %all-to-all-done = f32[128,1,2]{2,1,0:T(1,128)S(1)} async-done(((f32[128,1,2]{2,1,0:T(1,128)}), f32[128,1,2]{2,1,0:T(1,128)S(1)}, u32[]{:S(2)}, u32[]{:S(2)}) %all-to-all-start) | async-done | bytes 1056 | tf_op jit(solution)/shard_map/all_to_all | solution.py:608
  (33 shorter events, 3.2 us)
Async XLA Ops:
  0.6 14.0 %copy-start.1 = (bf16[2,256,256]{2,1,0:T(8,128)(2,1)S(1)}, bf16[2,256,256]{2,1,0:T(8,128)(2,1)}, u32[]{:S(2)}) copy-start(bf16[2,256,256]{2,1,0:T(8,128)(2,1)} %constant.8.clone.mixer) | copy-start | bytes 786436
  2.9 11.7 %collective-permute-start.2 = (f32[40,512]{1,0:T(8,128)}, f32[40,512]{1,0:T(8,128)S(1)}, u32[]{:S(2)}, u32[]{:S(2)}) collective-permute-start(f32[40,512]{1,0:T(8,128)} %get-tuple-element.25), channel_id=1, source_target_pairs={{0,16},{16,0},{32,48},{48,32},{64,80},{80,64},{96,112},{112,96},{1... | collective-permute-start | bytes 245768 | tf_op jit(solution)/shard_map/ppermute | solution.py:523
  4.4 10.3 %collective-permute-start.3 = (f32[40,512]{1,0:T(8,128)}, f32[40,512]{1,0:T(8,128)S(1)}, u32[]{:S(2)}, u32[]{:S(2)}) collective-permute-start(f32[40,512]{1,0:T(8,128)} %get-tuple-element.26), channel_id=1, source_target_pairs={{0,0},{16,32},{32,16},{48,64},{64,48},{80,96},{96,80},{112,112},{1... | collective-permute-start | bytes 245768 | tf_op jit(solution)/shard_map/ppermute | solution.py:524
  7.6 7.0 %collective-permute-start = (f32[4,8,512]{2,1,0:T(8,128)}, f32[4,8,512]{2,1,0:T(8,128)S(1)}, u32[]{:S(2)}, u32[]{:S(2)}) collective-permute-start(f32[4,8,512]{2,1,0:T(8,128)} %get-tuple-element.23), channel_id=1, source_target_pairs={{0,1},{1,0},{2,3},{3,2},{4,5},{5,4},{6,7},{7,6},{8,9},{9,8},{10,11... | collective-permute-start | bytes 196616 | tf_op jit(solution)/shard_map/ppermute | solution.py:522
  9.3 5.3 %collective-permute-start.1 = (f32[4,8,512]{2,1,0:T(8,128)}, f32[4,8,512]{2,1,0:T(8,128)S(1)}, u32[]{:S(2)}, u32[]{:S(2)}) collective-permute-start(f32[4,8,512]{2,1,0:T(8,128)} %get-tuple-element.24), channel_id=1, source_target_pairs={{0,0},{1,2},{2,1},{3,4},{4,3},{5,6},{6,5},{7,8},{8,7},{9,10},{10,9... | collective-permute-start | bytes 196616 | tf_op jit(solution)/shard_map/ppermute | solution.py:521
  10.8 1.1 %copy-start = (f32[45,8,512]{2,1,0:T(8,128)S(1)}, f32[45,8,512]{2,1,0:T(8,128)}, u32[]{:S(2)}) copy-start(f32[45,8,512]{2,1,0:T(8,128)} %get-tuple-element.22.kept) | copy-start | bytes 2211844
  17.0 1.3 %collective-permute-start.4 = (f32[16,896]{1,0:T(8,128)S(1)}, f32[16,896]{1,0:T(8,128)S(1)}, u32[]{:S(2)}, u32[]{:S(2)}) collective-permute-start(f32[16,896]{1,0:T(8,128)S(1)} %get-tuple-element.30), channel_id=1, source_target_pairs={{0,16},{16,0},{32,48},{48,32},{64,80},{80,64},{96,112},{112,96},{1... | collective-permute-start | bytes 172040 | tf_op jit(solution)/shard_map/ppermute | solution.py:472
  18.3 7.9 %collective-permute-start.5 = (bf16[16,896]{1,0:T(8,128)(2,1)S(1)}, bf16[16,896]{1,0:T(8,128)(2,1)S(1)}, u32[]{:S(2)}, u32[]{:S(2)}) collective-permute-start(bf16[16,896]{1,0:T(8,128)(2,1)S(1)} %add.40), channel_id=1, source_target_pairs={{0,4},{1,5},{2,6},{3,7},{4,0},{5,1},{6,2},{7,3},{8,12},{9,13},{10,... | collective-permute-start | bytes 86024 | tf_op jit(solution)/shard_map/ppermute | solution.py:472
  22.2 4.3 %collective-permute-start.6 = (bf16[16,896]{1,0:T(8,128)(2,1)S(1)}, bf16[16,896]{1,0:T(8,128)(2,1)S(1)}, u32[]{:S(2)}, u32[]{:S(2)}) collective-permute-start(bf16[16,896]{1,0:T(8,128)(2,1)S(1)} %add.40), channel_id=1, source_target_pairs={{0,8},{1,9},{2,10},{3,11},{4,12},{5,13},{6,14},{7,15},{8,0},{9,1},... | collective-permute-start | bytes 86024 | tf_op jit(solution)/shard_map/ppermute | solution.py:472
  25.0 3.9 %collective-permute-start.7 = (bf16[16,896]{1,0:T(8,128)(2,1)S(1)}, bf16[16,896]{1,0:T(8,128)(2,1)S(1)}, u32[]{:S(2)}, u32[]{:S(2)}) collective-permute-start(bf16[16,896]{1,0:T(8,128)(2,1)S(1)} %add.40), channel_id=1, source_target_pairs={{0,12},{1,13},{2,14},{3,15},{4,8},{5,9},{6,10},{7,11},{8,4},{9,5},... | collective-permute-start | bytes 86024 | tf_op jit(solution)/shard_map/ppermute | solution.py:472
  28.9 9.8 %copy-start.3 = (s32[128,1]{0,1:T(1,128)S(1)}, s32[128,1]{0,1:T(1,128)}, u32[]{:S(2)}) copy-start(s32[128,1]{0,1:T(1,128)} %param.13) | copy-start | bytes 1540
  28.9 19.5 %copy-start.2 = (s32[128,1]{0,1:T(1,128)S(1)}, s32[128,1]{0,1:T(1,128)}, u32[]{:S(2)}) copy-start(s32[128,1]{0,1:T(1,128)} %param.14) | copy-start | bytes 1540
  28.9 5.2 %collective-permute-start.10 = (bf16[16,896]{1,0:T(8,128)(2,1)S(1)}, bf16[16,896]{1,0:T(8,128)(2,1)S(1)}, u32[]{:S(2)}, u32[]{:S(2)}) collective-permute-start(bf16[16,896]{1,0:T(8,128)(2,1)S(1)} %add_add_fusion.2), channel_id=1, source_target_pairs={{0,3},{1,2},{2,1},{3,0},{4,7},{5,6},{6,5},{7,4},{8,11},{9,10},{10,... | collective-permute-start | bytes 86024 | tf_op jit(solution)/shard_map/ppermute | solution.py:472
  29.5 4.7 %collective-permute-start.8 = (bf16[16,896]{1,0:T(8,128)(2,1)S(1)}, bf16[16,896]{1,0:T(8,128)(2,1)S(1)}, u32[]{:S(2)}, u32[]{:S(2)}) collective-permute-start(bf16[16,896]{1,0:T(8,128)(2,1)S(1)} %add_add_fusion.2), channel_id=1, source_target_pairs={{0,1},{1,0},{2,3},{3,2},{4,5},{5,4},{6,7},{7,6},{8,9},{9,8},{10,11... | collective-permute-start | bytes 86024 | tf_op jit(solution)/shard_map/ppermute | solution.py:472
  29.6 4.9 %collective-permute-start.9 = (bf16[16,896]{1,0:T(8,128)(2,1)S(1)}, bf16[16,896]{1,0:T(8,128)(2,1)S(1)}, u32[]{:S(2)}, u32[]{:S(2)}) collective-permute-start(bf16[16,896]{1,0:T(8,128)(2,1)S(1)} %add_add_fusion.2), channel_id=1, source_target_pairs={{0,2},{1,3},{2,0},{3,1},{4,6},{5,7},{6,4},{7,5},{8,10},{9,11},{10,... | collective-permute-start | bytes 86024 | tf_op jit(solution)/shard_map/ppermute | solution.py:472
  34.5 8.3 %collective-permute-start.11 = (bf16[16,896]{1,0:T(8,128)(2,1)S(1)}, bf16[16,896]{1,0:T(8,128)(2,1)S(1)}, u32[]{:S(2)}, u32[]{:S(2)}) collective-permute-start(bf16[16,896]{1,0:T(8,128)(2,1)S(1)} %add_add_fusion.1), channel_id=1, source_target_pairs={{0,32},{16,48},{32,0},{48,16},{64,96},{80,112},{96,64},{112,80},{1... | collective-permute-start | bytes 86024 | tf_op jit(solution)/shard_map/ppermute | solution.py:472
  36.2 6.5 %collective-permute-start.12 = (bf16[16,896]{1,0:T(8,128)(2,1)S(1)}, bf16[16,896]{1,0:T(8,128)(2,1)S(1)}, u32[]{:S(2)}, u32[]{:S(2)}) collective-permute-start(bf16[16,896]{1,0:T(8,128)(2,1)S(1)} %add_add_fusion.1), channel_id=1, source_target_pairs={{0,64},{16,80},{32,96},{48,112},{64,0},{80,16},{96,32},{112,48},{1... | collective-permute-start | bytes 86024 | tf_op jit(solution)/shard_map/ppermute | solution.py:472
  38.5 4.2 %collective-permute-start.13 = (bf16[16,896]{1,0:T(8,128)(2,1)S(1)}, bf16[16,896]{1,0:T(8,128)(2,1)S(1)}, u32[]{:S(2)}, u32[]{:S(2)}) collective-permute-start(bf16[16,896]{1,0:T(8,128)(2,1)S(1)} %add_add_fusion.1), channel_id=1, source_target_pairs={{0,96},{16,112},{32,64},{48,80},{64,32},{80,48},{96,0},{112,16},{1... | collective-permute-start | bytes 86024 | tf_op jit(solution)/shard_map/ppermute | solution.py:472
  38.9 9.6 %collective-permute-start.15 = (bf16[2,440,128]{2,1,0:T(8,128)(2,1)S(1)}, bf16[2,440,128]{2,1,0:T(8,128)(2,1)S(1)}, u32[]{:S(2)}, u32[]{:S(2)}) collective-permute-start(bf16[2,440,128]{2,1,0:T(8,128)(2,1)S(1)} %upper.1), channel_id=1, source_target_pairs={{16,0},{32,16},{48,32},{64,48},{80,64},{96,80},{112,96},{0,112},{1... | collective-permute-start | bytes 675848 | tf_op jit(solution)/shard_map/ppermute | solution.py:583
  42.8 5.7 %collective-permute-start.14 = (f32[16,896]{1,0:T(8,128)S(1)}, f32[16,896]{1,0:T(8,128)S(1)}, u32[]{:S(2)}, u32[]{:S(2)}) collective-permute-start(f32[16,896]{1,0:T(8,128)S(1)} %add_add_fusion.own_half), channel_id=1, source_target_pairs={{0,16},{16,0},{32,48},{48,32},{64,80},{80,64},{96,112},{112,96},{1... | collective-permute-start | bytes 172040 | tf_op jit(solution)/shard_map/ppermute | solution.py:472
  49.9 15.3 %all-to-all-start = ((f32[128,1,2]{2,1,0:T(1,128)}), f32[128,1,2]{2,1,0:T(1,128)S(1)}, u32[]{:S(2)}, u32[]{:S(2)}) async-start(f32[128,1,2]{2,1,0:T(1,128)} %bitcast.7), calls=%async_computation | async-start | bytes 131072 | tf_op jit(solution)/shard_map/all_to_all | solution.py:608
